TPU v7x, 128 devices: a whole 4x4x4 slice. The times are simulated.
128 devices in a mesh: bx: 8 (over x, y_hi), by: 16 (over y_lo, z, core).
Axes of the slice: x: 4, y: 4 (y_hi: 2, y_lo: 2; y = y_hi * 2 + y_lo), z: 4, core: 2. Of those that a mesh axis runs over, the one named last changes fastest.
Arguments:
- features: bfloat16 [8, 16, 128, 25, 128], P('bx', 'by'), may hold values from -6 to 6
- send_index: int32 [8, 16, 3, 3, 16], P('bx', 'by'), may hold values from 0 to 128
- atom_vectors: float32 [8, 16, 3, 1024], P('bx', 'by'), may hold values from -4 to 4, as said below
- atom_source: int32 [8, 16, 1024], P('bx', 'by'), may hold values from 0 to 256
- atom_target: int32 [8, 16, 1024], P('bx', 'by'), may hold values from 0 to 128
- probe_vectors: float32 [8, 16, 3, 512], P('bx', 'by'), may hold values from -4 to 4, as said below
- probe_atoms: int32 [8, 16, 512], P('bx', 'by'), may hold values from 0 to 256
- density_grid: float32 [8, 16, 32768], P('bx', 'by'), may hold values from -6 to 6
- probe_index: int32 [8, 16, 128], P('bx', 'by'), may hold values from 0 to 32767
- radial_first: float32 [20, 64], replicated, may hold values from -1.25 to 1.25
- radial_second: float32 [64, 1280], replicated, may hold values from -0.75 to 0.75
- mixing: float32 [5, 128, 128], replicated, may hold values from -0.5 to 0.5
- probe_first: float32 [20, 64], replicated, may hold values from -1.25 to 1.25
- probe_second: float32 [64, 640], replicated, may hold values from -0.75 to 0.75
- readout_first: float32 [128, 128], replicated, may hold values from -0.5 to 0.5
- readout_second: float32 [128], replicated, may hold values from -0.5 to 0.5
Outputs:
- loss_value: float32 [], replicated
- feature_grad: float32 [8, 16, 128, 25, 128], P('bx', 'by')
- radial_first_grad: float32 [20, 64], replicated
- radial_second_grad: float32 [64, 1280], replicated
- mixing_grad: float32 [5, 128, 128], replicated
- probe_first_grad: float32 [20, 64], replicated
- probe_second_grad: float32 [64, 640], replicated
- readout_first_grad: float32 [128, 128], replicated
- readout_second_grad: float32 [128], replicated
Inputs may be any that keep to these rules, and one draw needn't show every extreme that they name: `atom_vectors`: each column is a displacement of length 0.7 to 4.0. `probe_vectors`: each column is a displacement of length 0.7 to 4.0.
All inputs are finite; a program needn't handle non-finite values.
Results may differ from a plain program's by a relative error of at most 0.0075.
Values may be sent and summed in bfloat16 or wider, within the bound.
No kernel may reach another device: no remote copies, remote signals or barrier semaphores. Data moves between devices by JAX's collectives and lax.ppermute only.
A program may use at most 192 MiB of HBM per device.

v0:
```python
import functools

import jax
import jax.numpy as jnp
from jax import lax
from jax.experimental import pallas as pl
from jax.experimental.pallas import tpu as pltpu
from jax.sharding import PartitionSpec as P

C = 128
COMP = 25
BASIS = 20
HIDDEN = 64
ATOMS = 128
EDGES = 1024
PEDGES = 512
PROBES = 128
WIDE = COMP * C
EB = 256
DEGREES = (1, 3, 5, 7, 9)
STARTS = (0, 1, 4, 9, 16)
HIGHEST = lax.Precision.HIGHEST
F32 = jnp.float32
BF16 = jnp.bfloat16
REDUCE_ROWS = 2048


def dot(a, b):
    return jnp.dot(a, b, preferred_element_type=F32)


def dot_exact(a, b):
    return jnp.dot(a, b, preferred_element_type=F32, precision=HIGHEST)


def dot_nt(a, b, precision=None):
    return lax.dot_general(
        a, b, (((1,), (1,)), ((), ())), preferred_element_type=F32, precision=precision
    )


def dot_tn(a, b, precision=None):
    return lax.dot_general(
        a, b, (((0,), (0,)), ((), ())), preferred_element_type=F32, precision=precision
    )


def split(a):
    high = a.astype(BF16)
    return high, (a - high.astype(F32)).astype(BF16)


def sigmoid(a):
    return 1.0 / (1.0 + jnp.exp(-a))


def cols(component):
    return slice(component * C, (component + 1) * C)


def chunks(degree):
    first = STARTS[degree]
    last = first + DEGREES[degree]
    return [(at, min(at + 2, last)) for at in range(first, last, 2)]


def harmonics(x, y, z):
    z_square = z * z
    return [
        jnp.ones_like(x),
        1.7320508 * y,
        1.7320508 * z,
        1.7320508 * x,
        3.8729833 * x * y,
        3.8729833 * y * z,
        1.118034 * (3.0 * z_square - 1.0),
        3.8729833 * x * z,
        1.9364917 * (x * x - y * y),
        2.0916501 * y * (3.0 * x * x - y * y),
        10.246951 * x * y * z,
        1.6201852 * y * (5.0 * z_square - 1.0),
        1.3228757 * z * (5.0 * z_square - 3.0),
        1.6201852 * x * (5.0 * z_square - 1.0),
        5.1234754 * z * (x * x - y * y),
        2.0916501 * x * (x * x - 3.0 * y * y),
        8.8741197 * x * y * (x * x - y * y),
        6.2749502 * y * z * (3.0 * x * x - y * y),
        3.354102 * x * y * (7.0 * z_square - 1.0),
        2.3717082 * y * z * (7.0 * z_square - 3.0),
        0.375 * (35.0 * z_square * z_square - 30.0 * z_square + 3.0),
        2.3717082 * x * z * (7.0 * z_square - 3.0),
        1.677051 * (x * x - y * y) * (7.0 * z_square - 1.0),
        6.2749502 * x * z * (x * x - 3.0 * y * y),
        2.2185299 * (x * x * x * x - 6.0 * x * x * y * y + y * y * y * y),
    ]


def pack_kernel(features, send_index, own, low, middle, high, chosen_out, placed_out, lists):
    lists[...] = jnp.zeros_like(lists)
    for at in range(8):
        i, j = divmod(at if at < 4 else at + 1, 3)
        lists[at : at + 1, 0:16] = send_index[i, j : j + 1, :].astype(F32)
    turned = lists[...].T
    lane = lax.broadcasted_iota(jnp.int32, (16, C), 1).astype(F32)
    hits = [(turned[0:16, at : at + 1] == lane).astype(F32) for at in range(8)]
    chosen = jnp.concatenate(hits, axis=0)
    chosen_out[...] = chosen.astype(BF16)
    placed_out[...] = chosen.T.astype(BF16)
    for component in range(COMP):
        own[:, cols(component)] = features[component]
    send_packets(chosen_out[...], own, low, middle, high)


def send_packets(chosen, rows, low, middle, high):
    for first in range(0, COMP, 2):
        wide = slice(first * C, min(first + 2, COMP) * C)
        packet = dot(chosen, rows[:, wide]).astype(BF16)
        low[:, wide] = packet[0:48]
        middle[:, wide] = packet[48:80]
        high[:, wide] = packet[80:128]


def geometry(vectors, index_rows, edges, turned, basis_out):
    x, y, z = vectors[0:1], vectors[1:2], vectors[2:3]
    radius = jnp.sqrt(x * x + y * y + z * z)
    rows = harmonics(x / radius, y / radius, z / radius) + index_rows
    for at, row in enumerate(rows):
        turned[at : at + 1, :] = row
    center = 0.5 + 4.0 * lax.broadcasted_iota(jnp.int32, (24, edges), 0).astype(F32) / (BASIS - 1)
    offset = (radius - center) / 0.4
    basis = jnp.exp(-(offset * offset))
    live = lax.broadcasted_iota(jnp.int32, (24, edges), 0) < BASIS
    basis_out[...] = jnp.where(live, basis, 0.0)
    return turned[...].T


def prepare_kernel(
    vectors,
    source,
    target,
    probe_vectors,
    probe_atoms,
    grid,
    probe_index,
    first,
    second,
    pfirst,
    psecond,
    columns_out,
    basis_out,
    pre_out,
    hidden3_out,
    hidden_rows_out,
    second3_out,
    pcolumns_out,
    pbasis_out,
    ppre_out,
    phidden3_out,
    phidden_rows_out,
    psecond3_out,
    picked_out,
    turned,
    pturned,
):
    turned[...] = jnp.zeros_like(turned)
    pturned[...] = jnp.zeros_like(pturned)
    row = source[...]
    slot = jnp.where(row > ATOMS, row - 1, jnp.where(row == ATOMS, 512, row))
    columns_out[...] = geometry(
        vectors[...], [slot.astype(F32), target[...].astype(F32)], EDGES, turned, basis_out
    )
    prow = probe_atoms[...]
    pslot = jnp.where(prow > ATOMS, prow - 1, jnp.where(prow == ATOMS, 512, prow))
    pcolumns_out[...] = geometry(
        probe_vectors[...], [pslot.astype(F32)], PEDGES, pturned, pbasis_out
    )

    for basis, layer, pre, hidden3, hidden_rows in (
        (basis_out, first, pre_out, hidden3_out, hidden_rows_out),
        (pbasis_out, pfirst, ppre_out, phidden3_out, phidden_rows_out),
    ):
        before = dot_tn(layer[...], basis[0:BASIS, :], HIGHEST)
        pre[...] = before.T
        hidden = before * sigmoid(before)
        upper, lower = split(hidden)
        hidden_rows[0:HIDDEN, :] = upper
        hidden_rows[HIDDEN : 2 * HIDDEN, :] = lower
        upper, lower = split(hidden.T)
        hidden3[:, 0:HIDDEN] = upper
        hidden3[:, HIDDEN : 2 * HIDDEN] = upper
        hidden3[:, 2 * HIDDEN : 3 * HIDDEN] = lower
    for degree in range(5):
        for path in range(2):
            upper, lower = split(second[:, cols(path * 5 + degree)])
            at = cols(2 * degree + path)
            second3_out[0:HIDDEN, at] = upper
            second3_out[HIDDEN : 2 * HIDDEN, at] = lower
            second3_out[2 * HIDDEN : 3 * HIDDEN, at] = upper
    upper, lower = split(psecond[...])
    psecond3_out[0:HIDDEN, :] = upper
    psecond3_out[HIDDEN : 2 * HIDDEN, :] = lower
    psecond3_out[2 * HIDDEN : 3 * HIDDEN, :] = upper

    place = probe_index[...]
    grid_row = lax.broadcasted_iota(jnp.int32, (grid.shape[0], PROBES), 0)
    hit = (place // C == grid_row).astype(F32)
    lines = dot_tn(grid[...], hit, HIGHEST)
    lane = lax.broadcasted_iota(jnp.int32, (C, PROBES), 0)
    values = jnp.sum(jnp.where(place % C == lane, lines, 0.0), axis=0, keepdims=True)
    picked_out[...] = jnp.broadcast_to(values, (C, PROBES)).T


def fill_ghosts(rows, base, low, high, left, right):
    pieces = (
        left[16:32],
        low[16:32],
        right[16:32],
        left[0:16],
        right[0:16],
        left[32:48],
        high[16:32],
        right[32:48],
    )
    for at, piece in enumerate(pieces):
        rows[base + 16 * at : base + 16 * at + 16, :] = piece


def comp_rows(component, count=1):
    return slice(component * ATOMS, (component + count) * ATOMS)


def wide_chunks():
    return [(at, min(at + 2, COMP)) for at in range(0, COMP, 2)]


def one_hot_lanes(column, width):
    lane = lax.broadcasted_iota(jnp.int32, (EB, width), 1).astype(F32)
    return (column == lane).astype(F32).astype(BF16)


def one_hot_rows(row, height):
    place = lax.broadcasted_iota(jnp.int32, (height, row.shape[1]), 0)
    return (row == place).astype(F32).astype(BF16)


def fold_source(row):
    return jnp.where(row > ATOMS, row - 1, jnp.where(row == ATOMS, 512, row))


def layer_kernel(
    own,
    low,
    high,
    left,
    right,
    columns,
    target,
    hidden3,
    second3,
    mixing,
    chosen,
    updated,
    gathered,
    mixed,
    table,
    low_out,
    middle_out,
    high_out,
    messages,
    lower_rows,
):
    table[0:ATOMS, :] = own[...]
    fill_ghosts(table, ATOMS, low, high, left, right)

    def block(step, carry):
        rows = pl.ds(pl.multiple_of(step * EB, EB), EB)
        column = columns[rows, :]
        pick = one_hot_lanes(column[:, 25:26], 2 * ATOMS)
        hidden = hidden3[rows, :]
        scalar = dot(pick, table[:, cols(0)])
        for degree in range(5):
            weight = dot(hidden, second3[:, 2 * degree * C : 2 * (degree + 1) * C])
            straight = weight[:, 0:C]
            cross = weight[:, C:] * scalar
            for first, last in chunks(degree):
                sender = dot(pick, table[:, first * C : last * C])
                for component in range(first, last):
                    value = sender[:, cols(component - first)]
                    message = straight * value + cross * column[:, component : component + 1]
                    messages[rows, cols(component)] = message.astype(BF16)
        return carry

    lax.fori_loop(0, EDGES // EB, block, 0)
    put = one_hot_rows(target[...], ATOMS)
    for first, last in wide_chunks():
        here = dot(put, messages[:, first * C : last * C]) * 0.125
        for component in range(first, last):
            upper, lower = split(here[:, cols(component - first)])
            gathered[comp_rows(component), :] = upper
            lower_rows[comp_rows(component), :] = lower
    gate = None
    for degree in range(5):
        upper, lower = split(mixing[degree])
        for component in range(STARTS[degree], STARTS[degree] + DEGREES[degree]):
            rows = comp_rows(component)
            out = dot(gathered[rows, :], upper)
            out += dot(lower_rows[rows, :], upper) + dot(gathered[rows, :], lower)
            mixed[rows, :] = out
            if component == 0:
                gate = sigmoid(out)
            new = own[:, cols(component)].astype(F32) + out * gate
            updated[:, cols(component)] = new.astype(BF16)
    send_packets(chosen[...], updated, low_out, middle_out, high_out)


def sum_table_grads(put, messages, own_grad, low, middle, high, add):
    for first, last in wide_chunks():
        wide = slice(first * C, last * C)
        total = dot(put, messages[:, wide])
        for component in range(first, last):
            here = total[0:ATOMS, cols(component - first)]
            if add is not None:
                here = here + add[comp_rows(component), :]
            own_grad[comp_rows(component), :] = here
        ghosts = total[ATOMS:, :].astype(BF16)
        low[:, wide] = ghosts[0:48]
        middle[:, wide] = ghosts[48:80]
        high[:, wide] = ghosts[80:128]


def probe_kernel(
    own,
    low,
    high,
    left,
    right,
    columns,
    atoms,
    hidden3,
    second3,
    first_readout,
    second_readout,
    picked,
    grad_own,
    low_out,
    middle_out,
    high_out,
    weight_grad,
    readout_grads,
    table,
    partial,
    contribution,
    messages,
):
    table[0:ATOMS, :] = own[...]
    fill_ghosts(table, ATOMS, low, high, left, right)

    def forward(step, carry):
        rows = pl.ds(pl.multiple_of(step * EB, EB), EB)
        column = columns[rows, :]
        pick = one_hot_lanes(column[:, 25:26], 2 * ATOMS)
        hidden = hidden3[rows, :]
        total = jnp.zeros((EB, C), F32)
        for degree in range(5):
            weight = dot(hidden, second3[:, cols(degree)])
            here = jnp.zeros((EB, C), F32)
            for first, last in chunks(degree):
                sender = dot(pick, table[:, first * C : last * C])
                for component in range(first, last):
                    value = sender[:, cols(component - first)]
                    here = here + value * column[:, component : component + 1]
            partial[rows, cols(degree)] = here
            total = total + weight * here
        contribution[rows, :] = total
        return carry

    lax.fori_loop(0, PEDGES // EB, forward, 0)

    edge = lax.broadcasted_iota(jnp.int32, (PROBES, PEDGES), 1)
    probe = lax.broadcasted_iota(jnp.int32, (PROBES, PEDGES), 0)
    pool = (edge // 4 == probe).astype(F32)
    summed = dot_exact(pool, contribution[...])
    before = dot_exact(summed, first_readout[...])
    gate = sigmoid(before)
    hidden = before * gate
    vector = second_readout[...]
    density = jnp.sum(hidden * vector, axis=1, keepdims=True)
    misfit = density - picked[...]
    loss = jnp.sum(misfit[:, 0:1] * misfit[:, 0:1], axis=0, keepdims=True) / (2.0 * PROBES)
    slope = misfit / PROBES
    d_before = slope * vector * gate * (1.0 + before * (1.0 - gate))
    readout_grads[0:C, :] = dot_tn(summed, d_before, HIGHEST)
    readout_grads[C : C + 8, :] = jnp.broadcast_to(
        jnp.sum(hidden * slope, axis=0, keepdims=True), (8, C)
    )
    readout_grads[C + 8 : C + 16, :] = jnp.broadcast_to(loss, (8, C))
    d_summed = dot_nt(d_before, first_readout[...], HIGHEST)
    contribution[...] = dot_tn(pool, d_summed, HIGHEST)

    def backward(step, carry):
        rows = pl.ds(pl.multiple_of(step * EB, EB), EB)
        column = columns[rows, :]
        hidden = hidden3[rows, :]
        slope_here = contribution[rows, :]
        for degree in range(5):
            weight = dot(hidden, second3[:, cols(degree)])
            weight_grad[rows, cols(degree)] = (slope_here * partial[rows, cols(degree)]).astype(BF16)
            down = slope_here * weight
            for component in range(STARTS[degree], STARTS[degree] + DEGREES[degree]):
                value = down * column[:, component : component + 1]
                messages[rows, cols(component)] = value.astype(BF16)
        return carry

    lax.fori_loop(0, PEDGES // EB, backward, 0)
    put = one_hot_rows(fold_source(atoms[...]), 2 * ATOMS)
    sum_table_grads(put, messages, grad_own, low_out, middle_out, high_out, None)


def network_grads(weight_grad, basis, pre, hidden_rows, second3):
    both = dot(hidden_rows[...], weight_grad[...])
    second = both[0:HIDDEN, :] + both[HIDDEN:, :]
    grads = weight_grad[...]
    d_hidden = dot_nt(grads, second3[0:HIDDEN, :]) + dot_nt(grads, second3[HIDDEN : 2 * HIDDEN, :])
    before = pre[...]
    gate = sigmoid(before)
    d_before = d_hidden * gate * (1.0 + before * (1.0 - gate))
    return second, dot_exact(basis[...], d_before)


def probe_network_kernel(weight_grad, basis, pre, hidden_rows, second3, readout_grads, out):
    second, first = network_grads(weight_grad, basis, pre, hidden_rows, second3)
    for degree in range(5):
        out[degree * HIDDEN : (degree + 1) * HIDDEN, :] = second[:, cols(degree)]
    out[320:464, :] = readout_grads[...]
    out[464:512, :] = jnp.zeros((48, C), F32)
    out[464:488, 0:HIDDEN] = first


def layer_back_kernel(
    core,
    grad_own,
    low,
    high,
    left,
    right,
    table,
    gathered,
    mixed,
    columns,
    basis,
    pre,
    hidden3,
    hidden_rows,
    second3,
    mixing,
    placed,
    probe_grads,
    grad_updated,
    d_gathered,
    mine_out,
    other_out,
    returned,
    upper_rows,
    lower_rows,
    weight_grad,
    reduced,
):
    fill_ghosts(returned, 0, low, high, left, right)
    for first, last in wide_chunks():
        back = dot(placed[...], returned[:, first * C : last * C])
        for component in range(first, last):
            rows = comp_rows(component)
            whole = grad_own[rows, :] + back[:, cols(component - first)]
            grad_updated[rows, :] = whole.astype(BF16)
    gate_in = mixed[comp_rows(0), :]
    gate = sigmoid(gate_in)
    d_gate = jnp.zeros((ATOMS, C), F32)
    for component in range(COMP - 1, -1, -1):
        rows = comp_rows(component)
        d_updated = grad_updated[rows, :].astype(F32)
        if component > 0:
            d_gate = d_gate + d_updated * mixed[rows, :]
            d_mixed = d_updated * gate
        else:
            d_mixed = d_updated * gate * (1.0 + gate_in * (1.0 - gate)) + d_gate * gate * (
                1.0 - gate
            )
        upper, lower = split(d_mixed)
        upper_rows[rows, :] = upper
        lower_rows[rows, :] = lower
    for degree in range(5):
        upper, lower = split(mixing[degree])
        rows = comp_rows(STARTS[degree], DEGREES[degree])
        reduced[640 + degree * C : 640 + (degree + 1) * C, :] = dot_tn(
            gathered[rows, :], upper_rows[rows, :]
        )
        for component in range(STARTS[degree], STARTS[degree] + DEGREES[degree]):
            rows = comp_rows(component)
            out = dot_nt(upper_rows[rows, :], upper)
            out += dot_nt(lower_rows[rows, :], upper) + dot_nt(upper_rows[rows, :], lower)
            d_gathered[:, cols(component)] = (out * 0.125).astype(BF16)

    def block(step, carry):
        rows = pl.ds(pl.multiple_of(step * EB, EB), EB)
        column = columns[rows, :]
        pick = one_hot_lanes(column[:, 25:26], 2 * ATOMS)
        pick_target = one_hot_lanes(column[:, 26:27], ATOMS)
        scalar = dot(pick, table[:, cols(0)])
        for degree in range(5):
            d_straight = jnp.zeros((EB, C), F32)
            d_cross = jnp.zeros((EB, C), F32)
            for first, last in chunks(degree):
                wide = slice(first * C, last * C)
                sender = dot(pick, table[:, wide])
                d_message = dot(pick_target, d_gathered[:, wide])
                for component in range(first, last):
                    here = cols(component - first)
                    d_here = d_message[:, here]
                    d_straight = d_straight + d_here * sender[:, here]
                    d_cross = d_cross + d_here * column[:, component : component + 1]
            weight_grad[rows, cols(2 * degree)] = d_straight.astype(BF16)
            weight_grad[rows, cols(2 * degree + 1)] = (d_cross * scalar).astype(BF16)
        return carry

    lax.fori_loop(0, EDGES // EB, block, 0)
    second, first = network_grads(weight_grad, basis, pre, hidden_rows, second3)
    for degree in range(5):
        for path in range(2):
            at = (path * 5 + degree) * HIDDEN
            reduced[at : at + HIDDEN, :] = second[:, cols(2 * degree + path)]
    reduced[1280:1792, :] = probe_grads[...]
    reduced[1792:REDUCE_ROWS, :] = jnp.zeros((REDUCE_ROWS - 1792, C), F32)
    reduced[1792:1816, 0:HIDDEN] = first
    half = REDUCE_ROWS // 2
    side = core[0]
    mine_out[...] = reduced[pl.ds(pl.multiple_of(side * half, half), half), :]
    other_out[...] = reduced[pl.ds(pl.multiple_of((1 - side) * half, half), half), :]


def table_back_kernel(
    grad_updated,
    d_gathered,
    columns,
    source,
    hidden3,
    second3,
    field_grad,
    low_out,
    middle_out,
    high_out,
    messages,
):
    def block(step, carry):
        rows = pl.ds(pl.multiple_of(step * EB, EB), EB)
        column = columns[rows, :]
        pick_target = one_hot_lanes(column[:, 26:27], ATOMS)
        hidden = hidden3[rows, :]
        d_scalar = jnp.zeros((EB, C), F32)
        for degree in (4, 3, 2, 1, 0):
            weight = dot(hidden, second3[:, 2 * degree * C : 2 * (degree + 1) * C])
            straight = weight[:, 0:C]
            d_cross = jnp.zeros((EB, C), F32)
            for first, last in chunks(degree):
                d_message = dot(pick_target, d_gathered[:, first * C : last * C])
                for component in range(first, last):
                    d_here = d_message[:, cols(component - first)]
                    d_cross = d_cross + d_here * column[:, component : component + 1]
                    value = straight * d_here
                    if component == 0:
                        value = value + d_scalar + d_cross * weight[:, C:]
                    messages[rows, cols(component)] = value.astype(BF16)
            d_scalar = d_scalar + d_cross * weight[:, C:]
        return carry

    lax.fori_loop(0, EDGES // EB, block, 0)
    put = one_hot_rows(fold_source(source[...]), 2 * ATOMS)
    sum_table_grads(put, messages, field_grad, low_out, middle_out, high_out, grad_updated)


def finish_kernel(field_grad, low, high, left, right, placed, out, returned):
    fill_ghosts(returned, 0, low, high, left, right)
    for first, last in wide_chunks():
        back = dot(placed[...], returned[:, first * C : last * C])
        for component in range(first, last):
            out[component] = field_grad[comp_rows(component), :] + back[:, cols(component - first)]


def unpack_kernel(
    core, mine, other, loss, first, second, mixing, pfirst, psecond, readout, vector, sums
):
    half = REDUCE_ROWS // 2
    side = core[0]
    sums[pl.ds(pl.multiple_of(side * half, half), half), :] = mine[...]
    sums[pl.ds(pl.multiple_of((1 - side) * half, half), half), :] = other[...]
    for block in range(10):
        second[:, cols(block)] = sums[block * HIDDEN : (block + 1) * HIDDEN, :]
    for degree in range(5):
        mixing[degree] = sums[640 + degree * C : 640 + (degree + 1) * C, :]
        psecond[:, cols(degree)] = sums[1280 + degree * HIDDEN : 1280 + (degree + 1) * HIDDEN, :]
    readout[...] = sums[1600:1728, :]
    vector[...] = sums[1728:1729, :]
    loss[...] = sums[1736:1737, :]
    pfirst[...] = sums[1744 : 1744 + BASIS, 0:HIDDEN]
    first[...] = sums[1792 : 1792 + BASIS, 0:HIDDEN]


def call(kernel, outs, scratch, flops, *operands):
    shapes = [jax.ShapeDtypeStruct(shape, dtype) for shape, dtype in outs]
    moved = sum(x.size * x.dtype.itemsize for x in list(operands) + shapes)
    whole = pl.BlockSpec(memory_space=pltpu.VMEM)
    scalar = pl.BlockSpec(memory_space=pltpu.SMEM)
    return pl.pallas_call(
        kernel,
        out_shape=shapes,
        in_specs=[scalar if x.shape == (1,) else whole for x in operands],
        out_specs=[whole] * len(shapes),
        scratch_shapes=[pltpu.VMEM(shape, dtype) for shape, dtype in scratch],
        compiler_params=pltpu.CompilerParams(vmem_limit_bytes=50 * 1024 * 1024),
        cost_estimate=pl.CostEstimate(flops=flops, bytes_accessed=moved, transcendentals=0),
    )(*operands)


PACKETS = [((48, WIDE), BF16), ((32, WIDE), BF16), ((48, WIDE), BF16)]


def ring(axis):
    count = lax.axis_size(axis)
    up = [(i, (i + 1) % count) for i in range(count)]
    down = [(b, a) for a, b in up]
    return up, down


def exchange(low_packet, middle_packet, high_packet):
    up, down = ring("bx")
    low = lax.ppermute(high_packet, "bx", up)
    high = lax.ppermute(low_packet, "bx", down)
    up, down = ring("by")
    left = lax.ppermute(
        jnp.concatenate([middle_packet[16:32], low[32:48], high[32:48]]), "by", up
    )
    right = lax.ppermute(jnp.concatenate([middle_packet[0:16], low[0:16], high[0:16]]), "by", down)
    return low, high, left, right


def reduce_halves(mine, other):
    n_x, n_y = lax.axis_size("bx"), lax.axis_size("by")
    count = n_x * n_y // 2
    axes = ("bx", "by")
    swap = [(i, i ^ 1) for i in range(n_y)]
    groups = [[2 * i + core for i in range(count)] for core in range(2)]
    pair = (mine + lax.ppermute(other, "by", swap)).reshape(count, -1, C)

    def finish():
        pieces = lax.all_to_all(pair, axes, 0, 0, axis_index_groups=groups, tiled=True)
        share = jnp.sum(pieces, axis=0)
        spread = jnp.broadcast_to(share[None], pair.shape)
        whole = lax.all_to_all(spread, axes, 0, 0, axis_index_groups=groups, tiled=True)
        whole = whole.reshape(mine.shape)
        return whole, lax.ppermute(whole, "by", swap)

    return pair, finish


def on_device(
    features,
    send_index,
    atom_vectors,
    atom_source,
    atom_target,
    probe_vectors,
    probe_atoms,
    density_grid,
    probe_index,
    radial_first,
    radial_second,
    mixing,
    probe_first,
    probe_second,
    readout_first,
    readout_second,
):
    field = features[0, 0].transpose(1, 0, 2)
    source = atom_source.reshape(1, EDGES)
    target = atom_target.reshape(1, EDGES)
    atoms = probe_atoms.reshape(1, PEDGES)
    core = (lax.axis_index("by") % 2).reshape(1)

    own, low, middle, high, chosen, placed = call(
        pack_kernel,
        [((ATOMS, WIDE), BF16)] + PACKETS + [((C, ATOMS), BF16), ((ATOMS, C), BF16)],
        [((C, C), F32)],
        2 * C * C * WIDE,
        field,
        send_index[0, 0],
    )
    received = exchange(low, middle, high)
    (
        columns,
        basis,
        pre,
        hidden3,
        hidden_rows,
        second3,
        pcolumns,
        pbasis,
        ppre,
        phidden3,
        phidden_rows,
        psecond3,
        picked,
    ) = call(
        prepare_kernel,
        [
            ((EDGES, C), F32),
            ((24, EDGES), F32),
            ((EDGES, HIDDEN), F32),
            ((EDGES, 3 * HIDDEN), BF16),
            ((2 * HIDDEN, EDGES), BF16),
            ((3 * HIDDEN, 10 * C), BF16),
            ((PEDGES, C), F32),
            ((24, PEDGES), F32),
            ((PEDGES, HIDDEN), F32),
            ((PEDGES, 3 * HIDDEN), BF16),
            ((2 * HIDDEN, PEDGES), BF16),
            ((3 * HIDDEN, 5 * C), BF16),
            ((PROBES, C), F32),
        ],
        [((C, EDGES), F32), ((C, PEDGES), F32)],
        10**9,
        atom_vectors[0, 0],
        source,
        target,
        probe_vectors[0, 0],
        atoms,
        density_grid.reshape(-1, C),
        probe_index.reshape(1, PROBES),
        radial_first,
        radial_second,
        probe_first,
        probe_second,
    )
    updated, gathered, mixed, table, low, middle, high = call(
        layer_kernel,
        [
            ((ATOMS, WIDE), BF16),
            ((COMP * ATOMS, C), BF16),
            ((COMP * ATOMS, C), F32),
            ((2 * ATOMS, WIDE), BF16),
        ]
        + PACKETS,
        [((EDGES, WIDE), BF16), ((COMP * ATOMS, C), BF16)],
        4 * 10**9,
        own,
        *received,
        columns,
        target,
        hidden3,
        second3,
        mixing,
        chosen,
    )
    received = exchange(low, middle, high)
    grad_own, low, middle, high, weight_grad, readout_grads = call(
        probe_kernel,
        [((COMP * ATOMS, C), F32)]
        + PACKETS
        + [
            ((PEDGES, 5 * C), BF16),
            ((C + 16, C), F32),
        ],
        [
            ((2 * ATOMS, WIDE), BF16),
            ((PEDGES, 5 * C), F32),
            ((PEDGES, C), F32),
            ((PEDGES, WIDE), BF16),
        ],
        4 * 10**9,
        updated,
        *received,
        pcolumns,
        atoms,
        phidden3,
        psecond3,
        readout_first,
        readout_second.reshape(1, C),
        picked,
    )
    received = exchange(low, middle, high)
    (probe_grads,) = call(
        probe_network_kernel,
        [((512, C), F32)],
        [],
        10**9,
        weight_grad,
        pbasis,
        ppre,
        phidden_rows,
        psecond3,
        readout_grads,
    )
    grad_updated, d_gathered, mine, other = call(
        layer_back_kernel,
        [
            ((COMP * ATOMS, C), BF16),
            ((ATOMS, WIDE), BF16),
            ((REDUCE_ROWS // 2, C), F32),
            ((REDUCE_ROWS // 2, C), F32),
        ],
        [
            ((C, WIDE), BF16),
            ((COMP * ATOMS, C), BF16),
            ((COMP * ATOMS, C), BF16),
            ((EDGES, 10 * C), BF16),
            ((REDUCE_ROWS, C), F32),
        ],
        6 * 10**9,
        core,
        grad_own,
        *received,
        table,
        gathered,
        mixed,
        columns,
        basis,
        pre,
        hidden3,
        hidden_rows,
        second3,
        mixing,
        placed,
        probe_grads,
    )
    pair, finish_sums = reduce_halves(mine, other)
    _, grad_updated, d_gathered = lax.optimization_barrier((pair, grad_updated, d_gathered))
    field_grad, low, middle, high = call(
        table_back_kernel,
        [((COMP * ATOMS, C), F32)] + PACKETS,
        [((EDGES, WIDE), BF16)],
        4 * 10**9,
        grad_updated,
        d_gathered,
        columns,
        source,
        hidden3,
        second3,
    )
    received = exchange(low, middle, high)
    mine, other = finish_sums()
    (feature_grad,) = call(
        finish_kernel,
        [((COMP, ATOMS, C), F32)],
        [((C, WIDE), BF16)],
        2 * C * C * WIDE,
        field_grad,
        *received,
        placed,
    )
    loss, first, second, mixing_grad, pfirst, psecond, readout, vector = call(
        unpack_kernel,
        [
            ((1, C), F32),
            ((BASIS, HIDDEN), F32),
            ((HIDDEN, 10 * C), F32),
            ((5, C, C), F32),
            ((BASIS, HIDDEN), F32),
            ((HIDDEN, 5 * C), F32),
            ((C, C), F32),
            ((1, C), F32),
        ],
        [((REDUCE_ROWS, C), F32)],
        10**6,
        core,
        mine,
        other,
    )
    return (
        loss[0, 0],
        feature_grad.transpose(1, 0, 2)[None, None],
        first,
        second,
        mixing_grad,
        pfirst,
        psecond,
        readout,
        vector[0],
    )


def solution(mesh):
    brick = [P("bx", "by", *([None] * (rank - 2))) for rank in (5, 5, 4, 3, 3, 4, 3, 3, 3)]
    in_specs = tuple(brick) + (P(),) * 7
    out_specs = (P(), P("bx", "by", None, None, None)) + (P(),) * 7
    return jax.shard_map(
        on_device, mesh=mesh, in_specs=in_specs, out_specs=out_specs, check_vma=False
    )
```

profile of v0, /device:TPU:1, one launch (start us, length us, event | category | flops | bytes accessed | tf_op | source)
XLA Modules:
  0.0 189.2 jit_solution(1341691188052579304)
XLA Ops:
  0.6 0.7 copy.33
  1.3 1.1 copy-done.1
  2.5 0.0 copy-start.6
  2.5 0.0 copy-start.8
  2.5 0.0 copy-start.9
  2.5 0.0 copy-start.10
  2.5 0.0 copy-start.11
  2.6 0.5 shard_map.223
  3.1 3.8 %collective-permute-start = (bf16[48,3200]{1,0:T(8,128)(2,1)S(1)}, bf16[48,3200]{1,0:T(8,128)(2,1)S(1)}, u32[]{:S(2)}, u32[]{:S(2)}) collective-permute-start(bf16[48,3200]{1,0:T(8,128)(2,1)S(1)} %get-tuple-element.60), channel_id=1, source_target_pairs={{0,16},{16,32},{32,48},{48,64},{64,80},{80,96},{96,112},{112,0},{1... | collective-permute-start | bytes 921608 | tf_op jit(solution)/shard_map/ppermute | solution.py:635
  6.9 2.3 %collective-permute-start.1 = (bf16[48,3200]{1,0:T(8,128)(2,1)S(1)}, bf16[48,3200]{1,0:T(8,128)(2,1)S(1)}, u32[]{:S(2)}, u32[]{:S(2)}) collective-permute-start(bf16[48,3200]{1,0:T(8,128)(2,1)S(1)} %get-tuple-element.61), channel_id=1, source_target_pairs={{16,0},{32,16},{48,32},{64,48},{80,64},{96,80},{112,96},{0,112},{1... | collective-permute-start | bytes 921608 | tf_op jit(solution)/shard_map/ppermute | solution.py:636
  9.2 10.2 %collective-permute-done.low = bf16[48,3200]{1,0:T(8,128)(2,1)S(1)} collective-permute-done((bf16[48,3200]{1,0:T(8,128)(2,1)S(1)}, bf16[48,3200]{1,0:T(8,128)(2,1)S(1)}, u32[]{:S(2)}, u32[]{:S(2)}) %collective-permute-start) | collective-permute-done | bytes 307232 | tf_op jit(solution)/shard_map/ppermute | solution.py:635
  19.5 4.0 %collective-permute-done.1.high = bf16[48,3200]{1,0:T(8,128)(2,1)S(1)} collective-permute-done((bf16[48,3200]{1,0:T(8,128)(2,1)S(1)}, bf16[48,3200]{1,0:T(8,128)(2,1)S(1)}, u32[]{:S(2)}, u32[]{:S(2)}) %collective-permute-start.1) | collective-permute-done | bytes 307232 | tf_op jit(solution)/shard_map/ppermute | solution.py:636
  23.5 0.6 collective-permute-start.3
  24.1 1.6 collective-permute-start.2
  25.8 0.0 copy-start.4
  25.8 2.5 %shard_map.224 = (f32[1024,128]{1,0:T(8,128)S(1)}, f32[24,1024]{1,0:T(8,128)S(1)}, f32[1024,64]{1,0:T(8,128)S(1)}, bf16[1024,192]{1,0:T(8,128)(2,1)}, bf16[128,1...) custom-call(f32[3,1024]{1,0:T(4,128)S(1)} %bitcast.31, ...), custom_call_target="tpu_custom_call" | custom-call | flops 1000000000 | bytes 3774976 | tf_op jit(solution)/shard_map/pallas_call | solution.py:612
  28.3 0.8 copy-done.19
  29.1 0.7 copy-done.22
  29.8 0.6 copy-done.24
  30.5 0.6 copy-done.26
  31.1 1.2 copy-done.17
  32.4 9.2 %shard_map.225 = (bf16[128,3200]{1,0:T(8,128)(2,1)}, bf16[3200,128]{1,0:T(8,128)(2,1)}, f32[3200,128]{1,0:T(8,128)}, bf16[256,3200]{1,0:T(8,128)(2,1)}, bf16[48,...) custom-call(bf16[128,3200]{1,0:T(8,128)(2,1)} %copy-done.2, ...), custom_call_target="tpu_custom_call" | custom-call | flops 4000000000 | bytes 9555968 | tf_op jit(solution)/shard_map/pallas_call | solution.py:612
  41.6 0.8 copy-done.20
  42.4 0.8 collective-permute-start.4
  43.2 4.3 %collective-permute-start.5 = (bf16[48,3200]{1,0:T(8,128)(2,1)S(1)}, bf16[48,3200]{1,0:T(8,128)(2,1)S(1)}, u32[]{:S(2)}, u32[]{:S(2)}) collective-permute-start(bf16[48,3200]{1,0:T(8,128)(2,1)S(1)} %get-tuple-element.69), channel_id=1, source_target_pairs={{16,0},{32,16},{48,32},{64,48},{80,64},{96,80},{112,96},{0,112},{1... | collective-permute-start | bytes 921608 | tf_op jit(solution)/shard_map/ppermute | solution.py:636
  47.5 4.3 %collective-permute-done.4.low = bf16[48,3200]{1,0:T(8,128)(2,1)S(1)} collective-permute-done((bf16[48,3200]{1,0:T(8,128)(2,1)S(1)}, bf16[48,3200]{1,0:T(8,128)(2,1)S(1)}, u32[]{:S(2)}, u32[]{:S(2)}) %collective-permute-start.4) | collective-permute-done | bytes 307232 | tf_op jit(solution)/shard_map/ppermute | solution.py:635
  51.8 6.5 %collective-permute-done.5.high = bf16[48,3200]{1,0:T(8,128)(2,1)S(1)} collective-permute-done((bf16[48,3200]{1,0:T(8,128)(2,1)S(1)}, bf16[48,3200]{1,0:T(8,128)(2,1)S(1)}, u32[]{:S(2)}, u32[]{:S(2)}) %collective-permute-start.5) | collective-permute-done | bytes 307232 | tf_op jit(solution)/shard_map/ppermute | solution.py:636
  58.4 2.7 %collective-permute-start.7 = (bf16[48,3200]{1,0:T(8,128)(2,1)S(1)}, bf16[48,3200]{1,0:T(8,128)(2,1)S(1)}, u32[]{:S(2)}, u32[]{:S(2)}) collective-permute-start(bf16[48,3200]{1,0:T(8,128)(2,1)S(1)} %pad_maximum_fusion.3), channel_id=1, source_target_pairs={{1,0},{2,1},{3,2},{4,3},{5,4},{6,5},{7,6},{8,7},{9,8},{10,9},{11,1... | collective-permute-start | bytes 921608 | tf_op jit(solution)/shard_map/ppermute | solution.py:641
  61.1 1.6 collective-permute-start.6
  62.7 4.2 %collective-permute-done.7.right = bf16[48,3200]{1,0:T(8,128)(2,1)S(1)} collective-permute-done((bf16[48,3200]{1,0:T(8,128)(2,1)S(1)}, bf16[48,3200]{1,0:T(8,128)(2,1)S(1)}, u32[]{:S(2)}, u32[]{:S(2)}) %collective-permute-start.7) | collective-permute-done | bytes 307232 | tf_op jit(solution)/shard_map/ppermute | solution.py:641
  66.9 9.2 %shard_map.226 = (f32[3200,128]{1,0:T(8,128)}, bf16[48,3200]{1,0:T(8,128)(2,1)S(1)}, bf16[32,3200]{1,0:T(8,128)(2,1)S(1)}, bf16[48,3200]{1,0:T(8,128)(2,1)S(1)},...) custom-call(bf16[128,3200]{1,0:T(8,128)(2,1)} %get-tuple-element.67.own, ...), custom_call_target="tpu_custom_call" | custom-call | flops 4000000000 | bytes 6072832 | tf_op jit(solution)/shard_map/pallas_call | solution.py:612
  76.1 5.1 %collective-permute-start.9 = (bf16[48,3200]{1,0:T(8,128)(2,1)S(1)}, bf16[48,3200]{1,0:T(8,128)(2,1)S(1)}, u32[]{:S(2)}, u32[]{:S(2)}) collective-permute-start(bf16[48,3200]{1,0:T(8,128)(2,1)S(1)} %get-tuple-element.77), channel_id=1, source_target_pairs={{16,0},{32,16},{48,32},{64,48},{80,64},{96,80},{112,96},{0,112},{1... | collective-permute-start | bytes 921608 | tf_op jit(solution)/shard_map/ppermute | solution.py:636
  81.2 4.3 %collective-permute-done.8.low = bf16[48,3200]{1,0:T(8,128)(2,1)S(1)} collective-permute-done((bf16[48,3200]{1,0:T(8,128)(2,1)S(1)}, bf16[48,3200]{1,0:T(8,128)(2,1)S(1)}, u32[]{:S(2)}, u32[]{:S(2)}) %collective-permute-start.8) | collective-permute-done | bytes 307232 | tf_op jit(solution)/shard_map/ppermute | solution.py:635
  85.6 1.1 collective-permute-done.9.high
  86.6 0.7 pad_maximum_fusion.5
  87.4 8.1 %collective-permute-start.11 = (bf16[48,3200]{1,0:T(8,128)(2,1)}, bf16[48,3200]{1,0:T(8,128)(2,1)S(1)}, u32[]{:S(2)}, u32[]{:S(2)}) collective-permute-start(bf16[48,3200]{1,0:T(8,128)(2,1)} %pad_maximum_fusion.5), channel_id=1, source_target_pairs={{1,0},{2,1},{3,2},{4,3},{5,4},{6,5},{7,6},{8,7},{9,8},{10,9},{11,1... | collective-permute-start | bytes 921608 | tf_op jit(solution)/shard_map/ppermute | solution.py:641
  95.5 0.7 pad_maximum_fusion.4
  96.2 0.8 collective-permute-start.10
  97.1 0.8 shard_map.227.probe_grads
  97.9 3.2 %collective-permute-done.11.right = bf16[48,3200]{1,0:T(8,128)(2,1)S(1)} collective-permute-done((bf16[48,3200]{1,0:T(8,128)(2,1)}, bf16[48,3200]{1,0:T(8,128)(2,1)S(1)}, u32[]{:S(2)}, u32[]{:S(2)}) %collective-permute-start.11) | collective-permute-done | bytes 307232 | tf_op jit(solution)/shard_map/ppermute | solution.py:641
  101.0 0.8 collective-permute-done.10.left
  101.9 13.6 %shard_map.228 = (bf16[3200,128]{1,0:T(8,128)(2,1)}, bf16[128,3200]{1,0:T(8,128)(2,1)}, f32[1024,128]{1,0:T(8,128)S(1)}, f32[1024,128]{1,0:T(8,128)S(1)}) custom-call(s32[1]{0:T(128)} %bitcast.core, f32[3200,128]{1,0:T(8,128)} %get-tuple-element.75.grad_own, bf16[48,3200]{1,0:T(8,128)(2,1)S(1)} %collective-permute-done.8.low, ...), custom_call_target="tpu_custom_call" | custom-call | flops 6000000000 | bytes 12304388 | tf_op jit(solution)/shard_map/pallas_call | solution.py:612
  115.5 7.4 %collective-permute-start.12 = (f32[1024,128]{1,0:T(8,128)S(1)}, f32[1024,128]{1,0:T(8,128)S(1)}, u32[]{:S(2)}, u32[]{:S(2)}) collective-permute-start(f32[1024,128]{1,0:T(8,128)S(1)} %get-tuple-element.92), channel_id=1, source_target_pairs={{0,1},{1,0},{2,3},{3,2},{4,5},{5,4},{6,7},{7,6},{8,9},{9,8},{10,11... | collective-permute-start | bytes 1572872 | tf_op jit(solution)/shard_map/ppermute | solution.py:651
  122.9 1.5 collective-permute-done.12
  124.4 0.9 add.8
  125.3 5.7 %all-to-all-start = ((f32[64,16,128]{2,1,0:T(8,128)}), f32[64,16,128]{2,1,0:T(8,128)}, u32[]{:S(2)}, u32[]{:S(2)}) async-start(f32[64,16,128]{2,1,0:T(8,128)} %bitcast.42), calls=%async_computation | async-start | bytes 1048576 | tf_op jit(solution)/shard_map/all_to_all | solution.py:654
  131.0 1.1 copy-done.29
  132.2 7.4 %shard_map.230 = (f32[3200,128]{1,0:T(8,128)}, bf16[48,3200]{1,0:T(8,128)(2,1)S(1)}, bf16[32,3200]{1,0:T(8,128)(2,1)S(1)}, bf16[48,3200]{1,0:T(8,128)(2,1)S(1)}) custom-call(bf16[3200,128]{1,0:T(8,128)(2,1)S(1)} %copy-done.28, bf16[128,3200]{1,0:T(8,128)(2,1)S(1)} %copy-done.29, f32[1024,128]{1,0:T(8,128)S(1)} %copy-done.16, s32[1,1024]{1,0:T(1,128)S(1)} %bitcast.37, ...), custom_call_target="tpu_custom_call" | custom-call | flops 4000000000 | bytes 5509120 | tf_op jit(solution)/shard_map/pallas_call | solution.py:612
  139.6 2.4 %collective-permute-start.14 = (bf16[48,3200]{1,0:T(8,128)(2,1)S(1)}, bf16[48,3200]{1,0:T(8,128)(2,1)S(1)}, u32[]{:S(2)}, u32[]{:S(2)}) collective-permute-start(bf16[48,3200]{1,0:T(8,128)(2,1)S(1)} %get-tuple-element.99), channel_id=1, source_target_pairs={{0,16},{16,32},{32,48},{48,64},{64,80},{80,96},{96,112},{112,0},{1... | collective-permute-start | bytes 921608 | tf_op jit(solution)/shard_map/ppermute | solution.py:635
  142.0 2.7 %collective-permute-start.15 = (bf16[48,3200]{1,0:T(8,128)(2,1)S(1)}, bf16[48,3200]{1,0:T(8,128)(2,1)S(1)}, u32[]{:S(2)}, u32[]{:S(2)}) collective-permute-start(bf16[48,3200]{1,0:T(8,128)(2,1)S(1)} %get-tuple-element.100), channel_id=1, source_target_pairs={{16,0},{32,16},{48,32},{64,48},{80,64},{96,80},{112,96},{0,112},{1... | collective-permute-start | bytes 921608 | tf_op jit(solution)/shard_map/ppermute | solution.py:636
  144.7 9.8 %collective-permute-done.14.low = bf16[48,3200]{1,0:T(8,128)(2,1)S(1)} collective-permute-done((bf16[48,3200]{1,0:T(8,128)(2,1)S(1)}, bf16[48,3200]{1,0:T(8,128)(2,1)S(1)}, u32[]{:S(2)}, u32[]{:S(2)}) %collective-permute-start.14) | collective-permute-done | bytes 307232 | tf_op jit(solution)/shard_map/ppermute | solution.py:635
  154.5 1.1 reduce_sum.9
  155.6 0.8 broadcast_in_dim.4
  156.5 11.1 %all-to-all-start.1 = ((f32[64,16,128]{2,1,0:T(8,128)}), f32[64,16,128]{2,1,0:T(8,128)S(1)}, u32[]{:S(2)}, u32[]{:S(2)}) async-start(f32[64,16,128]{2,1,0:T(8,128)} %broadcast_in_dim.4), calls=%async_computation.1 | async-start | bytes 1048576 | tf_op jit(solution)/shard_map/all_to_all | solution.py:657
  167.6 0.7 fusion.1
  168.2 0.7 pad_maximum_fusion.7
  169.0 1.8 collective-permute-start.17
  170.8 7.7 %all-to-all-done.1 = f32[64,16,128]{2,1,0:T(8,128)S(1)} async-done(((f32[64,16,128]{2,1,0:T(8,128)}), f32[64,16,128]{2,1,0:T(8,128)S(1)}, u32[]{:S(2)}, u32[]{:S(2)}) %all-to-all-start.1) | async-done | bytes 524320 | tf_op jit(solution)/shard_map/all_to_all | solution.py:657
  178.5 3.1 %collective-permute-start.13 = (f32[1024,128]{1,0:T(8,128)S(1)}, f32[1024,128]{1,0:T(8,128)S(1)}, u32[]{:S(2)}, u32[]{:S(2)}) collective-permute-start(f32[1024,128]{1,0:T(8,128)S(1)} %bitcast.27), channel_id=1, source_target_pairs={{0,1},{1,0},{2,3},{3,2},{4,5},{5,4},{6,7},{7,6},{8,9},{9,8},{10,11... | collective-permute-start | bytes 1572872 | tf_op jit(solution)/shard_map/ppermute | solution.py:659
  181.6 0.9 pad_maximum_fusion.6
  182.5 0.4 collective-permute-start.16
  182.9 3.8 %collective-permute-done.16.left = bf16[48,3200]{1,0:T(8,128)(2,1)S(1)} collective-permute-done((bf16[48,3200]{1,0:T(8,128)(2,1)S(1)}, bf16[48,3200]{1,0:T(8,128)(2,1)S(1)}, u32[]{:S(2)}, u32[]{:S(2)}) %collective-permute-start.16) | collective-permute-done | bytes 307232 | tf_op jit(solution)/shard_map/ppermute | solution.py:638
  186.7 1.5 shard_map.231
  188.3 1.0 shard_map.229
  (75 shorter events, 0.4 us)
Async XLA Ops:
  1.3 1.1 copy-start.1
  2.5 23.2 %copy-start.30 = (f32[1,1,3,1024]{3,1,2,0:T(1,128)S(1)}, f32[1,1,3,1024]{3,1,2,0:T(1,128)}, u32[]{:S(2)}) copy-start(f32[1,1,3,1024]{3,1,2,0:T(1,128)} %param.18) | copy-start | bytes 36868
  2.5 23.2 %copy-start.31 = (f32[1,1,3,512]{3,1,2,0:T(1,128)S(1)}, f32[1,1,3,512]{3,1,2,0:T(1,128)}, u32[]{:S(2)}) copy-start(f32[1,1,3,512]{3,1,2,0:T(1,128)} %param.21) | copy-start | bytes 18436
  2.5 23.3 %copy-start.3 = (f32[64,1280]{1,0:T(8,128)S(1)}, f32[64,1280]{1,0:T(8,128)}, u32[]{:S(2)}) copy-start(f32[64,1280]{1,0:T(8,128)} %second.1) | copy-start | bytes 983044
  2.5 23.3 %copy-start.5 = (f32[64,640]{1,0:T(8,128)S(1)}, f32[64,640]{1,0:T(8,128)}, u32[]{:S(2)}) copy-start(f32[64,640]{1,0:T(8,128)} %psecond.1) | copy-start | bytes 491524
  2.5 23.3 %copy-start.6 = (f32[1,1,32768]{2,1,0:T(1,128)S(1)}, f32[1,1,32768]{2,1,0:T(1,128)}, u32[]{:S(2)}) copy-start(f32[1,1,32768]{2,1,0:T(1,128)} %param.23) | copy-start | bytes 393220
  2.5 23.3 %copy-start.8 = (f32[20,64]{1,0:T(8,128)S(1)}, f32[20,64]{1,0:T(8,128)}, u32[]{:S(2)}) copy-start(f32[20,64]{1,0:T(8,128)} %first.1) | copy-start | bytes 15364
  2.5 23.3 %copy-start.9 = (f32[20,64]{1,0:T(8,128)S(1)}, f32[20,64]{1,0:T(8,128)}, u32[]{:S(2)}) copy-start(f32[20,64]{1,0:T(8,128)} %pfirst.1) | copy-start | bytes 15364
  2.5 23.3 %copy-start.10 = (s32[1,1,1024]{2,1,0:T(1,128)S(1)}, s32[1,1,1024]{2,1,0:T(1,128)}, u32[]{:S(2)}) copy-start(s32[1,1,1024]{2,1,0:T(1,128)} %param.20) | copy-start | bytes 12292
  2.5 23.3 %copy-start.11 = (s32[1,1,1024]{2,1,0:T(1,128)S(1)}, s32[1,1,1024]{2,1,0:T(1,128)}, u32[]{:S(2)}) copy-start(s32[1,1,1024]{2,1,0:T(1,128)} %param.19) | copy-start | bytes 12292
  2.6 23.3 %copy-start.12 = (s32[1,1,512]{2,1,0:T(1,128)S(1)}, s32[1,1,512]{2,1,0:T(1,128)}, u32[]{:S(2)}) copy-start(s32[1,1,512]{2,1,0:T(1,128)} %param.22) | copy-start | bytes 6148
  2.6 23.3 %copy-start.13 = (s32[1,1,128]{2,1,0:T(1,128)S(1)}, s32[1,1,128]{2,1,0:T(1,128)}, u32[]{:S(2)}) copy-start(s32[1,1,128]{2,1,0:T(1,128)} %param.24) | copy-start | bytes 1540
  3.1 22.6 %copy-start.2 = (bf16[128,3200]{1,0:T(8,128)(2,1)}, bf16[128,3200]{1,0:T(8,128)(2,1)S(1)}, u32[]{:S(2)}) copy-start(bf16[128,3200]{1,0:T(8,128)(2,1)S(1)} %get-tuple-element.59.own) | copy-start | bytes 2457604
  3.1 16.3 %collective-permute-start = (bf16[48,3200]{1,0:T(8,128)(2,1)S(1)}, bf16[48,3200]{1,0:T(8,128)(2,1)S(1)}, u32[]{:S(2)}, u32[]{:S(2)}) collective-permute-start(bf16[48,3200]{1,0:T(8,128)(2,1)S(1)} %get-tuple-element.60), channel_id=1, source_target_pairs={{0,16},{16,32},{32,48},{48,64},{64,80},{80,96},{96,112},{112,0},{1... | collective-permute-start | bytes 921608 | tf_op jit(solution)/shard_map/ppermute | solution.py:635
  6.9 16.5 %collective-permute-start.1 = (bf16[48,3200]{1,0:T(8,128)(2,1)S(1)}, bf16[48,3200]{1,0:T(8,128)(2,1)S(1)}, u32[]{:S(2)}, u32[]{:S(2)}) collective-permute-start(bf16[48,3200]{1,0:T(8,128)(2,1)S(1)} %get-tuple-element.61), channel_id=1, source_target_pairs={{16,0},{32,16},{48,32},{64,48},{80,64},{96,80},{112,96},{0,112},{1... | collective-permute-start | bytes 921608 | tf_op jit(solution)/shard_map/ppermute | solution.py:636
  23.5 7.6 %collective-permute-start.3 = (bf16[48,3200]{1,0:T(8,128)(2,1)S(1)}, bf16[48,3200]{1,0:T(8,128)(2,1)S(1)}, u32[]{:S(2)}, u32[]{:S(2)}) collective-permute-start(bf16[48,3200]{1,0:T(8,128)(2,1)S(1)} %pad_maximum_fusion.1), channel_id=1, source_target_pairs={{1,0},{2,1},{3,2},{4,3},{5,4},{6,5},{7,6},{8,7},{9,8},{10,9},{11,1... | collective-permute-start | bytes 921608 | tf_op jit(solution)/shard_map/ppermute | solution.py:641
  24.1 7.0 %collective-permute-start.2 = (bf16[48,3200]{1,0:T(8,128)(2,1)S(1)}, bf16[48,3200]{1,0:T(8,128)(2,1)S(1)}, u32[]{:S(2)}, u32[]{:S(2)}) collective-permute-start(bf16[48,3200]{1,0:T(8,128)(2,1)S(1)} %pad_maximum_fusion), channel_id=1, source_target_pairs={{0,1},{1,2},{2,3},{3,4},{4,5},{5,6},{6,7},{7,8},{8,9},{9,10},{10,1... | collective-permute-start | bytes 921608 | tf_op jit(solution)/shard_map/ppermute | solution.py:638
  25.8 5.3 %copy-start.4 = (f32[5,128,128]{2,1,0:T(8,128)S(1)}, f32[5,128,128]{2,1,0:T(8,128)}, u32[]{:S(2)}) copy-start(f32[5,128,128]{2,1,0:T(8,128)} %mixing.3) | copy-start | bytes 983044
  28.3 0.8 copy-start.19
  29.1 0.7 copy-start.22
  29.8 0.6 copy-start.24
  30.5 0.6 copy-start.26
  31.1 10.5 %copy-start.15 = (f32[1024,128]{1,0:T(8,128)}, f32[1024,128]{1,0:T(8,128)S(1)}, u32[]{:S(2)}) copy-start(f32[1024,128]{1,0:T(8,128)S(1)} %get-tuple-element.63.columns) | copy-start | bytes 1572868
  31.1 1.2 copy-start.17
  41.6 0.8 copy-start.20
  42.4 24.5 %copy-start.7 = (f32[128,128]{1,0:T(8,128)S(1)}, f32[128,128]{1,0:T(8,128)}, u32[]{:S(2)}) copy-start(f32[128,128]{1,0:T(8,128)} %first_readout.1) | copy-start | bytes 196612
  42.4 24.5 %copy-start.14 = (f32[128]{0:T(128)S(1)}, f32[128]{0:T(128)}, u32[]{:S(2)}) copy-start(f32[128]{0:T(128)} %param.31) | copy-start | bytes 1540
  42.4 9.4 %collective-permute-start.4 = (bf16[48,3200]{1,0:T(8,128)(2,1)S(1)}, bf16[48,3200]{1,0:T(8,128)(2,1)S(1)}, u32[]{:S(2)}, u32[]{:S(2)}) collective-permute-start(bf16[48,3200]{1,0:T(8,128)(2,1)S(1)} %get-tuple-element.68), channel_id=1, source_target_pairs={{0,16},{16,32},{32,48},{48,64},{64,80},{80,96},{96,112},{112,0},{1... | collective-permute-start | bytes 921608 | tf_op jit(solution)/shard_map/ppermute | solution.py:635
  43.2 15.1 %collective-permute-start.5 = (bf16[48,3200]{1,0:T(8,128)(2,1)S(1)}, bf16[48,3200]{1,0:T(8,128)(2,1)S(1)}, u32[]{:S(2)}, u32[]{:S(2)}) collective-permute-start(bf16[48,3200]{1,0:T(8,128)(2,1)S(1)} %get-tuple-element.69), channel_id=1, source_target_pairs={{16,0},{32,16},{48,32},{64,48},{80,64},{96,80},{112,96},{0,112},{1... | collective-permute-start | bytes 921608 | tf_op jit(solution)/shard_map/ppermute | solution.py:636
  58.4 8.6 %collective-permute-start.7 = (bf16[48,3200]{1,0:T(8,128)(2,1)S(1)}, bf16[48,3200]{1,0:T(8,128)(2,1)S(1)}, u32[]{:S(2)}, u32[]{:S(2)}) collective-permute-start(bf16[48,3200]{1,0:T(8,128)(2,1)S(1)} %pad_maximum_fusion.3), channel_id=1, source_target_pairs={{1,0},{2,1},{3,2},{4,3},{5,4},{6,5},{7,6},{8,7},{9,8},{10,9},{11,1... | collective-permute-start | bytes 921608 | tf_op jit(solution)/shard_map/ppermute | solution.py:641
  61.1 5.8 %collective-permute-start.6 = (bf16[48,3200]{1,0:T(8,128)(2,1)S(1)}, bf16[48,3200]{1,0:T(8,128)(2,1)S(1)}, u32[]{:S(2)}, u32[]{:S(2)}) collective-permute-start(bf16[48,3200]{1,0:T(8,128)(2,1)S(1)} %pad_maximum_fusion.2), channel_id=1, source_target_pairs={{0,1},{1,2},{2,3},{3,4},{4,5},{5,6},{6,7},{7,8},{8,9},{9,10},{10,1... | collective-permute-start | bytes 921608 | tf_op jit(solution)/shard_map/ppermute | solution.py:638
  76.1 20.9 %copy-start.25 = (f32[24,512]{1,0:T(8,128)S(1)}, f32[24,512]{1,0:T(8,128)}, u32[]{:S(2)}) copy-start(f32[24,512]{1,0:T(8,128)} %copy-done.24) | copy-start | bytes 147460
  76.1 9.4 %collective-permute-start.8 = (bf16[48,3200]{1,0:T(8,128)(2,1)S(1)}, bf16[48,3200]{1,0:T(8,128)(2,1)S(1)}, u32[]{:S(2)}, u32[]{:S(2)}) collective-permute-start(bf16[48,3200]{1,0:T(8,128)(2,1)S(1)} %get-tuple-element.76), channel_id=1, source_target_pairs={{0,16},{16,32},{32,48},{48,64},{64,80},{80,96},{96,112},{112,0},{1... | collective-permute-start | bytes 921608 | tf_op jit(solution)/shard_map/ppermute | solution.py:635
  76.1 10.5 %collective-permute-start.9 = (bf16[48,3200]{1,0:T(8,128)(2,1)S(1)}, bf16[48,3200]{1,0:T(8,128)(2,1)S(1)}, u32[]{:S(2)}, u32[]{:S(2)}) collective-permute-start(bf16[48,3200]{1,0:T(8,128)(2,1)S(1)} %get-tuple-element.77), channel_id=1, source_target_pairs={{16,0},{32,16},{48,32},{64,48},{80,64},{96,80},{112,96},{0,112},{1... | collective-permute-start | bytes 921608 | tf_op jit(solution)/shard_map/ppermute | solution.py:636
  87.4 13.7 %collective-permute-start.11 = (bf16[48,3200]{1,0:T(8,128)(2,1)}, bf16[48,3200]{1,0:T(8,128)(2,1)S(1)}, u32[]{:S(2)}, u32[]{:S(2)}) collective-permute-start(bf16[48,3200]{1,0:T(8,128)(2,1)} %pad_maximum_fusion.5), channel_id=1, source_target_pairs={{1,0},{2,1},{3,2},{4,3},{5,4},{6,5},{7,6},{8,7},{9,8},{10,9},{11,1... | collective-permute-start | bytes 921608 | tf_op jit(solution)/shard_map/ppermute | solution.py:641
  96.2 5.6 %collective-permute-start.10 = (bf16[48,3200]{1,0:T(8,128)(2,1)}, bf16[48,3200]{1,0:T(8,128)(2,1)S(1)}, u32[]{:S(2)}, u32[]{:S(2)}) collective-permute-start(bf16[48,3200]{1,0:T(8,128)(2,1)} %pad_maximum_fusion.4), channel_id=1, source_target_pairs={{0,1},{1,2},{2,3},{3,4},{4,5},{5,6},{6,7},{7,8},{8,9},{9,10},{10,1... | collective-permute-start | bytes 921608 | tf_op jit(solution)/shard_map/ppermute | solution.py:638
  97.0 4.8 %copy-start.21 = (bf16[192,1280]{1,0:T(8,128)(2,1)S(1)}, bf16[192,1280]{1,0:T(8,128)(2,1)}, u32[]{:S(2)}) copy-start(bf16[192,1280]{1,0:T(8,128)(2,1)} %copy-done.20) | copy-start | bytes 1474564
  97.1 4.8 %copy-start.23 = (bf16[128,1024]{1,0:T(8,128)(2,1)S(1)}, bf16[128,1024]{1,0:T(8,128)(2,1)}, u32[]{:S(2)}) copy-start(bf16[128,1024]{1,0:T(8,128)(2,1)} %copy-done.22) | copy-start | bytes 786436
  97.1 4.8 %copy-start.27 = (f32[24,1024]{1,0:T(8,128)S(1)}, f32[24,1024]{1,0:T(8,128)}, u32[]{:S(2)}) copy-start(f32[24,1024]{1,0:T(8,128)} %copy-done.26) | copy-start | bytes 294916
  115.5 15.5 %copy-start.16 = (f32[1024,128]{1,0:T(8,128)S(1)}, f32[1024,128]{1,0:T(8,128)}, u32[]{:S(2)}) copy-start(f32[1024,128]{1,0:T(8,128)} %copy-done.15) | copy-start | bytes 1572868
  115.5 15.5 %copy-start.18 = (bf16[1024,192]{1,0:T(8,128)(2,1)S(1)}, bf16[1024,192]{1,0:T(8,128)(2,1)}, u32[]{:S(2)}) copy-start(bf16[1024,192]{1,0:T(8,128)(2,1)} %get-tuple-element.64.hidden3) | copy-start | bytes 1179652
  115.5 15.5 %copy-start.28 = (bf16[3200,128]{1,0:T(8,128)(2,1)S(1)}, bf16[3200,128]{1,0:T(8,128)(2,1)}, u32[]{:S(2)}) copy-start(bf16[3200,128]{1,0:T(8,128)(2,1)} %get-tuple-element.96.grad_updated) | copy-start | bytes 2457604
  115.5 8.9 %collective-permute-start.12 = (f32[1024,128]{1,0:T(8,128)S(1)}, f32[1024,128]{1,0:T(8,128)S(1)}, u32[]{:S(2)}, u32[]{:S(2)}) collective-permute-start(f32[1024,128]{1,0:T(8,128)S(1)} %get-tuple-element.92), channel_id=1, source_target_pairs={{0,1},{1,0},{2,3},{3,2},{4,5},{5,4},{6,7},{7,6},{8,9},{9,8},{10,11... | collective-permute-start | bytes 1572872 | tf_op jit(solution)/shard_map/ppermute | solution.py:651
  125.3 29.2 %all-to-all-start = ((f32[64,16,128]{2,1,0:T(8,128)}), f32[64,16,128]{2,1,0:T(8,128)}, u32[]{:S(2)}, u32[]{:S(2)}) async-start(f32[64,16,128]{2,1,0:T(8,128)} %bitcast.42), calls=%async_computation | async-start | bytes 1048576 | tf_op jit(solution)/shard_map/all_to_all | solution.py:654
  131.0 1.1 copy-start.29
  139.6 14.9 %collective-permute-start.14 = (bf16[48,3200]{1,0:T(8,128)(2,1)S(1)}, bf16[48,3200]{1,0:T(8,128)(2,1)S(1)}, u32[]{:S(2)}, u32[]{:S(2)}) collective-permute-start(bf16[48,3200]{1,0:T(8,128)(2,1)S(1)} %get-tuple-element.99), channel_id=1, source_target_pairs={{0,16},{16,32},{32,48},{48,64},{64,80},{80,96},{96,112},{112,0},{1... | collective-permute-start | bytes 921608 | tf_op jit(solution)/shard_map/ppermute | solution.py:635
  142.0 25.6 %collective-permute-start.15 = (bf16[48,3200]{1,0:T(8,128)(2,1)S(1)}, bf16[48,3200]{1,0:T(8,128)(2,1)S(1)}, u32[]{:S(2)}, u32[]{:S(2)}) collective-permute-start(bf16[48,3200]{1,0:T(8,128)(2,1)S(1)} %get-tuple-element.100), channel_id=1, source_target_pairs={{16,0},{32,16},{48,32},{64,48},{80,64},{96,80},{112,96},{0,112},{1... | collective-permute-start | bytes 921608 | tf_op jit(solution)/shard_map/ppermute | solution.py:636
  155.6 31.1 %copy-start = (f32[3200,128]{1,0:T(8,128)S(1)}, f32[3200,128]{1,0:T(8,128)}, u32[]{:S(2)}) copy-start(f32[3200,128]{1,0:T(8,128)} %get-tuple-element.98.field_grad) | copy-start | bytes 4915204
  156.5 22.0 %all-to-all-start.1 = ((f32[64,16,128]{2,1,0:T(8,128)}), f32[64,16,128]{2,1,0:T(8,128)S(1)}, u32[]{:S(2)}, u32[]{:S(2)}) async-start(f32[64,16,128]{2,1,0:T(8,128)} %broadcast_in_dim.4), calls=%async_computation.1 | async-start | bytes 1048576 | tf_op jit(solution)/shard_map/all_to_all | solution.py:657
  169.0 13.9 %collective-permute-start.17 = (bf16[48,3200]{1,0:T(8,128)(2,1)}, bf16[48,3200]{1,0:T(8,128)(2,1)S(1)}, u32[]{:S(2)}, u32[]{:S(2)}) collective-permute-start(bf16[48,3200]{1,0:T(8,128)(2,1)} %pad_maximum_fusion.7), channel_id=1, source_target_pairs={{1,0},{2,1},{3,2},{4,3},{5,4},{6,5},{7,6},{8,7},{9,8},{10,9},{11,1... | collective-permute-start | bytes 921608 | tf_op jit(solution)/shard_map/ppermute | solution.py:641
  178.5 9.8 %collective-permute-start.13 = (f32[1024,128]{1,0:T(8,128)S(1)}, f32[1024,128]{1,0:T(8,128)S(1)}, u32[]{:S(2)}, u32[]{:S(2)}) collective-permute-start(f32[1024,128]{1,0:T(8,128)S(1)} %bitcast.27), channel_id=1, source_target_pairs={{0,1},{1,0},{2,3},{3,2},{4,5},{5,4},{6,7},{7,6},{8,9},{9,8},{10,11... | collective-permute-start | bytes 1572872 | tf_op jit(solution)/shard_map/ppermute | solution.py:659
  182.5 4.2 %collective-permute-start.16 = (bf16[48,3200]{1,0:T(8,128)(2,1)S(1)}, bf16[48,3200]{1,0:T(8,128)(2,1)S(1)}, u32[]{:S(2)}, u32[]{:S(2)}) collective-permute-start(bf16[48,3200]{1,0:T(8,128)(2,1)S(1)} %pad_maximum_fusion.6), channel_id=1, source_target_pairs={{0,1},{1,2},{2,3},{3,4},{4,5},{5,6},{6,7},{7,8},{8,9},{9,10},{10,1... | collective-permute-start | bytes 921608 | tf_op jit(solution)/shard_map/ppermute | solution.py:638
where the time goes:
time: 193 us; the launch traced here: 189 us
  starting transfers between devices  66.2 us (34%)
  waiting for transfers between devices  61.4 us (32%)
  Pallas kernels  45.9 us (24%)
  local copies, waits for them, and re-layouts  9.57 us (5%)
  other arithmetic  5.24 us (3%)
    pallas_call x9, Pallas kernels, call(): pl.pallas_call(kernel, out_shape=shapes, in_specs=[scalar if x.shape == (...  45.9 us
    ppermute x4, waiting for transfers between devices, exchange(): low = lax.ppermute(high_packet, 'bx', up)  28.6 us
    ppermute x4, starting transfers between devices, exchange(): high = lax.ppermute(low_packet, 'bx', down)  14.3 us
    ppermute x4, starting transfers between devices, exchange(): lax.ppermute(jnp.concatenate([middle_packet[0:16], low[0:16], high[0:16]]...  13.2 us
    ppermute x4, waiting for transfers between devices, exchange(): high = lax.ppermute(low_packet, 'bx', down)  11.5 us
    all_to_all x1, starting transfers between devices, finish(): lax.all_to_all(spread, axes, 0, 0, axis_index_groups=groups, tiled=True)  11.1 us
    unnamed x67, local copies, waits for them, and re-layouts  7.91 us
    all_to_all x1, waiting for transfers between devices, finish(): lax.all_to_all(spread, axes, 0, 0, axis_index_groups=groups, tiled=True)  7.67 us
  transfers between devices with their start and end apart: 20, of which 13 were waited for; matrix products, arithmetic and copies ran while one was open for 3% of the time, Pallas kernels for 6%

commit v1 on v0

--- a/solution.py
+++ b/solution.py
@@ -2,6 +2,7 @@
 
 import jax
 import jax.numpy as jnp
+import numpy as np
 from jax import lax
 from jax.experimental import pallas as pl
 from jax.experimental.pallas import tpu as pltpu
@@ -436,34 +437,29 @@
     out[464:488, 0:HIDDEN] = first
 
 
-def layer_back_kernel(
-    core,
+def table_back_kernel(
     grad_own,
     low,
     high,
     left,
     right,
-    table,
-    gathered,
     mixed,
     columns,
-    basis,
-    pre,
+    source,
     hidden3,
-    hidden_rows,
     second3,
     mixing,
     placed,
-    probe_grads,
+    field_grad,
+    d_gathered,
+    d_mixed_out,
+    low_out,
+    middle_out,
+    high_out,
+    returned,
     grad_updated,
-    d_gathered,
-    mine_out,
-    other_out,
-    returned,
-    upper_rows,
     lower_rows,
-    weight_grad,
-    reduced,
+    messages,
 ):
     fill_ghosts(returned, 0, low, high, left, right)
     for first, last in wide_chunks():
@@ -486,19 +482,65 @@
                 1.0 - gate
             )
         upper, lower = split(d_mixed)
-        upper_rows[rows, :] = upper
+        d_mixed_out[rows, :] = upper
         lower_rows[rows, :] = lower
     for degree in range(5):
         upper, lower = split(mixing[degree])
+        for component in range(STARTS[degree], STARTS[degree] + DEGREES[degree]):
+            rows = comp_rows(component)
+            out = dot_nt(d_mixed_out[rows, :], upper)
+            out += dot_nt(lower_rows[rows, :], upper) + dot_nt(d_mixed_out[rows, :], lower)
+            d_gathered[:, cols(component)] = (out * 0.125).astype(BF16)
+
+    def block(step, carry):
+        rows = pl.ds(pl.multiple_of(step * EB, EB), EB)
+        column = columns[rows, :]
+        pick_target = one_hot_lanes(column[:, 26:27], ATOMS)
+        hidden = hidden3[rows, :]
+        d_scalar = jnp.zeros((EB, C), F32)
+        for degree in (4, 3, 2, 1, 0):
+            weight = dot(hidden, second3[:, 2 * degree * C : 2 * (degree + 1) * C])
+            straight = weight[:, 0:C]
+            d_cross = jnp.zeros((EB, C), F32)
+            for first, last in chunks(degree):
+                d_message = dot(pick_target, d_gathered[:, first * C : last * C])
+                for component in range(first, last):
+                    d_here = d_message[:, cols(component - first)]
+                    d_cross = d_cross + d_here * column[:, component : component + 1]
+                    value = straight * d_here
+                    if component == 0:
+                        value = value + d_scalar + d_cross * weight[:, C:]
+                    messages[rows, cols(component)] = value.astype(BF16)
+            d_scalar = d_scalar + d_cross * weight[:, C:]
+        return carry
+
+    lax.fori_loop(0, EDGES // EB, block, 0)
+    put = one_hot_rows(fold_source(source[...]), 2 * ATOMS)
+    sum_table_grads(put, messages, field_grad, low_out, middle_out, high_out, grad_updated)
+
+
+def weights_back_kernel(
+    core,
+    d_gathered,
+    d_mixed,
+    table,
+    gathered,
+    columns,
+    basis,
+    pre,
+    hidden_rows,
+    second3,
+    probe_grads,
+    mine_out,
+    other_out,
+    weight_grad,
+    reduced,
+):
+    for degree in range(5):
         rows = comp_rows(STARTS[degree], DEGREES[degree])
         reduced[640 + degree * C : 640 + (degree + 1) * C, :] = dot_tn(
-            gathered[rows, :], upper_rows[rows, :]
+            gathered[rows, :], d_mixed[rows, :]
         )
-        for component in range(STARTS[degree], STARTS[degree] + DEGREES[degree]):
-            rows = comp_rows(component)
-            out = dot_nt(upper_rows[rows, :], upper)
-            out += dot_nt(lower_rows[rows, :], upper) + dot_nt(upper_rows[rows, :], lower)
-            d_gathered[:, cols(component)] = (out * 0.125).astype(BF16)
 
     def block(step, carry):
         rows = pl.ds(pl.multiple_of(step * EB, EB), EB)
@@ -537,44 +579,13 @@
     other_out[...] = reduced[pl.ds(pl.multiple_of((1 - side) * half, half), half), :]
 
 
-def table_back_kernel(
-    grad_updated,
-    d_gathered,
-    columns,
-    source,
-    hidden3,
-    second3,
-    field_grad,
-    low_out,
-    middle_out,
-    high_out,
-    messages,
-):
-    def block(step, carry):
-        rows = pl.ds(pl.multiple_of(step * EB, EB), EB)
-        column = columns[rows, :]
-        pick_target = one_hot_lanes(column[:, 26:27], ATOMS)
-        hidden = hidden3[rows, :]
-        d_scalar = jnp.zeros((EB, C), F32)
-        for degree in (4, 3, 2, 1, 0):
-            weight = dot(hidden, second3[:, 2 * degree * C : 2 * (degree + 1) * C])
-            straight = weight[:, 0:C]
-            d_cross = jnp.zeros((EB, C), F32)
-            for first, last in chunks(degree):
-                d_message = dot(pick_target, d_gathered[:, first * C : last * C])
-                for component in range(first, last):
-                    d_here = d_message[:, cols(component - first)]
-                    d_cross = d_cross + d_here * column[:, component : component + 1]
-                    value = straight * d_here
-                    if component == 0:
-                        value = value + d_scalar + d_cross * weight[:, C:]
-                    messages[rows, cols(component)] = value.astype(BF16)
-            d_scalar = d_scalar + d_cross * weight[:, C:]
-        return carry
-
-    lax.fori_loop(0, EDGES // EB, block, 0)
-    put = one_hot_rows(fold_source(source[...]), 2 * ATOMS)
-    sum_table_grads(put, messages, field_grad, low_out, middle_out, high_out, grad_updated)
+def share_kernel(pieces, out):
+    count = pieces.shape[0]
+    total = pieces[0]
+    for at in range(1, count):
+        total = total + pieces[at]
+    for at in range(count):
+        out[at] = total
 
 
 def finish_kernel(field_grad, low, high, left, right, placed, out, returned):
@@ -607,6 +618,7 @@
 def call(kernel, outs, scratch, flops, *operands):
     shapes = [jax.ShapeDtypeStruct(shape, dtype) for shape, dtype in outs]
     moved = sum(x.size * x.dtype.itemsize for x in list(operands) + shapes)
+    held = sum(np.prod(shape) * jnp.dtype(dtype).itemsize for shape, dtype in scratch)
     whole = pl.BlockSpec(memory_space=pltpu.VMEM)
     scalar = pl.BlockSpec(memory_space=pltpu.SMEM)
     return pl.pallas_call(
@@ -615,12 +627,21 @@
         in_specs=[scalar if x.shape == (1,) else whole for x in operands],
         out_specs=[whole] * len(shapes),
         scratch_shapes=[pltpu.VMEM(shape, dtype) for shape, dtype in scratch],
-        compiler_params=pltpu.CompilerParams(vmem_limit_bytes=50 * 1024 * 1024),
+        compiler_params=pltpu.CompilerParams(vmem_limit_bytes=int(held) + 12 * 1024 * 1024),
         cost_estimate=pl.CostEstimate(flops=flops, bytes_accessed=moved, transcendentals=0),
     )(*operands)
 
 
 PACKETS = [((48, WIDE), BF16), ((32, WIDE), BF16), ((48, WIDE), BF16)]
+
+
+def relay_kernel(middle, low, high, to_right, to_left):
+    to_right[0:16, :] = middle[16:32, :]
+    to_right[16:32, :] = low[32:48, :]
+    to_right[32:48, :] = high[32:48, :]
+    to_left[0:16, :] = middle[0:16, :]
+    to_left[16:32, :] = low[0:16, :]
+    to_left[32:48, :] = high[0:16, :]
 
 
 def ring(axis):
@@ -635,11 +656,12 @@
     low = lax.ppermute(high_packet, "bx", up)
     high = lax.ppermute(low_packet, "bx", down)
     up, down = ring("by")
-    left = lax.ppermute(
-        jnp.concatenate([middle_packet[16:32], low[32:48], high[32:48]]), "by", up
-    )
-    right = lax.ppermute(jnp.concatenate([middle_packet[0:16], low[0:16], high[0:16]]), "by", down)
-    return low, high, left, right
+    to_right, to_left = call(
+        relay_kernel, [((48, WIDE), BF16)] * 2, [], 10**5, middle_packet, low, high
+    )
+    left = lax.ppermute(to_right, "by", up)
+    right = lax.ppermute(to_left, "by", down)
+    return (low, high, left, right), (to_right, to_left)
 
 
 def reduce_halves(mine, other):
@@ -649,16 +671,11 @@
     swap = [(i, i ^ 1) for i in range(n_y)]
     groups = [[2 * i + core for i in range(count)] for core in range(2)]
     pair = (mine + lax.ppermute(other, "by", swap)).reshape(count, -1, C)
-
-    def finish():
-        pieces = lax.all_to_all(pair, axes, 0, 0, axis_index_groups=groups, tiled=True)
-        share = jnp.sum(pieces, axis=0)
-        spread = jnp.broadcast_to(share[None], pair.shape)
-        whole = lax.all_to_all(spread, axes, 0, 0, axis_index_groups=groups, tiled=True)
-        whole = whole.reshape(mine.shape)
-        return whole, lax.ppermute(whole, "by", swap)
-
-    return pair, finish
+    pieces = lax.all_to_all(pair, axes, 0, 0, axis_index_groups=groups, tiled=True)
+    (spread,) = call(share_kernel, [(pair.shape, F32)], [], 10**6, pieces)
+    whole = lax.all_to_all(spread, axes, 0, 0, axis_index_groups=groups, tiled=True)
+    whole = whole.reshape(mine.shape)
+    return whole, lambda after: lax.ppermute(lax.optimization_barrier((whole, after))[0], "by", swap)
 
 
 def on_device(
@@ -693,7 +710,7 @@
         field,
         send_index[0, 0],
     )
-    received = exchange(low, middle, high)
+    received, _ = exchange(low, middle, high)
     (
         columns,
         basis,
@@ -759,7 +776,7 @@
         mixing,
         chosen,
     )
-    received = exchange(low, middle, high)
+    received, _ = exchange(low, middle, high)
     grad_own, low, middle, high, weight_grad, readout_grads = call(
         probe_kernel,
         [((COMP * ATOMS, C), F32)]
@@ -785,7 +802,7 @@
         readout_second.reshape(1, C),
         picked,
     )
-    received = exchange(low, middle, high)
+    received, _ = exchange(low, middle, high)
     (probe_grads,) = call(
         probe_network_kernel,
         [((512, C), F32)],
@@ -798,54 +815,49 @@
         psecond3,
         readout_grads,
     )
-    grad_updated, d_gathered, mine, other = call(
-        layer_back_kernel,
+    field_grad, d_gathered, d_mixed, low, middle, high = call(
+        table_back_kernel,
         [
+            ((COMP * ATOMS, C), F32),
+            ((ATOMS, WIDE), BF16),
             ((COMP * ATOMS, C), BF16),
-            ((ATOMS, WIDE), BF16),
-            ((REDUCE_ROWS // 2, C), F32),
-            ((REDUCE_ROWS // 2, C), F32),
-        ],
+        ]
+        + PACKETS,
         [
             ((C, WIDE), BF16),
             ((COMP * ATOMS, C), BF16),
             ((COMP * ATOMS, C), BF16),
-            ((EDGES, 10 * C), BF16),
-            ((REDUCE_ROWS, C), F32),
+            ((EDGES, WIDE), BF16),
         ],
         6 * 10**9,
-        core,
         grad_own,
         *received,
-        table,
-        gathered,
         mixed,
-        columns,
-        basis,
-        pre,
-        hidden3,
-        hidden_rows,
-        second3,
-        mixing,
-        placed,
-        probe_grads,
-    )
-    pair, finish_sums = reduce_halves(mine, other)
-    _, grad_updated, d_gathered = lax.optimization_barrier((pair, grad_updated, d_gathered))
-    field_grad, low, middle, high = call(
-        table_back_kernel,
-        [((COMP * ATOMS, C), F32)] + PACKETS,
-        [((EDGES, WIDE), BF16)],
-        4 * 10**9,
-        grad_updated,
-        d_gathered,
         columns,
         source,
         hidden3,
         second3,
-    )
-    received = exchange(low, middle, high)
-    mine, other = finish_sums()
+        mixing,
+        placed,
+    )
+    received, relays = exchange(low, middle, high)
+    mine, other = call(
+        weights_back_kernel,
+        [((REDUCE_ROWS // 2, C), F32), ((REDUCE_ROWS // 2, C), F32)],
+        [((EDGES, 10 * C), BF16), ((REDUCE_ROWS, C), F32)],
+        6 * 10**9,
+        core,
+        d_gathered,
+        d_mixed,
+        table,
+        gathered,
+        columns,
+        basis,
+        pre,
+        hidden_rows,
+        second3,
+        probe_grads,
+    )
     (feature_grad,) = call(
         finish_kernel,
         [((COMP, ATOMS, C), F32)],
@@ -855,6 +867,9 @@
         *received,
         placed,
     )
+    mine, other, *_ = lax.optimization_barrier((mine, other, received[0], received[1]))
+    mine, swapped = reduce_halves(mine, other)
+    other = swapped(feature_grad)
     loss, first, second, mixing_grad, pfirst, psecond, readout, vector = call(
         unpack_kernel,
         [

time: 193 us -> 174 us (0.902); the launches traced: 189 us -> 174 us
  starting transfers between devices: 66.2 us -> 38.9 us
  blocking collectives: 0 us -> 18.5 us
  Pallas kernels: 45.9 us -> 36.3 us
  waiting for transfers between devices: 61.4 us -> 68.7 us
  other arithmetic: 5.24 us -> 0.05 us
    all_to_all x0 -> x1, blocking collectives: none -> 18.5 us  [reduce_halves(): lax.all_to_all(pair, axes, 0, 0, axis_index_groups=groups, tiled=True)]
    ppermute x9, waiting for transfers between devices: 12 us -> 24.3 us  [the longest x4 12.3 us: exchange(): left = lax.ppermute(to_right, 'by', up)]
    all_to_all x2 -> x1, starting transfers between devices: 16.8 us -> 4.87 us  [reduce_halves(): lax.all_to_all(spread, axes, 0, 0, axis_index_groups=groups, tiled=True)]
    pallas_call x9 -> x14, Pallas kernels: 45.9 us -> 36.3 us  [call(): pl.pallas_call(kernel, out_shape=shapes, in_specs=[scalar if x.shape == (...]
    ppermute x9, starting transfers between devices: 20.7 us -> 12 us  [the longest x4 8.51 us: exchange(): left = lax.ppermute(to_right, 'by', up)]
    all_to_all x2 -> x1, waiting for transfers between devices: 7.68 us -> 0.01 us  [reduce_halves(): lax.all_to_all(spread, axes, 0, 0, axis_index_groups=groups, tiled=True)]
    ppermute x4, waiting for transfers between devices: 11.5 us -> 18.7 us  [exchange(): high = lax.ppermute(low_packet, 'bx', down)]
    ppermute x1, starting transfers between devices: 7.36 us -> 0.61 us  [reduce_halves(): pair = (mine + lax.ppermute(other, 'by', swap)).reshape(count, -1, C)]
  transfers between devices with their start and end apart: 20 -> 19, of which waited for: 13 -> 16; matrix products, arithmetic and copies ran while one was open for 3% -> 0% of each run, Pallas kernels for 6% -> 7%
where the time goes in v1:
time: 174 us
  waiting for transfers between devices  68.7 us (39%)
  starting transfers between devices  38.9 us (22%)
  Pallas kernels  36.3 us (21%)
  blocking collectives  18.5 us (11%)
  local copies, waits for them, and re-layouts  10.2 us (6%)
    pallas_call x14, Pallas kernels, call(): pl.pallas_call(kernel, out_shape=shapes, in_specs=[scalar if x.shape == (...  36.3 us
    ppermute x4, waiting for transfers between devices, exchange(): low = lax.ppermute(high_packet, 'bx', up)  24.1 us
    ppermute x4, waiting for transfers between devices, exchange(): high = lax.ppermute(low_packet, 'bx', down)  18.7 us
    all_to_all x1, blocking collectives, reduce_halves(): lax.all_to_all(pair, axes, 0, 0, axis_index_groups=groups, tiled=True)  18.5 us
    ppermute x4, starting transfers between devices, exchange(): high = lax.ppermute(low_packet, 'bx', down)  16.8 us
    ppermute x4, waiting for transfers between devices, exchange(): left = lax.ppermute(to_right, 'by', up)  12.3 us
    ppermute x4, waiting for transfers between devices, exchange(): right = lax.ppermute(to_left, 'by', down)  10.5 us
    unnamed x81, local copies, waits for them, and re-layouts  10.2 us
  transfers between devices with their start and end apart: 19, of which 16 were waited for; matrix products, arithmetic and copies ran while one was open for 0% of the time, Pallas kernels for 7%

profile of v1, /device:TPU:1, one launch (start us, length us, event | category | flops | bytes accessed | tf_op | source)
XLA Modules:
  0.0 173.6 jit_solution(4994518666649753512)
XLA Ops:
  0.7 0.7 copy.33
  1.4 1.1 copy-done
  2.5 0.0 copy-start.6
  2.5 0.0 copy-start.9
  2.5 0.0 copy-start.10
  2.6 0.0 copy-start.11
  2.6 0.0 copy-start.13
  2.6 0.5 shard_map.223
  3.1 3.8 %collective-permute-start = (bf16[48,3200]{1,0:T(8,128)(2,1)S(1)}, bf16[48,3200]{1,0:T(8,128)(2,1)S(1)}, u32[]{:S(2)}, u32[]{:S(2)}) collective-permute-start(bf16[48,3200]{1,0:T(8,128)(2,1)S(1)} %get-tuple-element.69), channel_id=1, source_target_pairs={{0,16},{16,32},{32,48},{48,64},{64,80},{80,96},{96,112},{112,0},{1... | collective-permute-start | bytes 921608 | tf_op jit(solution)/shard_map/ppermute | solution.py:656
  6.9 2.3 %collective-permute-start.1 = (bf16[48,3200]{1,0:T(8,128)(2,1)S(1)}, bf16[48,3200]{1,0:T(8,128)(2,1)S(1)}, u32[]{:S(2)}, u32[]{:S(2)}) collective-permute-start(bf16[48,3200]{1,0:T(8,128)(2,1)S(1)} %get-tuple-element.70), channel_id=1, source_target_pairs={{16,0},{32,16},{48,32},{64,48},{80,64},{96,80},{112,96},{0,112},{1... | collective-permute-start | bytes 921608 | tf_op jit(solution)/shard_map/ppermute | solution.py:657
  9.2 10.2 %collective-permute-done.low = bf16[48,3200]{1,0:T(8,128)(2,1)S(1)} collective-permute-done((bf16[48,3200]{1,0:T(8,128)(2,1)S(1)}, bf16[48,3200]{1,0:T(8,128)(2,1)S(1)}, u32[]{:S(2)}, u32[]{:S(2)}) %collective-permute-start) | collective-permute-done | bytes 307232 | tf_op jit(solution)/shard_map/ppermute | solution.py:656
  19.5 4.0 %collective-permute-done.1.high = bf16[48,3200]{1,0:T(8,128)(2,1)S(1)} collective-permute-done((bf16[48,3200]{1,0:T(8,128)(2,1)S(1)}, bf16[48,3200]{1,0:T(8,128)(2,1)S(1)}, u32[]{:S(2)}, u32[]{:S(2)}) %collective-permute-start.1) | collective-permute-done | bytes 307232 | tf_op jit(solution)/shard_map/ppermute | solution.py:657
  23.5 2.1 %collective-permute-start.2 = (bf16[48,3200]{1,0:T(8,128)(2,1)S(1)}, bf16[48,3200]{1,0:T(8,128)(2,1)S(1)}, u32[]{:S(2)}, u32[]{:S(2)}) collective-permute-start(bf16[48,3200]{1,0:T(8,128)(2,1)S(1)} %get-tuple-element.72), channel_id=1, source_target_pairs={{0,1},{1,2},{2,3},{3,4},{4,5},{5,6},{6,7},{7,8},{8,9},{9,10},{10,1... | collective-permute-start | bytes 921608 | tf_op jit(solution)/shard_map/ppermute | solution.py:662
  25.7 0.0 copy-start.2
  25.7 1.7 shard_map.225
  27.5 0.8 copy-done.19
  28.3 0.7 copy-done.25
  29.0 0.6 copy-done.33
  29.6 0.0 collective-permute-done.2.left
  29.6 2.5 %collective-permute-done.3.right = bf16[48,3200]{1,0:T(8,128)(2,1)S(1)} collective-permute-done((bf16[48,3200]{1,0:T(8,128)(2,1)S(1)}, bf16[48,3200]{1,0:T(8,128)(2,1)S(1)}, u32[]{:S(2)}, u32[]{:S(2)}) %collective-permute-start.3) | collective-permute-done | bytes 307232 | tf_op jit(solution)/shard_map/ppermute | solution.py:663
  32.2 6.6 %shard_map.226 = (bf16[128,3200]{1,0:T(8,128)(2,1)S(1)}, bf16[3200,128]{1,0:T(8,128)(2,1)S(1)}, f32[3200,128]{1,0:T(8,128)S(1)}, bf16[256,3200]{1,0:T(8,128)(2,1...) custom-call(bf16[128,3200]{1,0:T(8,128)(2,1)S(1)} %get-tuple-element.68.own, ...), custom_call_target="tpu_custom_call" | custom-call | flops 4000000000 | bytes 9555968 | tf_op jit(solution)/shard_map/pallas_call | solution.py:624
  38.8 0.9 copy-done.35
  39.7 0.7 collective-permute-start.4
  40.4 4.4 %collective-permute-start.5 = (bf16[48,3200]{1,0:T(8,128)(2,1)S(1)}, bf16[48,3200]{1,0:T(8,128)(2,1)S(1)}, u32[]{:S(2)}, u32[]{:S(2)}) collective-permute-start(bf16[48,3200]{1,0:T(8,128)(2,1)S(1)} %get-tuple-element.80), channel_id=1, source_target_pairs={{16,0},{32,16},{48,32},{64,48},{80,64},{96,80},{112,96},{0,112},{1... | collective-permute-start | bytes 921608 | tf_op jit(solution)/shard_map/ppermute | solution.py:657
  44.8 8.4 %collective-permute-done.4.low = bf16[48,3200]{1,0:T(8,128)(2,1)S(1)} collective-permute-done((bf16[48,3200]{1,0:T(8,128)(2,1)S(1)}, bf16[48,3200]{1,0:T(8,128)(2,1)S(1)}, u32[]{:S(2)}, u32[]{:S(2)}) %collective-permute-start.4) | collective-permute-done | bytes 307232 | tf_op jit(solution)/shard_map/ppermute | solution.py:656
  53.2 3.4 %collective-permute-done.5.high = bf16[48,3200]{1,0:T(8,128)(2,1)S(1)} collective-permute-done((bf16[48,3200]{1,0:T(8,128)(2,1)S(1)}, bf16[48,3200]{1,0:T(8,128)(2,1)S(1)}, u32[]{:S(2)}, u32[]{:S(2)}) %collective-permute-start.5) | collective-permute-done | bytes 307232 | tf_op jit(solution)/shard_map/ppermute | solution.py:657
  56.6 1.5 collective-permute-start.6
  58.1 0.4 collective-permute-start.7
  58.5 3.4 %collective-permute-done.6.left = bf16[48,3200]{1,0:T(8,128)(2,1)S(1)} collective-permute-done((bf16[48,3200]{1,0:T(8,128)(2,1)S(1)}, bf16[48,3200]{1,0:T(8,128)(2,1)S(1)}, u32[]{:S(2)}, u32[]{:S(2)}) %collective-permute-start.6) | collective-permute-done | bytes 307232 | tf_op jit(solution)/shard_map/ppermute | solution.py:662
  61.9 2.8 %collective-permute-done.7.right = bf16[48,3200]{1,0:T(8,128)(2,1)S(1)} collective-permute-done((bf16[48,3200]{1,0:T(8,128)(2,1)S(1)}, bf16[48,3200]{1,0:T(8,128)(2,1)S(1)}, u32[]{:S(2)}, u32[]{:S(2)}) %collective-permute-start.7) | collective-permute-done | bytes 307232 | tf_op jit(solution)/shard_map/ppermute | solution.py:663
  64.7 6.9 %shard_map.228 = (f32[3200,128]{1,0:T(8,128)S(1)}, bf16[48,3200]{1,0:T(8,128)(2,1)S(1)}, bf16[32,3200]{1,0:T(8,128)(2,1)S(1)}, bf16[48,3200]{1,0:T(8,128)(2,1)S(...) custom-call(bf16[128,3200]{1,0:T(8,128)(2,1)S(1)} %get-tuple-element.78.own, ...), custom_call_target="tpu_custom_call" | custom-call | flops 4000000000 | bytes 6072832 | tf_op jit(solution)/shard_map/pallas_call | solution.py:624
  71.6 0.0 copy-start.31
  71.6 1.2 copy-done.31
  72.8 5.1 %collective-permute-start.9 = (bf16[48,3200]{1,0:T(8,128)(2,1)S(1)}, bf16[48,3200]{1,0:T(8,128)(2,1)S(1)}, u32[]{:S(2)}, u32[]{:S(2)}) collective-permute-start(bf16[48,3200]{1,0:T(8,128)(2,1)S(1)} %get-tuple-element.90), channel_id=1, source_target_pairs={{16,0},{32,16},{48,32},{64,48},{80,64},{96,80},{112,96},{0,112},{1... | collective-permute-start | bytes 921608 | tf_op jit(solution)/shard_map/ppermute | solution.py:657
  77.8 5.4 %collective-permute-done.8.low = bf16[48,3200]{1,0:T(8,128)(2,1)S(1)} collective-permute-done((bf16[48,3200]{1,0:T(8,128)(2,1)S(1)}, bf16[48,3200]{1,0:T(8,128)(2,1)S(1)}, u32[]{:S(2)}, u32[]{:S(2)}) %collective-permute-start.8) | collective-permute-done | bytes 307232 | tf_op jit(solution)/shard_map/ppermute | solution.py:656
  83.3 4.9 %collective-permute-done.9.high = bf16[48,3200]{1,0:T(8,128)(2,1)S(1)} collective-permute-done((bf16[48,3200]{1,0:T(8,128)(2,1)S(1)}, bf16[48,3200]{1,0:T(8,128)(2,1)S(1)}, u32[]{:S(2)}, u32[]{:S(2)}) %collective-permute-start.9) | collective-permute-done | bytes 307232 | tf_op jit(solution)/shard_map/ppermute | solution.py:657
  88.2 1.6 collective-permute-start.10
  89.8 1.1 collective-permute-start.11
  90.9 0.9 copy-done.16
  91.9 0.8 shard_map.231.probe_grads
  92.7 0.9 collective-permute-done.10.left
  93.6 2.8 %collective-permute-done.11.right = bf16[48,3200]{1,0:T(8,128)(2,1)S(1)} collective-permute-done((bf16[48,3200]{1,0:T(8,128)(2,1)S(1)}, bf16[48,3200]{1,0:T(8,128)(2,1)S(1)}, u32[]{:S(2)}, u32[]{:S(2)}) %collective-permute-start.11) | collective-permute-done | bytes 307232 | tf_op jit(solution)/shard_map/ppermute | solution.py:663
  96.4 0.7 copy-done.3
  97.1 1.0 copy-done.4
  98.1 1.4 copy-done.32
  99.5 8.5 %shard_map.230 = (f32[3200,128]{1,0:T(8,128)S(1)}, bf16[128,3200]{1,0:T(8,128)(2,1)S(1)}, bf16[3200,128]{1,0:T(8,128)(2,1)S(1)}, bf16[48,3200]{1,0:T(8,128)(2,1)...) custom-call(f32[3200,128]{1,0:T(8,128)S(1)} %copy-done.32, ...), custom_call_target="tpu_custom_call" | custom-call | flops 6000000000 | bytes 10375168 | tf_op jit(solution)/shard_map/pallas_call | solution.py:624
  108.1 0.1 collective-permute-start.12
  108.1 5.1 %collective-permute-start.13 = (bf16[48,3200]{1,0:T(8,128)(2,1)S(1)}, bf16[48,3200]{1,0:T(8,128)(2,1)S(1)}, u32[]{:S(2)}, u32[]{:S(2)}) collective-permute-start(bf16[48,3200]{1,0:T(8,128)(2,1)S(1)} %get-tuple-element.111), channel_id=1, source_target_pairs={{16,0},{32,16},{48,32},{64,48},{80,64},{96,80},{112,96},{0,112},{1... | collective-permute-start | bytes 921608 | tf_op jit(solution)/shard_map/ppermute | solution.py:657
  113.2 7.6 %shard_map.232 = (f32[1024,128]{1,0:T(8,128)S(1)}, f32[1024,128]{1,0:T(8,128)S(1)}) custom-call(s32[1]{0:T(128)} %bitcast.core, bf16[128,3200]{1,0:T(8,128)(2,1)S(1)} %get-tuple-element.96.d_gathered, bf16[3200,128]{1,0:T(8,128)(2,1)S(1)} %get-tuple-element.97.d_mixed, bf16[256,3200]{1,0:T(8,128)(2,1)S(1)} %copy-done.28, bf16[3200,128]{1,0:T(8,128)(2,1)S(1)} %copy-done.36, ...), custom_call_target="tpu_custom_call" | custom-call | flops 6000000000 | bytes 7045124 | tf_op jit(solution)/shard_map/pallas_call | solution.py:624
  120.9 0.0 collective-permute-done.12.low
  120.9 6.4 %collective-permute-done.13.high = bf16[48,3200]{1,0:T(8,128)(2,1)S(1)} collective-permute-done((bf16[48,3200]{1,0:T(8,128)(2,1)S(1)}, bf16[48,3200]{1,0:T(8,128)(2,1)S(1)}, u32[]{:S(2)}, u32[]{:S(2)}) %collective-permute-start.13) | collective-permute-done | bytes 307232 | tf_op jit(solution)/shard_map/ppermute | solution.py:657
  127.3 0.6 collective-permute-start.14
  127.9 1.5 collective-permute-done.14
  129.4 0.1 add.8
  129.5 18.5 %all_to_all.10.pieces = f32[64,16,128]{2,1,0:T(8,128)S(1)} all-to-all(f32[64,16,128]{2,1,0:T(8,128)S(1)} %bitcast.42), channel_id=1, replica_groups={{0,2,4,6,8,10,12,14,16,18,20,22,24,26,28,30,32,34,36,38,40,42,44,46,48,..., dimensions={0} | all-to-all | bytes 1048576 | tf_op jit(solution)/shard_map/all_to_all | solution.py:674
  148.0 0.9 shard_map.233
  148.9 4.9 %all-to-all-start.1 = ((f32[64,16,128]{2,1,0:T(8,128)}), f32[64,16,128]{2,1,0:T(8,128)S(1)}, u32[]{:S(2)}, u32[]{:S(2)}) async-start(f32[64,16,128]{2,1,0:T(8,128)} %shard_map.233), calls=%async_computation.1 | async-start | bytes 1048576 | tf_op jit(solution)/shard_map/all_to_all | solution.py:676
  153.8 3.4 %collective-permute-start.15 = (bf16[48,3200]{1,0:T(8,128)(2,1)S(1)}, bf16[48,3200]{1,0:T(8,128)(2,1)S(1)}, u32[]{:S(2)}, u32[]{:S(2)}) collective-permute-start(bf16[48,3200]{1,0:T(8,128)(2,1)S(1)} %get-tuple-element.116), channel_id=1, source_target_pairs={{0,1},{1,2},{2,3},{3,4},{4,5},{5,6},{6,7},{7,8},{8,9},{9,10},{10,1... | collective-permute-start | bytes 921608 | tf_op jit(solution)/shard_map/ppermute | solution.py:662
  157.2 8.0 %collective-permute-done.15.left = bf16[48,3200]{1,0:T(8,128)(2,1)S(1)} collective-permute-done((bf16[48,3200]{1,0:T(8,128)(2,1)S(1)}, bf16[48,3200]{1,0:T(8,128)(2,1)S(1)}, u32[]{:S(2)}, u32[]{:S(2)}) %collective-permute-start.15) | collective-permute-done | bytes 307232 | tf_op jit(solution)/shard_map/ppermute | solution.py:662
  165.2 2.4 %collective-permute-done.16.right = bf16[48,3200]{1,0:T(8,128)(2,1)S(1)} collective-permute-done((bf16[48,3200]{1,0:T(8,128)(2,1)S(1)}, bf16[48,3200]{1,0:T(8,128)(2,1)S(1)}, u32[]{:S(2)}, u32[]{:S(2)}) %collective-permute-start.16) | collective-permute-done | bytes 307232 | tf_op jit(solution)/shard_map/ppermute | solution.py:663
  167.6 1.5 shard_map.235
  169.1 2.0 %collective-permute-start.17 = (f32[1024,128]{1,0:T(8,128)S(1)}, f32[1024,128]{1,0:T(8,128)S(1)}, u32[]{:S(2)}, u32[]{:S(2)}) collective-permute-start(f32[1024,128]{1,0:T(8,128)S(1)} %bitcast.27), channel_id=1, source_target_pairs={{0,1},{1,0},{2,3},{3,2},{4,5},{5,4},{6,7},{7,6},{8,9},{9,8},{10,11... | collective-permute-start | bytes 1572872 | tf_op jit(solution)/shard_map/ppermute | solution.py:678
  171.1 1.5 collective-permute-done.17.other
  172.6 1.0 shard_map.236
  (71 shorter events, 0.3 us)
Async XLA Ops:
  0.6 25.0 %copy-start.8 = (f32[20,64]{1,0:T(8,128)S(1)}, f32[20,64]{1,0:T(8,128)}, u32[]{:S(2)}) copy-start(f32[20,64]{1,0:T(8,128)} %first.1) | copy-start | bytes 15364
  0.7 25.0 %copy-start.12 = (s32[1,1,512]{2,1,0:T(1,128)S(1)}, s32[1,1,512]{2,1,0:T(1,128)}, u32[]{:S(2)}) copy-start(s32[1,1,512]{2,1,0:T(1,128)} %param.22) | copy-start | bytes 6148
  1.4 1.1 copy-start
  2.5 23.1 %copy-start.38 = (f32[1,1,3,512]{3,1,2,0:T(1,128)S(1)}, f32[1,1,3,512]{3,1,2,0:T(1,128)}, u32[]{:S(2)}) copy-start(f32[1,1,3,512]{3,1,2,0:T(1,128)} %param.21) | copy-start | bytes 18436
  2.5 23.1 %copy-start.37 = (f32[1,1,3,1024]{3,1,2,0:T(1,128)S(1)}, f32[1,1,3,1024]{3,1,2,0:T(1,128)}, u32[]{:S(2)}) copy-start(f32[1,1,3,1024]{3,1,2,0:T(1,128)} %param.18) | copy-start | bytes 36868
  2.5 23.1 %copy-start.1 = (f32[64,1280]{1,0:T(8,128)S(1)}, f32[64,1280]{1,0:T(8,128)}, u32[]{:S(2)}) copy-start(f32[64,1280]{1,0:T(8,128)} %second.1) | copy-start | bytes 983044
  2.5 23.1 %copy-start.5 = (f32[64,640]{1,0:T(8,128)S(1)}, f32[64,640]{1,0:T(8,128)}, u32[]{:S(2)}) copy-start(f32[64,640]{1,0:T(8,128)} %psecond.1) | copy-start | bytes 491524
  2.5 23.1 %copy-start.6 = (f32[1,1,32768]{2,1,0:T(1,128)S(1)}, f32[1,1,32768]{2,1,0:T(1,128)}, u32[]{:S(2)}) copy-start(f32[1,1,32768]{2,1,0:T(1,128)} %param.23) | copy-start | bytes 393220
  2.5 23.1 %copy-start.9 = (f32[20,64]{1,0:T(8,128)S(1)}, f32[20,64]{1,0:T(8,128)}, u32[]{:S(2)}) copy-start(f32[20,64]{1,0:T(8,128)} %pfirst.1) | copy-start | bytes 15364
  2.5 23.1 %copy-start.10 = (s32[1,1,1024]{2,1,0:T(1,128)S(1)}, s32[1,1,1024]{2,1,0:T(1,128)}, u32[]{:S(2)}) copy-start(s32[1,1,1024]{2,1,0:T(1,128)} %param.20) | copy-start | bytes 12292
  2.6 23.1 %copy-start.11 = (s32[1,1,1024]{2,1,0:T(1,128)S(1)}, s32[1,1,1024]{2,1,0:T(1,128)}, u32[]{:S(2)}) copy-start(s32[1,1,1024]{2,1,0:T(1,128)} %param.19) | copy-start | bytes 12292
  2.6 23.1 %copy-start.13 = (s32[1,1,128]{2,1,0:T(1,128)S(1)}, s32[1,1,128]{2,1,0:T(1,128)}, u32[]{:S(2)}) copy-start(s32[1,1,128]{2,1,0:T(1,128)} %param.24) | copy-start | bytes 1540
  3.1 16.3 %collective-permute-start = (bf16[48,3200]{1,0:T(8,128)(2,1)S(1)}, bf16[48,3200]{1,0:T(8,128)(2,1)S(1)}, u32[]{:S(2)}, u32[]{:S(2)}) collective-permute-start(bf16[48,3200]{1,0:T(8,128)(2,1)S(1)} %get-tuple-element.69), channel_id=1, source_target_pairs={{0,16},{16,32},{32,48},{48,64},{64,80},{80,96},{96,112},{112,0},{1... | collective-permute-start | bytes 921608 | tf_op jit(solution)/shard_map/ppermute | solution.py:656
  6.9 16.5 %collective-permute-start.1 = (bf16[48,3200]{1,0:T(8,128)(2,1)S(1)}, bf16[48,3200]{1,0:T(8,128)(2,1)S(1)}, u32[]{:S(2)}, u32[]{:S(2)}) collective-permute-start(bf16[48,3200]{1,0:T(8,128)(2,1)S(1)} %get-tuple-element.70), channel_id=1, source_target_pairs={{16,0},{32,16},{48,32},{64,48},{80,64},{96,80},{112,96},{0,112},{1... | collective-permute-start | bytes 921608 | tf_op jit(solution)/shard_map/ppermute | solution.py:657
  23.5 6.1 %collective-permute-start.2 = (bf16[48,3200]{1,0:T(8,128)(2,1)S(1)}, bf16[48,3200]{1,0:T(8,128)(2,1)S(1)}, u32[]{:S(2)}, u32[]{:S(2)}) collective-permute-start(bf16[48,3200]{1,0:T(8,128)(2,1)S(1)} %get-tuple-element.72), channel_id=1, source_target_pairs={{0,1},{1,2},{2,3},{3,4},{4,5},{5,6},{6,7},{7,8},{8,9},{9,10},{10,1... | collective-permute-start | bytes 921608 | tf_op jit(solution)/shard_map/ppermute | solution.py:662
  25.6 6.6 %collective-permute-start.3 = (bf16[48,3200]{1,0:T(8,128)(2,1)S(1)}, bf16[48,3200]{1,0:T(8,128)(2,1)S(1)}, u32[]{:S(2)}, u32[]{:S(2)}) collective-permute-start(bf16[48,3200]{1,0:T(8,128)(2,1)S(1)} %get-tuple-element.73), channel_id=1, source_target_pairs={{1,0},{2,1},{3,2},{4,3},{5,4},{6,5},{7,6},{8,7},{9,8},{10,9},{11,1... | collective-permute-start | bytes 921608 | tf_op jit(solution)/shard_map/ppermute | solution.py:663
  25.7 6.5 %copy-start.2 = (f32[5,128,128]{2,1,0:T(8,128)S(1)}, f32[5,128,128]{2,1,0:T(8,128)}, u32[]{:S(2)}) copy-start(f32[5,128,128]{2,1,0:T(8,128)} %mixing.3) | copy-start | bytes 983044
  27.4 0.8 copy-start.19
  28.3 0.7 copy-start.25
  29.0 0.6 copy-start.33
  29.6 9.1 %copy-start.17 = (f32[1024,128]{1,0:T(8,128)}, f32[1024,128]{1,0:T(8,128)S(1)}, u32[]{:S(2)}) copy-start(f32[1024,128]{1,0:T(8,128)S(1)} %get-tuple-element.74.columns) | copy-start | bytes 1572868
  29.6 9.1 %copy-start.21 = (bf16[1024,192]{1,0:T(8,128)(2,1)}, bf16[1024,192]{1,0:T(8,128)(2,1)S(1)}, u32[]{:S(2)}) copy-start(bf16[1024,192]{1,0:T(8,128)(2,1)S(1)} %get-tuple-element.75.hidden3) | copy-start | bytes 1179652
  29.6 9.1 %copy-start.23 = (bf16[192,1280]{1,0:T(8,128)(2,1)}, bf16[192,1280]{1,0:T(8,128)(2,1)S(1)}, u32[]{:S(2)}) copy-start(bf16[192,1280]{1,0:T(8,128)(2,1)S(1)} %get-tuple-element.76.second3) | copy-start | bytes 1474564
  29.6 35.1 %copy-start.15 = (bf16[192,640]{1,0:T(8,128)(2,1)}, bf16[192,640]{1,0:T(8,128)(2,1)S(1)}, u32[]{:S(2)}) copy-start(bf16[192,640]{1,0:T(8,128)(2,1)S(1)} %get-tuple-element.86.second3) | copy-start | bytes 737284
  32.2 32.5 %copy-start.7 = (f32[128,128]{1,0:T(8,128)S(1)}, f32[128,128]{1,0:T(8,128)}, u32[]{:S(2)}) copy-start(f32[128,128]{1,0:T(8,128)} %first_readout.1) | copy-start | bytes 196612
  32.2 32.5 %copy-start.14 = (f32[128]{0:T(128)S(1)}, f32[128]{0:T(128)}, u32[]{:S(2)}) copy-start(f32[128]{0:T(128)} %param.31) | copy-start | bytes 1540
  38.8 0.9 copy-start.35
  39.7 31.9 %copy-start.27 = (bf16[256,3200]{1,0:T(8,128)(2,1)}, bf16[256,3200]{1,0:T(8,128)(2,1)S(1)}, u32[]{:S(2)}) copy-start(bf16[256,3200]{1,0:T(8,128)(2,1)S(1)} %get-tuple-element.98.table) | copy-start | bytes 4915204
  39.7 31.9 %copy-start.29 = (f32[3200,128]{1,0:T(8,128)}, f32[3200,128]{1,0:T(8,128)S(1)}, u32[]{:S(2)}) copy-start(f32[3200,128]{1,0:T(8,128)S(1)} %get-tuple-element.94.mixed) | copy-start | bytes 4915204
  39.7 13.5 %collective-permute-start.4 = (bf16[48,3200]{1,0:T(8,128)(2,1)S(1)}, bf16[48,3200]{1,0:T(8,128)(2,1)S(1)}, u32[]{:S(2)}, u32[]{:S(2)}) collective-permute-start(bf16[48,3200]{1,0:T(8,128)(2,1)S(1)} %get-tuple-element.79), channel_id=1, source_target_pairs={{0,16},{16,32},{32,48},{48,64},{64,80},{80,96},{96,112},{112,0},{1... | collective-permute-start | bytes 921608 | tf_op jit(solution)/shard_map/ppermute | solution.py:656
  40.4 16.2 %collective-permute-start.5 = (bf16[48,3200]{1,0:T(8,128)(2,1)S(1)}, bf16[48,3200]{1,0:T(8,128)(2,1)S(1)}, u32[]{:S(2)}, u32[]{:S(2)}) collective-permute-start(bf16[48,3200]{1,0:T(8,128)(2,1)S(1)} %get-tuple-element.80), channel_id=1, source_target_pairs={{16,0},{32,16},{48,32},{64,48},{80,64},{96,80},{112,96},{0,112},{1... | collective-permute-start | bytes 921608 | tf_op jit(solution)/shard_map/ppermute | solution.py:657
  56.6 5.3 %collective-permute-start.6 = (bf16[48,3200]{1,0:T(8,128)(2,1)S(1)}, bf16[48,3200]{1,0:T(8,128)(2,1)S(1)}, u32[]{:S(2)}, u32[]{:S(2)}) collective-permute-start(bf16[48,3200]{1,0:T(8,128)(2,1)S(1)} %get-tuple-element.82), channel_id=1, source_target_pairs={{0,1},{1,2},{2,3},{3,4},{4,5},{5,6},{6,7},{7,8},{8,9},{9,10},{10,1... | collective-permute-start | bytes 921608 | tf_op jit(solution)/shard_map/ppermute | solution.py:662
  58.1 6.6 %collective-permute-start.7 = (bf16[48,3200]{1,0:T(8,128)(2,1)S(1)}, bf16[48,3200]{1,0:T(8,128)(2,1)S(1)}, u32[]{:S(2)}, u32[]{:S(2)}) collective-permute-start(bf16[48,3200]{1,0:T(8,128)(2,1)S(1)} %get-tuple-element.83), channel_id=1, source_target_pairs={{1,0},{2,1},{3,2},{4,3},{5,4},{6,5},{7,6},{8,7},{9,8},{10,9},{11,1... | collective-permute-start | bytes 921608 | tf_op jit(solution)/shard_map/ppermute | solution.py:663
  71.6 1.2 copy-start.31
  72.8 10.5 %collective-permute-start.8 = (bf16[48,3200]{1,0:T(8,128)(2,1)S(1)}, bf16[48,3200]{1,0:T(8,128)(2,1)S(1)}, u32[]{:S(2)}, u32[]{:S(2)}) collective-permute-start(bf16[48,3200]{1,0:T(8,128)(2,1)S(1)} %get-tuple-element.89), channel_id=1, source_target_pairs={{0,16},{16,32},{32,48},{48,64},{64,80},{80,96},{96,112},{112,0},{1... | collective-permute-start | bytes 921608 | tf_op jit(solution)/shard_map/ppermute | solution.py:656
  72.8 15.4 %collective-permute-start.9 = (bf16[48,3200]{1,0:T(8,128)(2,1)S(1)}, bf16[48,3200]{1,0:T(8,128)(2,1)S(1)}, u32[]{:S(2)}, u32[]{:S(2)}) collective-permute-start(bf16[48,3200]{1,0:T(8,128)(2,1)S(1)} %get-tuple-element.90), channel_id=1, source_target_pairs={{16,0},{32,16},{48,32},{64,48},{80,64},{96,80},{112,96},{0,112},{1... | collective-permute-start | bytes 921608 | tf_op jit(solution)/shard_map/ppermute | solution.py:657
  88.2 5.4 %collective-permute-start.10 = (bf16[48,3200]{1,0:T(8,128)(2,1)S(1)}, bf16[48,3200]{1,0:T(8,128)(2,1)S(1)}, u32[]{:S(2)}, u32[]{:S(2)}) collective-permute-start(bf16[48,3200]{1,0:T(8,128)(2,1)S(1)} %get-tuple-element.92), channel_id=1, source_target_pairs={{0,1},{1,2},{2,3},{3,4},{4,5},{5,6},{6,7},{7,8},{8,9},{9,10},{10,1... | collective-permute-start | bytes 921608 | tf_op jit(solution)/shard_map/ppermute | solution.py:662
  89.8 6.6 %collective-permute-start.11 = (bf16[48,3200]{1,0:T(8,128)(2,1)S(1)}, bf16[48,3200]{1,0:T(8,128)(2,1)S(1)}, u32[]{:S(2)}, u32[]{:S(2)}) collective-permute-start(bf16[48,3200]{1,0:T(8,128)(2,1)S(1)} %get-tuple-element.93), channel_id=1, source_target_pairs={{1,0},{2,1},{3,2},{4,3},{5,4},{6,5},{7,6},{8,7},{9,8},{10,9},{11,1... | collective-permute-start | bytes 921608 | tf_op jit(solution)/shard_map/ppermute | solution.py:663
  90.9 0.9 copy-start.16
  91.8 5.3 %copy-start.18 = (f32[1024,128]{1,0:T(8,128)S(1)}, f32[1024,128]{1,0:T(8,128)}, u32[]{:S(2)}) copy-start(f32[1024,128]{1,0:T(8,128)} %copy-done.17) | copy-start | bytes 1572868
  91.8 5.3 %copy-start.22 = (bf16[1024,192]{1,0:T(8,128)(2,1)S(1)}, bf16[1024,192]{1,0:T(8,128)(2,1)}, u32[]{:S(2)}) copy-start(bf16[1024,192]{1,0:T(8,128)(2,1)} %copy-done.21) | copy-start | bytes 1179652
  91.8 5.3 %copy-start.24 = (bf16[192,1280]{1,0:T(8,128)(2,1)S(1)}, bf16[192,1280]{1,0:T(8,128)(2,1)}, u32[]{:S(2)}) copy-start(bf16[192,1280]{1,0:T(8,128)(2,1)} %copy-done.23) | copy-start | bytes 1474564
  91.8 5.3 %copy-start.30 = (f32[3200,128]{1,0:T(8,128)S(1)}, f32[3200,128]{1,0:T(8,128)}, u32[]{:S(2)}) copy-start(f32[3200,128]{1,0:T(8,128)} %copy-done.29) | copy-start | bytes 4915204
  96.4 0.7 copy-start.3
  97.1 1.0 copy-start.4
  98.1 1.4 copy-start.32
  99.5 13.7 %copy-start.20 = (f32[1024,64]{1,0:T(8,128)S(1)}, f32[1024,64]{1,0:T(8,128)}, u32[]{:S(2)}) copy-start(f32[1024,64]{1,0:T(8,128)} %copy-done.19) | copy-start | bytes 786436
  99.5 13.7 %copy-start.26 = (bf16[128,1024]{1,0:T(8,128)(2,1)S(1)}, bf16[128,1024]{1,0:T(8,128)(2,1)}, u32[]{:S(2)}) copy-start(bf16[128,1024]{1,0:T(8,128)(2,1)} %copy-done.25) | copy-start | bytes 786436
  99.5 13.7 %copy-start.28 = (bf16[256,3200]{1,0:T(8,128)(2,1)S(1)}, bf16[256,3200]{1,0:T(8,128)(2,1)}, u32[]{:S(2)}) copy-start(bf16[256,3200]{1,0:T(8,128)(2,1)} %copy-done.27) | copy-start | bytes 4915204
  99.5 13.7 %copy-start.34 = (f32[24,1024]{1,0:T(8,128)S(1)}, f32[24,1024]{1,0:T(8,128)}, u32[]{:S(2)}) copy-start(f32[24,1024]{1,0:T(8,128)} %copy-done.33) | copy-start | bytes 294916
  99.5 13.7 %copy-start.36 = (bf16[3200,128]{1,0:T(8,128)(2,1)S(1)}, bf16[3200,128]{1,0:T(8,128)(2,1)}, u32[]{:S(2)}) copy-start(bf16[3200,128]{1,0:T(8,128)(2,1)} %copy-done.35) | copy-start | bytes 2457604
  108.1 12.8 %collective-permute-start.12 = (bf16[48,3200]{1,0:T(8,128)(2,1)S(1)}, bf16[48,3200]{1,0:T(8,128)(2,1)S(1)}, u32[]{:S(2)}, u32[]{:S(2)}) collective-permute-start(bf16[48,3200]{1,0:T(8,128)(2,1)S(1)} %get-tuple-element.110), channel_id=1, source_target_pairs={{0,16},{16,32},{32,48},{48,64},{64,80},{80,96},{96,112},{112,0},{1... | collective-permute-start | bytes 921608 | tf_op jit(solution)/shard_map/ppermute | solution.py:656
  108.1 19.1 %collective-permute-start.13 = (bf16[48,3200]{1,0:T(8,128)(2,1)S(1)}, bf16[48,3200]{1,0:T(8,128)(2,1)S(1)}, u32[]{:S(2)}, u32[]{:S(2)}) collective-permute-start(bf16[48,3200]{1,0:T(8,128)(2,1)S(1)} %get-tuple-element.111), channel_id=1, source_target_pairs={{16,0},{32,16},{48,32},{64,48},{80,64},{96,80},{112,96},{0,112},{1... | collective-permute-start | bytes 921608 | tf_op jit(solution)/shard_map/ppermute | solution.py:657
  127.3 2.2 %collective-permute-start.14 = (f32[1024,128]{1,0:T(8,128)S(1)}, f32[1024,128]{1,0:T(8,128)S(1)}, u32[]{:S(2)}, u32[]{:S(2)}) collective-permute-start(f32[1024,128]{1,0:T(8,128)S(1)} %get-tuple-element.113), channel_id=1, source_target_pairs={{0,1},{1,0},{2,3},{3,2},{4,5},{5,4},{6,7},{7,6},{8,9},{9,8},{10,11... | collective-permute-start | bytes 1572872 | tf_op jit(solution)/shard_map/ppermute | solution.py:673
  148.9 20.2 %all-to-all-start.1 = ((f32[64,16,128]{2,1,0:T(8,128)}), f32[64,16,128]{2,1,0:T(8,128)S(1)}, u32[]{:S(2)}, u32[]{:S(2)}) async-start(f32[64,16,128]{2,1,0:T(8,128)} %shard_map.233), calls=%async_computation.1 | async-start | bytes 1048576 | tf_op jit(solution)/shard_map/all_to_all | solution.py:676
  153.8 11.4 %collective-permute-start.15 = (bf16[48,3200]{1,0:T(8,128)(2,1)S(1)}, bf16[48,3200]{1,0:T(8,128)(2,1)S(1)}, u32[]{:S(2)}, u32[]{:S(2)}) collective-permute-start(bf16[48,3200]{1,0:T(8,128)(2,1)S(1)} %get-tuple-element.116), channel_id=1, source_target_pairs={{0,1},{1,2},{2,3},{3,4},{4,5},{5,6},{6,7},{7,8},{8,9},{9,10},{10,1... | collective-permute-start | bytes 921608 | tf_op jit(solution)/shard_map/ppermute | solution.py:662
  157.1 10.4 %collective-permute-start.16 = (bf16[48,3200]{1,0:T(8,128)(2,1)S(1)}, bf16[48,3200]{1,0:T(8,128)(2,1)S(1)}, u32[]{:S(2)}, u32[]{:S(2)}) collective-permute-start(bf16[48,3200]{1,0:T(8,128)(2,1)S(1)} %get-tuple-element.117), channel_id=1, source_target_pairs={{1,0},{2,1},{3,2},{4,3},{5,4},{6,5},{7,6},{8,7},{9,8},{10,9},{11,1... | collective-permute-start | bytes 921608 | tf_op jit(solution)/shard_map/ppermute | solution.py:663
  169.1 3.5 %collective-permute-start.17 = (f32[1024,128]{1,0:T(8,128)S(1)}, f32[1024,128]{1,0:T(8,128)S(1)}, u32[]{:S(2)}, u32[]{:S(2)}) collective-permute-start(f32[1024,128]{1,0:T(8,128)S(1)} %bitcast.27), channel_id=1, source_target_pairs={{0,1},{1,0},{2,3},{3,2},{4,5},{5,4},{6,7},{7,6},{8,9},{9,8},{10,11... | collective-permute-start | bytes 1572872 | tf_op jit(solution)/shard_map/ppermute | solution.py:678

commit v2 on v1

--- a/solution.py
+++ b/solution.py
@@ -17,7 +17,7 @@
 PEDGES = 512
 PROBES = 128
 WIDE = COMP * C
-EB = 256
+EB = 512
 DEGREES = (1, 3, 5, 7, 9)
 STARTS = (0, 1, 4, 9, 16)
 HIGHEST = lax.Precision.HIGHEST
@@ -96,7 +96,7 @@
     ]
 
 
-def pack_kernel(features, send_index, own, low, middle, high, chosen_out, placed_out, lists):
+def pack_kernel(core, features, send_index, own, low, middle, high, chosen_out, placed_out, lists):
     lists[...] = jnp.zeros_like(lists)
     for at in range(8):
         i, j = divmod(at if at < 4 else at + 1, 3)
@@ -707,6 +707,7 @@
         [((ATOMS, WIDE), BF16)] + PACKETS + [((C, ATOMS), BF16), ((ATOMS, C), BF16)],
         [((C, C), F32)],
         2 * C * C * WIDE,
+        core,
         field,
         send_index[0, 0],
     )

time: 174 us -> 167 us (0.960)
  local copies, waits for them, and re-layouts: 10.2 us -> 1.93 us
  waiting for transfers between devices: 68.7 us -> 71.5 us
    unnamed x81 -> x33, local copies, waits for them, and re-layouts: 10.2 us -> 1.93 us
    ppermute x4, waiting for transfers between devices: 12.3 us -> 14.8 us  [exchange(): left = lax.ppermute(to_right, 'by', up)]
  transfers between devices with their start and end apart: 19 -> 19, of which waited for: 16 -> 17; matrix products, arithmetic and copies ran while one was open for 0% -> 0% of each run, Pallas kernels for 7% -> 7%
where the time goes in v2:
time: 167 us
  waiting for transfers between devices  71.5 us (43%)
  starting transfers between devices  39.1 us (23%)
  Pallas kernels  35 us (21%)
  blocking collectives  18.4 us (11%)
  local copies, waits for them, and re-layouts  1.93 us (1%)
    pallas_call x14, Pallas kernels, call(): pl.pallas_call(kernel, out_shape=shapes, in_specs=[scalar if x.shape == (...  35 us
    ppermute x4, waiting for transfers between devices, exchange(): low = lax.ppermute(high_packet, 'bx', up)  24.1 us
    ppermute x4, waiting for transfers between devices, exchange(): high = lax.ppermute(low_packet, 'bx', down)  18.8 us
    all_to_all x1, blocking collectives, reduce_halves(): lax.all_to_all(pair, axes, 0, 0, axis_index_groups=groups, tiled=True)  18.4 us
    ppermute x4, starting transfers between devices, exchange(): high = lax.ppermute(low_packet, 'bx', down)  16.8 us
    ppermute x4, waiting for transfers between devices, exchange(): left = lax.ppermute(to_right, 'by', up)  14.8 us
    ppermute x4, waiting for transfers between devices, exchange(): right = lax.ppermute(to_left, 'by', down)  10.7 us
    ppermute x4, starting transfers between devices, exchange(): left = lax.ppermute(to_right, 'by', up)  8.3 us
  transfers between devices with their start and end apart: 19, of which 17 were waited for; matrix products, arithmetic and copies ran while one was open for 0% of the time, Pallas kernels for 7%

profile of v2, /device:TPU:1, one launch (start us, length us, event | category | flops | bytes accessed | tf_op | source)
XLA Modules:
  0.0 166.9 jit_solution(3708166120972558543)
XLA Ops:
  0.6 0.0 copy-start.14
  0.7 0.0 copy-start.7
  0.7 0.0 copy-start.6
  0.7 0.0 copy-start.11
  0.7 0.0 copy-start.10
  0.7 0.0 copy-start.8
  0.7 0.0 copy-start.9
  0.7 0.7 copy.33
  1.4 1.1 copy-done
  2.6 0.5 shard_map.223
  3.1 3.8 %collective-permute-start = (bf16[48,3200]{1,0:T(8,128)(2,1)S(1)}, bf16[48,3200]{1,0:T(8,128)(2,1)S(1)}, u32[]{:S(2)}, u32[]{:S(2)}) collective-permute-start(bf16[48,3200]{1,0:T(8,128)(2,1)S(1)} %get-tuple-element.69), channel_id=1, source_target_pairs={{0,16},{16,32},{32,48},{48,64},{64,80},{80,96},{96,112},{112,0},{1... | collective-permute-start | bytes 921608 | tf_op jit(solution)/shard_map/ppermute | solution.py:656
  7.0 2.3 %collective-permute-start.1 = (bf16[48,3200]{1,0:T(8,128)(2,1)S(1)}, bf16[48,3200]{1,0:T(8,128)(2,1)S(1)}, u32[]{:S(2)}, u32[]{:S(2)}) collective-permute-start(bf16[48,3200]{1,0:T(8,128)(2,1)S(1)} %get-tuple-element.70), channel_id=1, source_target_pairs={{16,0},{32,16},{48,32},{64,48},{80,64},{96,80},{112,96},{0,112},{1... | collective-permute-start | bytes 921608 | tf_op jit(solution)/shard_map/ppermute | solution.py:657
  9.2 10.2 %collective-permute-done.low = bf16[48,3200]{1,0:T(8,128)(2,1)S(1)} collective-permute-done((bf16[48,3200]{1,0:T(8,128)(2,1)S(1)}, bf16[48,3200]{1,0:T(8,128)(2,1)S(1)}, u32[]{:S(2)}, u32[]{:S(2)}) %collective-permute-start) | collective-permute-done | bytes 307232 | tf_op jit(solution)/shard_map/ppermute | solution.py:656
  19.5 4.0 %collective-permute-done.1.high = bf16[48,3200]{1,0:T(8,128)(2,1)S(1)} collective-permute-done((bf16[48,3200]{1,0:T(8,128)(2,1)S(1)}, bf16[48,3200]{1,0:T(8,128)(2,1)S(1)}, u32[]{:S(2)}, u32[]{:S(2)}) %collective-permute-start.1) | collective-permute-done | bytes 307232 | tf_op jit(solution)/shard_map/ppermute | solution.py:657
  23.5 2.1 %collective-permute-start.2 = (bf16[48,3200]{1,0:T(8,128)(2,1)S(1)}, bf16[48,3200]{1,0:T(8,128)(2,1)S(1)}, u32[]{:S(2)}, u32[]{:S(2)}) collective-permute-start(bf16[48,3200]{1,0:T(8,128)(2,1)S(1)} %get-tuple-element.72), channel_id=1, source_target_pairs={{0,1},{1,2},{2,3},{3,4},{4,5},{5,6},{6,7},{7,8},{8,9},{9,10},{10,1... | collective-permute-start | bytes 921608 | tf_op jit(solution)/shard_map/ppermute | solution.py:662
  25.6 0.0 collective-permute-start.3
  25.6 0.0 copy-done.14
  25.6 0.0 copy-done.13
  25.7 0.0 copy-start.2
  25.7 1.7 %shard_map.225 = (f32[1024,128]{1,0:T(8,128)S(1)}, f32[24,1024]{1,0:T(8,128)S(1)}, f32[1024,64]{1,0:T(8,128)S(1)}, bf16[1024,192]{1,0:T(8,128)(2,1)S(1)}, bf16[1...) custom-call(f32[3,1024]{1,0:T(4,128)S(1)} %bitcast.31, ...), custom_call_target="tpu_custom_call" | custom-call | flops 1000000000 | bytes 3774976 | tf_op jit(solution)/shard_map/pallas_call | solution.py:624
  27.5 1.9 %collective-permute-done.2.left = bf16[48,3200]{1,0:T(8,128)(2,1)S(1)} collective-permute-done((bf16[48,3200]{1,0:T(8,128)(2,1)S(1)}, bf16[48,3200]{1,0:T(8,128)(2,1)S(1)}, u32[]{:S(2)}, u32[]{:S(2)}) %collective-permute-start.2) | collective-permute-done | bytes 307232 | tf_op jit(solution)/shard_map/ppermute | solution.py:662
  29.4 2.8 %collective-permute-done.3.right = bf16[48,3200]{1,0:T(8,128)(2,1)S(1)} collective-permute-done((bf16[48,3200]{1,0:T(8,128)(2,1)S(1)}, bf16[48,3200]{1,0:T(8,128)(2,1)S(1)}, u32[]{:S(2)}, u32[]{:S(2)}) %collective-permute-start.3) | collective-permute-done | bytes 307232 | tf_op jit(solution)/shard_map/ppermute | solution.py:663
  32.2 0.0 copy-done.2
  32.2 6.5 %shard_map.226 = (bf16[128,3200]{1,0:T(8,128)(2,1)S(1)}, bf16[3200,128]{1,0:T(8,128)(2,1)S(1)}, f32[3200,128]{1,0:T(8,128)S(1)}, bf16[256,3200]{1,0:T(8,128)(2,1...) custom-call(bf16[128,3200]{1,0:T(8,128)(2,1)S(1)} %get-tuple-element.68.own, ...), custom_call_target="tpu_custom_call" | custom-call | flops 4000000000 | bytes 9555968 | tf_op jit(solution)/shard_map/pallas_call | solution.py:624
  38.7 0.7 collective-permute-start.4
  39.4 4.4 %collective-permute-start.5 = (bf16[48,3200]{1,0:T(8,128)(2,1)S(1)}, bf16[48,3200]{1,0:T(8,128)(2,1)S(1)}, u32[]{:S(2)}, u32[]{:S(2)}) collective-permute-start(bf16[48,3200]{1,0:T(8,128)(2,1)S(1)} %get-tuple-element.80), channel_id=1, source_target_pairs={{16,0},{32,16},{48,32},{64,48},{80,64},{96,80},{112,96},{0,112},{1... | collective-permute-start | bytes 921608 | tf_op jit(solution)/shard_map/ppermute | solution.py:657
  43.8 8.4 %collective-permute-done.4.low = bf16[48,3200]{1,0:T(8,128)(2,1)S(1)} collective-permute-done((bf16[48,3200]{1,0:T(8,128)(2,1)S(1)}, bf16[48,3200]{1,0:T(8,128)(2,1)S(1)}, u32[]{:S(2)}, u32[]{:S(2)}) %collective-permute-start.4) | collective-permute-done | bytes 307232 | tf_op jit(solution)/shard_map/ppermute | solution.py:656
  52.3 3.4 %collective-permute-done.5.high = bf16[48,3200]{1,0:T(8,128)(2,1)S(1)} collective-permute-done((bf16[48,3200]{1,0:T(8,128)(2,1)S(1)}, bf16[48,3200]{1,0:T(8,128)(2,1)S(1)}, u32[]{:S(2)}, u32[]{:S(2)}) %collective-permute-start.5) | collective-permute-done | bytes 307232 | tf_op jit(solution)/shard_map/ppermute | solution.py:657
  55.7 1.5 collective-permute-start.6
  57.1 0.4 collective-permute-start.7
  57.6 3.4 %collective-permute-done.6.left = bf16[48,3200]{1,0:T(8,128)(2,1)S(1)} collective-permute-done((bf16[48,3200]{1,0:T(8,128)(2,1)S(1)}, bf16[48,3200]{1,0:T(8,128)(2,1)S(1)}, u32[]{:S(2)}, u32[]{:S(2)}) %collective-permute-start.6) | collective-permute-done | bytes 307232 | tf_op jit(solution)/shard_map/ppermute | solution.py:662
  61.0 2.8 %collective-permute-done.7.right = bf16[48,3200]{1,0:T(8,128)(2,1)S(1)} collective-permute-done((bf16[48,3200]{1,0:T(8,128)(2,1)S(1)}, bf16[48,3200]{1,0:T(8,128)(2,1)S(1)}, u32[]{:S(2)}, u32[]{:S(2)}) %collective-permute-start.7) | collective-permute-done | bytes 307232 | tf_op jit(solution)/shard_map/ppermute | solution.py:663
  63.7 0.0 copy-done.12
  63.7 5.2 %shard_map.228 = (f32[3200,128]{1,0:T(8,128)S(1)}, bf16[48,3200]{1,0:T(8,128)(2,1)S(1)}, bf16[32,3200]{1,0:T(8,128)(2,1)S(1)}, bf16[48,3200]{1,0:T(8,128)(2,1)S(...) custom-call(bf16[128,3200]{1,0:T(8,128)(2,1)S(1)} %get-tuple-element.78.own, ...), custom_call_target="tpu_custom_call" | custom-call | flops 4000000000 | bytes 6072832 | tf_op jit(solution)/shard_map/pallas_call | solution.py:624
  68.9 0.1 collective-permute-start.8
  69.0 5.1 %collective-permute-start.9 = (bf16[48,3200]{1,0:T(8,128)(2,1)S(1)}, bf16[48,3200]{1,0:T(8,128)(2,1)S(1)}, u32[]{:S(2)}, u32[]{:S(2)}) collective-permute-start(bf16[48,3200]{1,0:T(8,128)(2,1)S(1)} %get-tuple-element.90), channel_id=1, source_target_pairs={{16,0},{32,16},{48,32},{64,48},{80,64},{96,80},{112,96},{0,112},{1... | collective-permute-start | bytes 921608 | tf_op jit(solution)/shard_map/ppermute | solution.py:657
  74.1 5.4 %collective-permute-done.8.low = bf16[48,3200]{1,0:T(8,128)(2,1)S(1)} collective-permute-done((bf16[48,3200]{1,0:T(8,128)(2,1)S(1)}, bf16[48,3200]{1,0:T(8,128)(2,1)S(1)}, u32[]{:S(2)}, u32[]{:S(2)}) %collective-permute-start.8) | collective-permute-done | bytes 307232 | tf_op jit(solution)/shard_map/ppermute | solution.py:656
  79.5 5.0 %collective-permute-done.9.high = bf16[48,3200]{1,0:T(8,128)(2,1)S(1)} collective-permute-done((bf16[48,3200]{1,0:T(8,128)(2,1)S(1)}, bf16[48,3200]{1,0:T(8,128)(2,1)S(1)}, u32[]{:S(2)}, u32[]{:S(2)}) %collective-permute-start.9) | collective-permute-done | bytes 307232 | tf_op jit(solution)/shard_map/ppermute | solution.py:657
  84.5 1.4 collective-permute-start.10
  85.9 1.4 collective-permute-start.11
  87.4 0.8 shard_map.231.probe_grads
  88.2 1.5 collective-permute-done.10.left
  89.7 2.8 %collective-permute-done.11.right = bf16[48,3200]{1,0:T(8,128)(2,1)S(1)} collective-permute-done((bf16[48,3200]{1,0:T(8,128)(2,1)S(1)}, bf16[48,3200]{1,0:T(8,128)(2,1)S(1)}, u32[]{:S(2)}, u32[]{:S(2)}) %collective-permute-start.11) | collective-permute-done | bytes 307232 | tf_op jit(solution)/shard_map/ppermute | solution.py:663
  92.5 8.7 %shard_map.230 = (f32[3200,128]{1,0:T(8,128)S(1)}, bf16[128,3200]{1,0:T(8,128)(2,1)S(1)}, bf16[3200,128]{1,0:T(8,128)(2,1)S(1)}, bf16[48,3200]{1,0:T(8,128)(2,1)...) custom-call(f32[3200,128]{1,0:T(8,128)S(1)} %get-tuple-element.88.grad_own, ...), custom_call_target="tpu_custom_call" | custom-call | flops 6000000000 | bytes 10375168 | tf_op jit(solution)/shard_map/pallas_call | solution.py:624
  101.2 0.1 collective-permute-start.12
  101.3 5.1 %collective-permute-start.13 = (bf16[48,3200]{1,0:T(8,128)(2,1)S(1)}, bf16[48,3200]{1,0:T(8,128)(2,1)S(1)}, u32[]{:S(2)}, u32[]{:S(2)}) collective-permute-start(bf16[48,3200]{1,0:T(8,128)(2,1)S(1)} %get-tuple-element.111), channel_id=1, source_target_pairs={{16,0},{32,16},{48,32},{64,48},{80,64},{96,80},{112,96},{0,112},{1... | collective-permute-start | bytes 921608 | tf_op jit(solution)/shard_map/ppermute | solution.py:657
  106.4 7.9 %shard_map.232 = (f32[1024,128]{1,0:T(8,128)S(1)}, f32[1024,128]{1,0:T(8,128)S(1)}) custom-call(s32[1]{0:T(128)} %bitcast.core, bf16[128,3200]{1,0:T(8,128)(2,1)S(1)} %get-tuple-element.96.d_gathered, bf16[3200,128]{1,0:T(8,128)(2,1)S(1)} %get-tuple-element.97.d_mixed, bf16[256,3200]{1,0:T(8,128)(2,1)S(1)} %get-tuple-element.98.table, ...), custom_call_target="tpu_custom_call" | custom-call | flops 6000000000 | bytes 7045124 | tf_op jit(solution)/shard_map/pallas_call | solution.py:624
  114.3 0.0 collective-permute-done.12.low
  114.3 6.4 %collective-permute-done.13.high = bf16[48,3200]{1,0:T(8,128)(2,1)S(1)} collective-permute-done((bf16[48,3200]{1,0:T(8,128)(2,1)S(1)}, bf16[48,3200]{1,0:T(8,128)(2,1)S(1)}, u32[]{:S(2)}, u32[]{:S(2)}) %collective-permute-start.13) | collective-permute-done | bytes 307232 | tf_op jit(solution)/shard_map/ppermute | solution.py:657
  120.7 0.5 collective-permute-start.14
  121.2 1.5 collective-permute-done.14
  122.7 0.1 add.8
  122.8 18.4 %all_to_all.10.pieces = f32[64,16,128]{2,1,0:T(8,128)S(1)} all-to-all(f32[64,16,128]{2,1,0:T(8,128)S(1)} %bitcast.42), channel_id=1, replica_groups={{0,2,4,6,8,10,12,14,16,18,20,22,24,26,28,30,32,34,36,38,40,42,44,46,48,..., dimensions={0} | all-to-all | bytes 1048576 | tf_op jit(solution)/shard_map/all_to_all | solution.py:674
  141.2 0.9 shard_map.233
  142.1 4.9 %all-to-all-start.1 = ((f32[64,16,128]{2,1,0:T(8,128)}), f32[64,16,128]{2,1,0:T(8,128)S(1)}, u32[]{:S(2)}, u32[]{:S(2)}) async-start(f32[64,16,128]{2,1,0:T(8,128)} %shard_map.233), calls=%async_computation.1 | async-start | bytes 1048576 | tf_op jit(solution)/shard_map/all_to_all | solution.py:676
  147.1 3.4 %collective-permute-start.15 = (bf16[48,3200]{1,0:T(8,128)(2,1)S(1)}, bf16[48,3200]{1,0:T(8,128)(2,1)S(1)}, u32[]{:S(2)}, u32[]{:S(2)}) collective-permute-start(bf16[48,3200]{1,0:T(8,128)(2,1)S(1)} %get-tuple-element.116), channel_id=1, source_target_pairs={{0,1},{1,2},{2,3},{3,4},{4,5},{5,6},{6,7},{7,8},{8,9},{9,10},{10,1... | collective-permute-start | bytes 921608 | tf_op jit(solution)/shard_map/ppermute | solution.py:662
  150.4 0.0 collective-permute-start.16
  150.4 8.0 %collective-permute-done.15.left = bf16[48,3200]{1,0:T(8,128)(2,1)S(1)} collective-permute-done((bf16[48,3200]{1,0:T(8,128)(2,1)S(1)}, bf16[48,3200]{1,0:T(8,128)(2,1)S(1)}, u32[]{:S(2)}, u32[]{:S(2)}) %collective-permute-start.15) | collective-permute-done | bytes 307232 | tf_op jit(solution)/shard_map/ppermute | solution.py:662
  158.4 2.4 %collective-permute-done.16.right = bf16[48,3200]{1,0:T(8,128)(2,1)S(1)} collective-permute-done((bf16[48,3200]{1,0:T(8,128)(2,1)S(1)}, bf16[48,3200]{1,0:T(8,128)(2,1)S(1)}, u32[]{:S(2)}, u32[]{:S(2)}) %collective-permute-start.16) | collective-permute-done | bytes 307232 | tf_op jit(solution)/shard_map/ppermute | solution.py:663
  160.8 1.5 shard_map.235
  162.4 0.0 all-to-all-done.1
  162.4 2.0 %collective-permute-start.17 = (f32[1024,128]{1,0:T(8,128)S(1)}, f32[1024,128]{1,0:T(8,128)S(1)}, u32[]{:S(2)}, u32[]{:S(2)}) collective-permute-start(f32[1024,128]{1,0:T(8,128)S(1)} %bitcast.27), channel_id=1, source_target_pairs={{0,1},{1,0},{2,3},{3,2},{4,5},{5,4},{6,7},{7,6},{8,9},{9,8},{10,11... | collective-permute-start | bytes 1572872 | tf_op jit(solution)/shard_map/ppermute | solution.py:678
  164.4 1.5 collective-permute-done.17.other
  165.9 1.0 shard_map.236
  (23 shorter events, 0.2 us)
Async XLA Ops:
  0.6 25.0 %copy-start.14 = (f32[1,1,3,512]{3,1,2,0:T(1,128)S(1)}, f32[1,1,3,512]{3,1,2,0:T(1,128)}, u32[]{:S(2)}) copy-start(f32[1,1,3,512]{3,1,2,0:T(1,128)} %param.21) | copy-start | bytes 18436
  0.7 25.0 %copy-start.7 = (f32[20,64]{1,0:T(8,128)S(1)}, f32[20,64]{1,0:T(8,128)}, u32[]{:S(2)}) copy-start(f32[20,64]{1,0:T(8,128)} %pfirst.1) | copy-start | bytes 15364
  0.7 25.0 %copy-start.6 = (f32[20,64]{1,0:T(8,128)S(1)}, f32[20,64]{1,0:T(8,128)}, u32[]{:S(2)}) copy-start(f32[20,64]{1,0:T(8,128)} %first.1) | copy-start | bytes 15364
  0.7 25.0 %copy-start.11 = (s32[1,1,128]{2,1,0:T(1,128)S(1)}, s32[1,1,128]{2,1,0:T(1,128)}, u32[]{:S(2)}) copy-start(s32[1,1,128]{2,1,0:T(1,128)} %param.24) | copy-start | bytes 1540
  0.7 25.0 %copy-start.10 = (s32[1,1,512]{2,1,0:T(1,128)S(1)}, s32[1,1,512]{2,1,0:T(1,128)}, u32[]{:S(2)}) copy-start(s32[1,1,512]{2,1,0:T(1,128)} %param.22) | copy-start | bytes 6148
  0.7 25.0 %copy-start.8 = (s32[1,1,1024]{2,1,0:T(1,128)S(1)}, s32[1,1,1024]{2,1,0:T(1,128)}, u32[]{:S(2)}) copy-start(s32[1,1,1024]{2,1,0:T(1,128)} %param.20) | copy-start | bytes 12292
  0.7 25.0 %copy-start.9 = (s32[1,1,1024]{2,1,0:T(1,128)S(1)}, s32[1,1,1024]{2,1,0:T(1,128)}, u32[]{:S(2)}) copy-start(s32[1,1,1024]{2,1,0:T(1,128)} %param.19) | copy-start | bytes 12292
  1.4 1.1 copy-start
  2.6 23.0 %copy-start.13 = (f32[1,1,3,1024]{3,1,2,0:T(1,128)S(1)}, f32[1,1,3,1024]{3,1,2,0:T(1,128)}, u32[]{:S(2)}) copy-start(f32[1,1,3,1024]{3,1,2,0:T(1,128)} %param.18) | copy-start | bytes 36868
  2.6 23.1 %copy-start.1 = (f32[64,1280]{1,0:T(8,128)S(1)}, f32[64,1280]{1,0:T(8,128)}, u32[]{:S(2)}) copy-start(f32[64,1280]{1,0:T(8,128)} %second.1) | copy-start | bytes 983044
  2.6 23.1 %copy-start.3 = (f32[64,640]{1,0:T(8,128)S(1)}, f32[64,640]{1,0:T(8,128)}, u32[]{:S(2)}) copy-start(f32[64,640]{1,0:T(8,128)} %psecond.1) | copy-start | bytes 491524
  2.6 23.1 %copy-start.4 = (f32[1,1,32768]{2,1,0:T(1,128)S(1)}, f32[1,1,32768]{2,1,0:T(1,128)}, u32[]{:S(2)}) copy-start(f32[1,1,32768]{2,1,0:T(1,128)} %param.23) | copy-start | bytes 393220
  3.1 16.3 %collective-permute-start = (bf16[48,3200]{1,0:T(8,128)(2,1)S(1)}, bf16[48,3200]{1,0:T(8,128)(2,1)S(1)}, u32[]{:S(2)}, u32[]{:S(2)}) collective-permute-start(bf16[48,3200]{1,0:T(8,128)(2,1)S(1)} %get-tuple-element.69), channel_id=1, source_target_pairs={{0,16},{16,32},{32,48},{48,64},{64,80},{80,96},{96,112},{112,0},{1... | collective-permute-start | bytes 921608 | tf_op jit(solution)/shard_map/ppermute | solution.py:656
  7.0 16.5 %collective-permute-start.1 = (bf16[48,3200]{1,0:T(8,128)(2,1)S(1)}, bf16[48,3200]{1,0:T(8,128)(2,1)S(1)}, u32[]{:S(2)}, u32[]{:S(2)}) collective-permute-start(bf16[48,3200]{1,0:T(8,128)(2,1)S(1)} %get-tuple-element.70), channel_id=1, source_target_pairs={{16,0},{32,16},{48,32},{64,48},{80,64},{96,80},{112,96},{0,112},{1... | collective-permute-start | bytes 921608 | tf_op jit(solution)/shard_map/ppermute | solution.py:657
  23.5 5.9 %collective-permute-start.2 = (bf16[48,3200]{1,0:T(8,128)(2,1)S(1)}, bf16[48,3200]{1,0:T(8,128)(2,1)S(1)}, u32[]{:S(2)}, u32[]{:S(2)}) collective-permute-start(bf16[48,3200]{1,0:T(8,128)(2,1)S(1)} %get-tuple-element.72), channel_id=1, source_target_pairs={{0,1},{1,2},{2,3},{3,4},{4,5},{5,6},{6,7},{7,8},{8,9},{9,10},{10,1... | collective-permute-start | bytes 921608 | tf_op jit(solution)/shard_map/ppermute | solution.py:662
  25.6 6.6 %collective-permute-start.3 = (bf16[48,3200]{1,0:T(8,128)(2,1)S(1)}, bf16[48,3200]{1,0:T(8,128)(2,1)S(1)}, u32[]{:S(2)}, u32[]{:S(2)}) collective-permute-start(bf16[48,3200]{1,0:T(8,128)(2,1)S(1)} %get-tuple-element.73), channel_id=1, source_target_pairs={{1,0},{2,1},{3,2},{4,3},{5,4},{6,5},{7,6},{8,7},{9,8},{10,9},{11,1... | collective-permute-start | bytes 921608 | tf_op jit(solution)/shard_map/ppermute | solution.py:663
  25.7 6.5 %copy-start.2 = (f32[5,128,128]{2,1,0:T(8,128)S(1)}, f32[5,128,128]{2,1,0:T(8,128)}, u32[]{:S(2)}) copy-start(f32[5,128,128]{2,1,0:T(8,128)} %mixing.3) | copy-start | bytes 983044
  32.2 31.6 %copy-start.5 = (f32[128,128]{1,0:T(8,128)S(1)}, f32[128,128]{1,0:T(8,128)}, u32[]{:S(2)}) copy-start(f32[128,128]{1,0:T(8,128)} %first_readout.1) | copy-start | bytes 196612
  32.2 31.6 %copy-start.12 = (f32[128]{0:T(128)S(1)}, f32[128]{0:T(128)}, u32[]{:S(2)}) copy-start(f32[128]{0:T(128)} %param.31) | copy-start | bytes 1540
  38.7 13.6 %collective-permute-start.4 = (bf16[48,3200]{1,0:T(8,128)(2,1)S(1)}, bf16[48,3200]{1,0:T(8,128)(2,1)S(1)}, u32[]{:S(2)}, u32[]{:S(2)}) collective-permute-start(bf16[48,3200]{1,0:T(8,128)(2,1)S(1)} %get-tuple-element.79), channel_id=1, source_target_pairs={{0,16},{16,32},{32,48},{48,64},{64,80},{80,96},{96,112},{112,0},{1... | collective-permute-start | bytes 921608 | tf_op jit(solution)/shard_map/ppermute | solution.py:656
  39.4 16.2 %collective-permute-start.5 = (bf16[48,3200]{1,0:T(8,128)(2,1)S(1)}, bf16[48,3200]{1,0:T(8,128)(2,1)S(1)}, u32[]{:S(2)}, u32[]{:S(2)}) collective-permute-start(bf16[48,3200]{1,0:T(8,128)(2,1)S(1)} %get-tuple-element.80), channel_id=1, source_target_pairs={{16,0},{32,16},{48,32},{64,48},{80,64},{96,80},{112,96},{0,112},{1... | collective-permute-start | bytes 921608 | tf_op jit(solution)/shard_map/ppermute | solution.py:657
  55.7 5.3 %collective-permute-start.6 = (bf16[48,3200]{1,0:T(8,128)(2,1)S(1)}, bf16[48,3200]{1,0:T(8,128)(2,1)S(1)}, u32[]{:S(2)}, u32[]{:S(2)}) collective-permute-start(bf16[48,3200]{1,0:T(8,128)(2,1)S(1)} %get-tuple-element.82), channel_id=1, source_target_pairs={{0,1},{1,2},{2,3},{3,4},{4,5},{5,6},{6,7},{7,8},{8,9},{9,10},{10,1... | collective-permute-start | bytes 921608 | tf_op jit(solution)/shard_map/ppermute | solution.py:662
  57.1 6.6 %collective-permute-start.7 = (bf16[48,3200]{1,0:T(8,128)(2,1)S(1)}, bf16[48,3200]{1,0:T(8,128)(2,1)S(1)}, u32[]{:S(2)}, u32[]{:S(2)}) collective-permute-start(bf16[48,3200]{1,0:T(8,128)(2,1)S(1)} %get-tuple-element.83), channel_id=1, source_target_pairs={{1,0},{2,1},{3,2},{4,3},{5,4},{6,5},{7,6},{8,7},{9,8},{10,9},{11,1... | collective-permute-start | bytes 921608 | tf_op jit(solution)/shard_map/ppermute | solution.py:663
  68.9 10.5 %collective-permute-start.8 = (bf16[48,3200]{1,0:T(8,128)(2,1)S(1)}, bf16[48,3200]{1,0:T(8,128)(2,1)S(1)}, u32[]{:S(2)}, u32[]{:S(2)}) collective-permute-start(bf16[48,3200]{1,0:T(8,128)(2,1)S(1)} %get-tuple-element.89), channel_id=1, source_target_pairs={{0,16},{16,32},{32,48},{48,64},{64,80},{80,96},{96,112},{112,0},{1... | collective-permute-start | bytes 921608 | tf_op jit(solution)/shard_map/ppermute | solution.py:656
  69.0 15.5 %collective-permute-start.9 = (bf16[48,3200]{1,0:T(8,128)(2,1)S(1)}, bf16[48,3200]{1,0:T(8,128)(2,1)S(1)}, u32[]{:S(2)}, u32[]{:S(2)}) collective-permute-start(bf16[48,3200]{1,0:T(8,128)(2,1)S(1)} %get-tuple-element.90), channel_id=1, source_target_pairs={{16,0},{32,16},{48,32},{64,48},{80,64},{96,80},{112,96},{0,112},{1... | collective-permute-start | bytes 921608 | tf_op jit(solution)/shard_map/ppermute | solution.py:657
  84.5 5.2 %collective-permute-start.10 = (bf16[48,3200]{1,0:T(8,128)(2,1)S(1)}, bf16[48,3200]{1,0:T(8,128)(2,1)S(1)}, u32[]{:S(2)}, u32[]{:S(2)}) collective-permute-start(bf16[48,3200]{1,0:T(8,128)(2,1)S(1)} %get-tuple-element.92), channel_id=1, source_target_pairs={{0,1},{1,2},{2,3},{3,4},{4,5},{5,6},{6,7},{7,8},{8,9},{9,10},{10,1... | collective-permute-start | bytes 921608 | tf_op jit(solution)/shard_map/ppermute | solution.py:662
  85.9 6.6 %collective-permute-start.11 = (bf16[48,3200]{1,0:T(8,128)(2,1)S(1)}, bf16[48,3200]{1,0:T(8,128)(2,1)S(1)}, u32[]{:S(2)}, u32[]{:S(2)}) collective-permute-start(bf16[48,3200]{1,0:T(8,128)(2,1)S(1)} %get-tuple-element.93), channel_id=1, source_target_pairs={{1,0},{2,1},{3,2},{4,3},{5,4},{6,5},{7,6},{8,7},{9,8},{10,9},{11,1... | collective-permute-start | bytes 921608 | tf_op jit(solution)/shard_map/ppermute | solution.py:663
  101.2 13.1 %collective-permute-start.12 = (bf16[48,3200]{1,0:T(8,128)(2,1)S(1)}, bf16[48,3200]{1,0:T(8,128)(2,1)S(1)}, u32[]{:S(2)}, u32[]{:S(2)}) collective-permute-start(bf16[48,3200]{1,0:T(8,128)(2,1)S(1)} %get-tuple-element.110), channel_id=1, source_target_pairs={{0,16},{16,32},{32,48},{48,64},{64,80},{80,96},{96,112},{112,0},{1... | collective-permute-start | bytes 921608 | tf_op jit(solution)/shard_map/ppermute | solution.py:656
  101.3 19.4 %collective-permute-start.13 = (bf16[48,3200]{1,0:T(8,128)(2,1)S(1)}, bf16[48,3200]{1,0:T(8,128)(2,1)S(1)}, u32[]{:S(2)}, u32[]{:S(2)}) collective-permute-start(bf16[48,3200]{1,0:T(8,128)(2,1)S(1)} %get-tuple-element.111), channel_id=1, source_target_pairs={{16,0},{32,16},{48,32},{64,48},{80,64},{96,80},{112,96},{0,112},{1... | collective-permute-start | bytes 921608 | tf_op jit(solution)/shard_map/ppermute | solution.py:657
  120.7 2.0 %collective-permute-start.14 = (f32[1024,128]{1,0:T(8,128)S(1)}, f32[1024,128]{1,0:T(8,128)S(1)}, u32[]{:S(2)}, u32[]{:S(2)}) collective-permute-start(f32[1024,128]{1,0:T(8,128)S(1)} %get-tuple-element.113), channel_id=1, source_target_pairs={{0,1},{1,0},{2,3},{3,2},{4,5},{5,4},{6,7},{7,6},{8,9},{9,8},{10,11... | collective-permute-start | bytes 1572872 | tf_op jit(solution)/shard_map/ppermute | solution.py:673
  142.1 20.2 %all-to-all-start.1 = ((f32[64,16,128]{2,1,0:T(8,128)}), f32[64,16,128]{2,1,0:T(8,128)S(1)}, u32[]{:S(2)}, u32[]{:S(2)}) async-start(f32[64,16,128]{2,1,0:T(8,128)} %shard_map.233), calls=%async_computation.1 | async-start | bytes 1048576 | tf_op jit(solution)/shard_map/all_to_all | solution.py:676
  147.1 11.4 %collective-permute-start.15 = (bf16[48,3200]{1,0:T(8,128)(2,1)S(1)}, bf16[48,3200]{1,0:T(8,128)(2,1)S(1)}, u32[]{:S(2)}, u32[]{:S(2)}) collective-permute-start(bf16[48,3200]{1,0:T(8,128)(2,1)S(1)} %get-tuple-element.116), channel_id=1, source_target_pairs={{0,1},{1,2},{2,3},{3,4},{4,5},{5,6},{6,7},{7,8},{8,9},{9,10},{10,1... | collective-permute-start | bytes 921608 | tf_op jit(solution)/shard_map/ppermute | solution.py:662
  150.4 10.4 %collective-permute-start.16 = (bf16[48,3200]{1,0:T(8,128)(2,1)S(1)}, bf16[48,3200]{1,0:T(8,128)(2,1)S(1)}, u32[]{:S(2)}, u32[]{:S(2)}) collective-permute-start(bf16[48,3200]{1,0:T(8,128)(2,1)S(1)} %get-tuple-element.117), channel_id=1, source_target_pairs={{1,0},{2,1},{3,2},{4,3},{5,4},{6,5},{7,6},{8,7},{9,8},{10,9},{11,1... | collective-permute-start | bytes 921608 | tf_op jit(solution)/shard_map/ppermute | solution.py:663
  162.4 3.5 %collective-permute-start.17 = (f32[1024,128]{1,0:T(8,128)S(1)}, f32[1024,128]{1,0:T(8,128)S(1)}, u32[]{:S(2)}, u32[]{:S(2)}) collective-permute-start(f32[1024,128]{1,0:T(8,128)S(1)} %bitcast.27), channel_id=1, source_target_pairs={{0,1},{1,0},{2,3},{3,2},{4,5},{5,4},{6,7},{7,6},{8,9},{9,8},{10,11... | collective-permute-start | bytes 1572872 | tf_op jit(solution)/shard_map/ppermute | solution.py:678

commit v3 on v2

--- a/solution.py
+++ b/solution.py
@@ -24,6 +24,7 @@
 F32 = jnp.float32
 BF16 = jnp.bfloat16
 REDUCE_ROWS = 2048
+LOSS_ROW = 1736
 
 
 def dot(a, b):
@@ -96,7 +97,7 @@
     ]
 
 
-def pack_kernel(core, features, send_index, own, low, middle, high, chosen_out, placed_out, lists):
+def pack_kernel(core, owner, features, send_index, own, low, middle, high, chosen_out, placed_out, lists):
     lists[...] = jnp.zeros_like(lists)
     for at in range(8):
         i, j = divmod(at if at < 4 else at + 1, 3)
@@ -268,7 +269,7 @@
     middle_out,
     high_out,
     messages,
-    lower_rows,
+    parts,
 ):
     table[0:ATOMS, :] = own[...]
     fill_ghosts(table, ATOMS, low, high, left, right)
@@ -298,14 +299,15 @@
         for component in range(first, last):
             upper, lower = split(here[:, cols(component - first)])
             gathered[comp_rows(component), :] = upper
-            lower_rows[comp_rows(component), :] = lower
+            parts[comp_rows(component), 0:C] = upper
+            parts[comp_rows(component), C:] = lower
     gate = None
     for degree in range(5):
         upper, lower = split(mixing[degree])
+        twice = jnp.concatenate([upper, upper], axis=0)
         for component in range(STARTS[degree], STARTS[degree] + DEGREES[degree]):
             rows = comp_rows(component)
-            out = dot(gathered[rows, :], upper)
-            out += dot(lower_rows[rows, :], upper) + dot(gathered[rows, :], lower)
+            out = dot(parts[rows, :], twice) + dot(parts[rows, 0:C], lower)
             mixed[rows, :] = out
             if component == 0:
                 gate = sigmoid(out)
@@ -458,7 +460,7 @@
     high_out,
     returned,
     grad_updated,
-    lower_rows,
+    parts,
     messages,
 ):
     fill_ghosts(returned, 0, low, high, left, right)
@@ -483,13 +485,14 @@
             )
         upper, lower = split(d_mixed)
         d_mixed_out[rows, :] = upper
-        lower_rows[rows, :] = lower
+        parts[rows, 0:C] = upper
+        parts[rows, C:] = lower
     for degree in range(5):
-        upper, lower = split(mixing[degree])
+        upper, lower = split(mixing[degree].T)
+        twice = jnp.concatenate([upper, upper], axis=0)
         for component in range(STARTS[degree], STARTS[degree] + DEGREES[degree]):
             rows = comp_rows(component)
-            out = dot_nt(d_mixed_out[rows, :], upper)
-            out += dot_nt(lower_rows[rows, :], upper) + dot_nt(d_mixed_out[rows, :], lower)
+            out = dot(parts[rows, :], twice) + dot(parts[rows, 0:C], lower)
             d_gathered[:, cols(component)] = (out * 0.125).astype(BF16)
 
     def block(step, carry):
@@ -579,11 +582,15 @@
     other_out[...] = reduced[pl.ds(pl.multiple_of((1 - side) * half, half), half), :]
 
 
-def share_kernel(pieces, out):
+def share_kernel(place, pieces, out):
     count = pieces.shape[0]
     total = pieces[0]
     for at in range(1, count):
         total = total + pieces[at]
+    row = lax.broadcasted_iota(jnp.int32, total.shape, 0)
+    rest = total - total.astype(BF16).astype(F32)
+    ours = (row >= LOSS_ROW % total.shape[0] + 4) & (row < LOSS_ROW % total.shape[0] + 8)
+    total = jnp.where(ours & (place[0] == 1), rest, total).astype(BF16)
     for at in range(count):
         out[at] = total
 
@@ -601,8 +608,8 @@
 ):
     half = REDUCE_ROWS // 2
     side = core[0]
-    sums[pl.ds(pl.multiple_of(side * half, half), half), :] = mine[...]
-    sums[pl.ds(pl.multiple_of((1 - side) * half, half), half), :] = other[...]
+    sums[pl.ds(pl.multiple_of(side * half, half), half), :] = mine[...].astype(F32)
+    sums[pl.ds(pl.multiple_of((1 - side) * half, half), half), :] = other[...].astype(F32)
     for block in range(10):
         second[:, cols(block)] = sums[block * HIDDEN : (block + 1) * HIDDEN, :]
     for degree in range(5):
@@ -610,7 +617,7 @@
         psecond[:, cols(degree)] = sums[1280 + degree * HIDDEN : 1280 + (degree + 1) * HIDDEN, :]
     readout[...] = sums[1600:1728, :]
     vector[...] = sums[1728:1729, :]
-    loss[...] = sums[1736:1737, :]
+    loss[...] = sums[LOSS_ROW : LOSS_ROW + 1, :] + sums[LOSS_ROW + 4 : LOSS_ROW + 5, :]
     pfirst[...] = sums[1744 : 1744 + BASIS, 0:HIDDEN]
     first[...] = sums[1792 : 1792 + BASIS, 0:HIDDEN]
 
@@ -664,7 +671,7 @@
     return (low, high, left, right), (to_right, to_left)
 
 
-def reduce_halves(mine, other):
+def reduce_halves(mine, other, owner):
     n_x, n_y = lax.axis_size("bx"), lax.axis_size("by")
     count = n_x * n_y // 2
     axes = ("bx", "by")
@@ -672,7 +679,7 @@
     groups = [[2 * i + core for i in range(count)] for core in range(2)]
     pair = (mine + lax.ppermute(other, "by", swap)).reshape(count, -1, C)
     pieces = lax.all_to_all(pair, axes, 0, 0, axis_index_groups=groups, tiled=True)
-    (spread,) = call(share_kernel, [(pair.shape, F32)], [], 10**6, pieces)
+    (spread,) = call(share_kernel, [(pair.shape, BF16)], [], 10**6, owner, pieces)
     whole = lax.all_to_all(spread, axes, 0, 0, axis_index_groups=groups, tiled=True)
     whole = whole.reshape(mine.shape)
     return whole, lambda after: lax.ppermute(lax.optimization_barrier((whole, after))[0], "by", swap)
@@ -700,7 +707,12 @@
     source = atom_source.reshape(1, EDGES)
     target = atom_target.reshape(1, EDGES)
     atoms = probe_atoms.reshape(1, PEDGES)
+    n_y = lax.axis_size("by")
     core = (lax.axis_index("by") % 2).reshape(1)
+    chunk = REDUCE_ROWS // (lax.axis_size("bx") * n_y)
+    half, place = divmod(LOSS_ROW, REDUCE_ROWS // 2)
+    loss_at = 2 * (place // chunk) + half
+    owner = (lax.axis_index("bx") * n_y + lax.axis_index("by") == loss_at).astype(jnp.int32).reshape(1)
 
     own, low, middle, high, chosen, placed = call(
         pack_kernel,
@@ -708,6 +720,7 @@
         [((C, C), F32)],
         2 * C * C * WIDE,
         core,
+        owner,
         field,
         send_index[0, 0],
     )
@@ -766,7 +779,7 @@
             ((2 * ATOMS, WIDE), BF16),
         ]
         + PACKETS,
-        [((EDGES, WIDE), BF16), ((COMP * ATOMS, C), BF16)],
+        [((EDGES, WIDE), BF16), ((COMP * ATOMS, 2 * C), BF16)],
         4 * 10**9,
         own,
         *received,
@@ -827,7 +840,7 @@
         [
             ((C, WIDE), BF16),
             ((COMP * ATOMS, C), BF16),
-            ((COMP * ATOMS, C), BF16),
+            ((COMP * ATOMS, 2 * C), BF16),
             ((EDGES, WIDE), BF16),
         ],
         6 * 10**9,
@@ -869,7 +882,7 @@
         placed,
     )
     mine, other, *_ = lax.optimization_barrier((mine, other, received[0], received[1]))
-    mine, swapped = reduce_halves(mine, other)
+    mine, swapped = reduce_halves(mine, other, owner)
     other = swapped(feature_grad)
     loss, first, second, mixing_grad, pfirst, psecond, readout, vector = call(
         unpack_kernel,

time: 167 us -> 162 us (0.970)
  blocking collectives: 18.4 us -> 0 us
  waiting for transfers between devices: 71.5 us -> 78.6 us
  starting transfers between devices: 39.1 us -> 45.4 us
    all_to_all x1 -> x0, blocking collectives: 18.4 us -> none  [reduce_halves(): lax.all_to_all(pair, axes, 0, 0, axis_index_groups=groups, tiled=True)]
    all_to_all x0 -> x1, waiting for transfers between devices: none -> 9.53 us  [reduce_halves(): lax.all_to_all(pair, axes, 0, 0, axis_index_groups=groups, tiled=True)]
    all_to_all x1, waiting for transfers between devices: 0.01 us -> 7.75 us  [reduce_halves(): lax.all_to_all(spread, axes, 0, 0, axis_index_groups=groups, tiled=True)]
    ppermute x4, waiting for transfers between devices: 14.8 us -> 7.09 us  [exchange(): left = lax.ppermute(to_right, 'by', up)]
    all_to_all x0 -> x1, starting transfers between devices: none -> 6.66 us  [reduce_halves(): lax.all_to_all(pair, axes, 0, 0, axis_index_groups=groups, tiled=True)]
    ppermute x4, waiting for transfers between devices: 10.7 us -> 8.33 us  [exchange(): right = lax.ppermute(to_left, 'by', down)]
  transfers between devices with their start and end apart: 19 -> 20, of which waited for: 17 -> 17; matrix products, arithmetic and copies ran while one was open for 0% -> 0% of each run, Pallas kernels for 7% -> 8%
where the time goes in v3:
time: 162 us; the launch traced here: 161 us
  waiting for transfers between devices  78.6 us (49%)
  starting transfers between devices  45.4 us (28%)
  Pallas kernels  33.5 us (21%)
  local copies, waits for them, and re-layouts  1.94 us (1%)
    pallas_call x14, Pallas kernels, call(): pl.pallas_call(kernel, out_shape=shapes, in_specs=[scalar if x.shape == (...  33.5 us
    ppermute x4, waiting for transfers between devices, exchange(): low = lax.ppermute(high_packet, 'bx', up)  24.1 us
    ppermute x4, waiting for transfers between devices, exchange(): high = lax.ppermute(low_packet, 'bx', down)  19.2 us
    ppermute x4, starting transfers between devices, exchange(): high = lax.ppermute(low_packet, 'bx', down)  16.8 us
    all_to_all x1, waiting for transfers between devices, reduce_halves(): lax.all_to_all(pair, axes, 0, 0, axis_index_groups=groups, tiled=True)  9.53 us
    ppermute x4, waiting for transfers between devices, exchange(): right = lax.ppermute(to_left, 'by', down)  8.33 us
    all_to_all x1, waiting for transfers between devices, reduce_halves(): lax.all_to_all(spread, axes, 0, 0, axis_index_groups=groups, tiled=True)  7.75 us
    ppermute x4, waiting for transfers between devices, exchange(): left = lax.ppermute(to_right, 'by', up)  7.09 us
  transfers between devices with their start and end apart: 20, of which 17 were waited for; matrix products, arithmetic and copies ran while one was open for 0% of the time, Pallas kernels for 8%

profile of v3, /device:TPU:1, one launch (start us, length us, event | category | flops | bytes accessed | tf_op | source)
XLA Modules:
  0.0 161.2 jit_solution(6301048179451607654)
XLA Ops:
  0.6 0.0 copy-start.14
  0.7 0.0 copy-start.13
  0.7 0.0 copy-start.7
  0.7 0.0 copy-start.6
  0.7 0.0 copy-start.11
  0.7 0.0 copy-start.10
  0.7 0.0 copy-start.8
  0.7 0.0 copy-start.9
  0.7 0.7 copy.33
  1.5 1.1 copy-done
  2.6 0.5 shard_map.223
  3.2 3.8 %collective-permute-start = (bf16[48,3200]{1,0:T(8,128)(2,1)S(1)}, bf16[48,3200]{1,0:T(8,128)(2,1)S(1)}, u32[]{:S(2)}, u32[]{:S(2)}) collective-permute-start(bf16[48,3200]{1,0:T(8,128)(2,1)S(1)} %get-tuple-element.69), channel_id=1, source_target_pairs={{0,16},{16,32},{32,48},{48,64},{64,80},{80,96},{96,112},{112,0},{1... | collective-permute-start | bytes 921608 | tf_op jit(solution)/shard_map/ppermute | solution.py:663
  7.0 2.3 %collective-permute-start.1 = (bf16[48,3200]{1,0:T(8,128)(2,1)S(1)}, bf16[48,3200]{1,0:T(8,128)(2,1)S(1)}, u32[]{:S(2)}, u32[]{:S(2)}) collective-permute-start(bf16[48,3200]{1,0:T(8,128)(2,1)S(1)} %get-tuple-element.70), channel_id=1, source_target_pairs={{16,0},{32,16},{48,32},{64,48},{80,64},{96,80},{112,96},{0,112},{1... | collective-permute-start | bytes 921608 | tf_op jit(solution)/shard_map/ppermute | solution.py:664
  9.2 10.2 %collective-permute-done.low = bf16[48,3200]{1,0:T(8,128)(2,1)S(1)} collective-permute-done((bf16[48,3200]{1,0:T(8,128)(2,1)S(1)}, bf16[48,3200]{1,0:T(8,128)(2,1)S(1)}, u32[]{:S(2)}, u32[]{:S(2)}) %collective-permute-start) | collective-permute-done | bytes 307232 | tf_op jit(solution)/shard_map/ppermute | solution.py:663
  19.5 4.0 %collective-permute-done.1.high = bf16[48,3200]{1,0:T(8,128)(2,1)S(1)} collective-permute-done((bf16[48,3200]{1,0:T(8,128)(2,1)S(1)}, bf16[48,3200]{1,0:T(8,128)(2,1)S(1)}, u32[]{:S(2)}, u32[]{:S(2)}) %collective-permute-start.1) | collective-permute-done | bytes 307232 | tf_op jit(solution)/shard_map/ppermute | solution.py:664
  23.5 2.1 %collective-permute-start.2 = (bf16[48,3200]{1,0:T(8,128)(2,1)S(1)}, bf16[48,3200]{1,0:T(8,128)(2,1)S(1)}, u32[]{:S(2)}, u32[]{:S(2)}) collective-permute-start(bf16[48,3200]{1,0:T(8,128)(2,1)S(1)} %get-tuple-element.72), channel_id=1, source_target_pairs={{0,1},{1,2},{2,3},{3,4},{4,5},{5,6},{6,7},{7,8},{8,9},{9,10},{10,1... | collective-permute-start | bytes 921608 | tf_op jit(solution)/shard_map/ppermute | solution.py:669
  25.6 0.0 collective-permute-start.3
  25.7 0.0 copy-start.2
  25.7 1.7 %shard_map.225 = (f32[1024,128]{1,0:T(8,128)S(1)}, f32[24,1024]{1,0:T(8,128)S(1)}, f32[1024,64]{1,0:T(8,128)S(1)}, bf16[1024,192]{1,0:T(8,128)(2,1)S(1)}, bf16[1...) custom-call(f32[3,1024]{1,0:T(4,128)S(1)} %bitcast.32, ...), custom_call_target="tpu_custom_call" | custom-call | flops 1000000000 | bytes 3774976 | tf_op jit(solution)/shard_map/pallas_call | solution.py:631
  27.5 1.9 %collective-permute-done.2.left = bf16[48,3200]{1,0:T(8,128)(2,1)S(1)} collective-permute-done((bf16[48,3200]{1,0:T(8,128)(2,1)S(1)}, bf16[48,3200]{1,0:T(8,128)(2,1)S(1)}, u32[]{:S(2)}, u32[]{:S(2)}) %collective-permute-start.2) | collective-permute-done | bytes 307232 | tf_op jit(solution)/shard_map/ppermute | solution.py:669
  29.4 2.8 %collective-permute-done.3.right = bf16[48,3200]{1,0:T(8,128)(2,1)S(1)} collective-permute-done((bf16[48,3200]{1,0:T(8,128)(2,1)S(1)}, bf16[48,3200]{1,0:T(8,128)(2,1)S(1)}, u32[]{:S(2)}, u32[]{:S(2)}) %collective-permute-start.3) | collective-permute-done | bytes 307232 | tf_op jit(solution)/shard_map/ppermute | solution.py:670
  32.2 0.0 copy-done.2
  32.2 6.0 %shard_map.226 = (bf16[128,3200]{1,0:T(8,128)(2,1)S(1)}, bf16[3200,128]{1,0:T(8,128)(2,1)S(1)}, f32[3200,128]{1,0:T(8,128)S(1)}, bf16[256,3200]{1,0:T(8,128)(2,1...) custom-call(bf16[128,3200]{1,0:T(8,128)(2,1)S(1)} %get-tuple-element.68.own, ...), custom_call_target="tpu_custom_call" | custom-call | flops 4000000000 | bytes 9555968 | tf_op jit(solution)/shard_map/pallas_call | solution.py:631
  38.2 0.7 collective-permute-start.4
  39.0 4.4 %collective-permute-start.5 = (bf16[48,3200]{1,0:T(8,128)(2,1)S(1)}, bf16[48,3200]{1,0:T(8,128)(2,1)S(1)}, u32[]{:S(2)}, u32[]{:S(2)}) collective-permute-start(bf16[48,3200]{1,0:T(8,128)(2,1)S(1)} %get-tuple-element.80), channel_id=1, source_target_pairs={{16,0},{32,16},{48,32},{64,48},{80,64},{96,80},{112,96},{0,112},{1... | collective-permute-start | bytes 921608 | tf_op jit(solution)/shard_map/ppermute | solution.py:664
  43.4 8.4 %collective-permute-done.4.low = bf16[48,3200]{1,0:T(8,128)(2,1)S(1)} collective-permute-done((bf16[48,3200]{1,0:T(8,128)(2,1)S(1)}, bf16[48,3200]{1,0:T(8,128)(2,1)S(1)}, u32[]{:S(2)}, u32[]{:S(2)}) %collective-permute-start.4) | collective-permute-done | bytes 307232 | tf_op jit(solution)/shard_map/ppermute | solution.py:663
  51.8 3.4 %collective-permute-done.5.high = bf16[48,3200]{1,0:T(8,128)(2,1)S(1)} collective-permute-done((bf16[48,3200]{1,0:T(8,128)(2,1)S(1)}, bf16[48,3200]{1,0:T(8,128)(2,1)S(1)}, u32[]{:S(2)}, u32[]{:S(2)}) %collective-permute-start.5) | collective-permute-done | bytes 307232 | tf_op jit(solution)/shard_map/ppermute | solution.py:664
  55.2 1.5 collective-permute-start.6
  56.7 0.4 collective-permute-start.7
  57.1 3.4 %collective-permute-done.6.left = bf16[48,3200]{1,0:T(8,128)(2,1)S(1)} collective-permute-done((bf16[48,3200]{1,0:T(8,128)(2,1)S(1)}, bf16[48,3200]{1,0:T(8,128)(2,1)S(1)}, u32[]{:S(2)}, u32[]{:S(2)}) %collective-permute-start.6) | collective-permute-done | bytes 307232 | tf_op jit(solution)/shard_map/ppermute | solution.py:669
  60.5 2.8 %collective-permute-done.7.right = bf16[48,3200]{1,0:T(8,128)(2,1)S(1)} collective-permute-done((bf16[48,3200]{1,0:T(8,128)(2,1)S(1)}, bf16[48,3200]{1,0:T(8,128)(2,1)S(1)}, u32[]{:S(2)}, u32[]{:S(2)}) %collective-permute-start.7) | collective-permute-done | bytes 307232 | tf_op jit(solution)/shard_map/ppermute | solution.py:670
  63.3 5.2 %shard_map.228 = (f32[3200,128]{1,0:T(8,128)S(1)}, bf16[48,3200]{1,0:T(8,128)(2,1)S(1)}, bf16[32,3200]{1,0:T(8,128)(2,1)S(1)}, bf16[48,3200]{1,0:T(8,128)(2,1)S(...) custom-call(bf16[128,3200]{1,0:T(8,128)(2,1)S(1)} %get-tuple-element.78.own, ...), custom_call_target="tpu_custom_call" | custom-call | flops 4000000000 | bytes 6072832 | tf_op jit(solution)/shard_map/pallas_call | solution.py:631
  68.5 0.1 collective-permute-start.8
  68.6 5.1 %collective-permute-start.9 = (bf16[48,3200]{1,0:T(8,128)(2,1)S(1)}, bf16[48,3200]{1,0:T(8,128)(2,1)S(1)}, u32[]{:S(2)}, u32[]{:S(2)}) collective-permute-start(bf16[48,3200]{1,0:T(8,128)(2,1)S(1)} %get-tuple-element.90), channel_id=1, source_target_pairs={{16,0},{32,16},{48,32},{64,48},{80,64},{96,80},{112,96},{0,112},{1... | collective-permute-start | bytes 921608 | tf_op jit(solution)/shard_map/ppermute | solution.py:664
  73.6 5.4 %collective-permute-done.8.low = bf16[48,3200]{1,0:T(8,128)(2,1)S(1)} collective-permute-done((bf16[48,3200]{1,0:T(8,128)(2,1)S(1)}, bf16[48,3200]{1,0:T(8,128)(2,1)S(1)}, u32[]{:S(2)}, u32[]{:S(2)}) %collective-permute-start.8) | collective-permute-done | bytes 307232 | tf_op jit(solution)/shard_map/ppermute | solution.py:663
  79.0 4.9 %collective-permute-done.9.high = bf16[48,3200]{1,0:T(8,128)(2,1)S(1)} collective-permute-done((bf16[48,3200]{1,0:T(8,128)(2,1)S(1)}, bf16[48,3200]{1,0:T(8,128)(2,1)S(1)}, u32[]{:S(2)}, u32[]{:S(2)}) %collective-permute-start.9) | collective-permute-done | bytes 307232 | tf_op jit(solution)/shard_map/ppermute | solution.py:664
  84.0 1.4 collective-permute-start.10
  85.5 1.2 collective-permute-start.11
  86.7 0.8 shard_map.231.probe_grads
  87.5 1.8 %collective-permute-done.10.left = bf16[48,3200]{1,0:T(8,128)(2,1)S(1)} collective-permute-done((bf16[48,3200]{1,0:T(8,128)(2,1)S(1)}, bf16[48,3200]{1,0:T(8,128)(2,1)S(1)}, u32[]{:S(2)}, u32[]{:S(2)}) %collective-permute-start.10) | collective-permute-done | bytes 307232 | tf_op jit(solution)/shard_map/ppermute | solution.py:669
  89.3 2.8 %collective-permute-done.11.right = bf16[48,3200]{1,0:T(8,128)(2,1)S(1)} collective-permute-done((bf16[48,3200]{1,0:T(8,128)(2,1)S(1)}, bf16[48,3200]{1,0:T(8,128)(2,1)S(1)}, u32[]{:S(2)}, u32[]{:S(2)}) %collective-permute-start.11) | collective-permute-done | bytes 307232 | tf_op jit(solution)/shard_map/ppermute | solution.py:670
  92.1 7.5 %shard_map.230 = (f32[3200,128]{1,0:T(8,128)S(1)}, bf16[128,3200]{1,0:T(8,128)(2,1)S(1)}, bf16[3200,128]{1,0:T(8,128)(2,1)S(1)}, bf16[48,3200]{1,0:T(8,128)(2,1)...) custom-call(f32[3200,128]{1,0:T(8,128)S(1)} %get-tuple-element.88.grad_own, ...), custom_call_target="tpu_custom_call" | custom-call | flops 6000000000 | bytes 10375168 | tf_op jit(solution)/shard_map/pallas_call | solution.py:631
  99.5 0.3 collective-permute-start.12
  99.8 5.1 %collective-permute-start.13 = (bf16[48,3200]{1,0:T(8,128)(2,1)S(1)}, bf16[48,3200]{1,0:T(8,128)(2,1)S(1)}, u32[]{:S(2)}, u32[]{:S(2)}) collective-permute-start(bf16[48,3200]{1,0:T(8,128)(2,1)S(1)} %get-tuple-element.111), channel_id=1, source_target_pairs={{16,0},{32,16},{48,32},{64,48},{80,64},{96,80},{112,96},{0,112},{1... | collective-permute-start | bytes 921608 | tf_op jit(solution)/shard_map/ppermute | solution.py:664
  104.9 7.4 %shard_map.232 = (f32[1024,128]{1,0:T(8,128)S(1)}, f32[1024,128]{1,0:T(8,128)S(1)}) custom-call(s32[1]{0:T(128)} %bitcast.core, bf16[128,3200]{1,0:T(8,128)(2,1)S(1)} %get-tuple-element.96.d_gathered, bf16[3200,128]{1,0:T(8,128)(2,1)S(1)} %get-tuple-element.97.d_mixed, bf16[256,3200]{1,0:T(8,128)(2,1)S(1)} %get-tuple-element.98.table, ...), custom_call_target="tpu_custom_call" | custom-call | flops 6000000000 | bytes 7045124 | tf_op jit(solution)/shard_map/pallas_call | solution.py:631
  112.3 0.0 collective-permute-done.12.low
  112.3 6.8 %collective-permute-done.13.high = bf16[48,3200]{1,0:T(8,128)(2,1)S(1)} collective-permute-done((bf16[48,3200]{1,0:T(8,128)(2,1)S(1)}, bf16[48,3200]{1,0:T(8,128)(2,1)S(1)}, u32[]{:S(2)}, u32[]{:S(2)}) %collective-permute-start.13) | collective-permute-done | bytes 307232 | tf_op jit(solution)/shard_map/ppermute | solution.py:664
  119.2 0.5 collective-permute-start.14
  119.7 1.5 collective-permute-done.14
  121.2 0.9 add.12
  122.1 6.7 %all-to-all-start = ((f32[64,16,128]{2,1,0:T(8,128)}), f32[64,16,128]{2,1,0:T(8,128)S(1)}, u32[]{:S(2)}, u32[]{:S(2)}) async-start(f32[64,16,128]{2,1,0:T(8,128)} %bitcast.43), calls=%async_computation | async-start | bytes 1048576 | tf_op jit(solution)/shard_map/all_to_all | solution.py:681
  128.7 0.9 shard_map.234
  129.6 1.8 %collective-permute-start.15 = (bf16[48,3200]{1,0:T(8,128)(2,1)}, bf16[48,3200]{1,0:T(8,128)(2,1)S(1)}, u32[]{:S(2)}, u32[]{:S(2)}) collective-permute-start(bf16[48,3200]{1,0:T(8,128)(2,1)} %get-tuple-element.116), channel_id=1, source_target_pairs={{0,1},{1,2},{2,3},{3,4},{4,5},{5,6},{6,7},{7,8},{8,9},{9,10},{10,1... | collective-permute-start | bytes 921608 | tf_op jit(solution)/shard_map/ppermute | solution.py:669
  131.4 0.0 collective-permute-start.16
  131.4 9.5 %all-to-all-done.pieces = f32[64,16,128]{2,1,0:T(8,128)S(1)} async-done(((f32[64,16,128]{2,1,0:T(8,128)}), f32[64,16,128]{2,1,0:T(8,128)S(1)}, u32[]{:S(2)}, u32[]{:S(2)}) %all-to-all-start) | async-done | bytes 524320 | tf_op jit(solution)/shard_map/all_to_all | solution.py:681
  141.0 0.8 shard_map.233
  141.8 4.6 %all-to-all-start.1 = ((bf16[64,16,128]{2,1,0:T(8,128)(2,1)}), bf16[64,16,128]{2,1,0:T(8,128)(2,1)S(1)}, u32[]{:S(2)}, u32[]{:S(2)}) async-start(bf16[64,16,128]{2,1,0:T(8,128)(2,1)} %shard_map.233), calls=%async_computation.1 | async-start | bytes 524288 | tf_op jit(solution)/shard_map/all_to_all | solution.py:683
  146.4 0.0 collective-permute-done.15.left
  146.4 0.0 collective-permute-done.16.right
  146.4 1.6 shard_map.235
  148.0 7.7 %all-to-all-done.1 = bf16[64,16,128]{2,1,0:T(8,128)(2,1)S(1)} async-done(((bf16[64,16,128]{2,1,0:T(8,128)(2,1)}), bf16[64,16,128]{2,1,0:T(8,128)(2,1)S(1)}, u32[]{:S(2)}, u32[]{:S(2)}) %all-to-all-start.1) | async-done | bytes 262176 | tf_op jit(solution)/shard_map/all_to_all | solution.py:683
  155.7 3.3 %collective-permute-start.17 = (bf16[1024,128]{1,0:T(8,128)(2,1)S(1)}, bf16[1024,128]{1,0:T(8,128)(2,1)S(1)}, u32[]{:S(2)}, u32[]{:S(2)}) collective-permute-start(bf16[1024,128]{1,0:T(8,128)(2,1)S(1)} %bitcast.28), channel_id=1, source_target_pairs={{0,1},{1,0},{2,3},{3,2},{4,5},{5,4},{6,7},{7,6},{8,9},{9,8},{10,11... | collective-permute-start | bytes 786440 | tf_op jit(solution)/shard_map/ppermute | solution.py:685
  159.1 1.2 collective-permute-done.17.other
  160.2 1.0 shard_map.236
  (24 shorter events, 0.2 us)
Async XLA Ops:
  0.6 25.0 %copy-start.14 = (f32[1,1,3,512]{3,1,2,0:T(1,128)S(1)}, f32[1,1,3,512]{3,1,2,0:T(1,128)}, u32[]{:S(2)}) copy-start(f32[1,1,3,512]{3,1,2,0:T(1,128)} %param.21) | copy-start | bytes 18436
  0.7 25.0 %copy-start.13 = (f32[1,1,3,1024]{3,1,2,0:T(1,128)S(1)}, f32[1,1,3,1024]{3,1,2,0:T(1,128)}, u32[]{:S(2)}) copy-start(f32[1,1,3,1024]{3,1,2,0:T(1,128)} %param.18) | copy-start | bytes 36868
  0.7 25.0 %copy-start.7 = (f32[20,64]{1,0:T(8,128)S(1)}, f32[20,64]{1,0:T(8,128)}, u32[]{:S(2)}) copy-start(f32[20,64]{1,0:T(8,128)} %pfirst.1) | copy-start | bytes 15364
  0.7 25.0 %copy-start.6 = (f32[20,64]{1,0:T(8,128)S(1)}, f32[20,64]{1,0:T(8,128)}, u32[]{:S(2)}) copy-start(f32[20,64]{1,0:T(8,128)} %first.1) | copy-start | bytes 15364
  0.7 25.0 %copy-start.11 = (s32[1,1,128]{2,1,0:T(1,128)S(1)}, s32[1,1,128]{2,1,0:T(1,128)}, u32[]{:S(2)}) copy-start(s32[1,1,128]{2,1,0:T(1,128)} %param.24) | copy-start | bytes 1540
  0.7 25.0 %copy-start.10 = (s32[1,1,512]{2,1,0:T(1,128)S(1)}, s32[1,1,512]{2,1,0:T(1,128)}, u32[]{:S(2)}) copy-start(s32[1,1,512]{2,1,0:T(1,128)} %param.22) | copy-start | bytes 6148
  0.7 25.0 %copy-start.8 = (s32[1,1,1024]{2,1,0:T(1,128)S(1)}, s32[1,1,1024]{2,1,0:T(1,128)}, u32[]{:S(2)}) copy-start(s32[1,1,1024]{2,1,0:T(1,128)} %param.20) | copy-start | bytes 12292
  0.7 25.0 %copy-start.9 = (s32[1,1,1024]{2,1,0:T(1,128)S(1)}, s32[1,1,1024]{2,1,0:T(1,128)}, u32[]{:S(2)}) copy-start(s32[1,1,1024]{2,1,0:T(1,128)} %param.19) | copy-start | bytes 12292
  1.5 1.1 copy-start
  2.6 23.1 %copy-start.1 = (f32[64,1280]{1,0:T(8,128)S(1)}, f32[64,1280]{1,0:T(8,128)}, u32[]{:S(2)}) copy-start(f32[64,1280]{1,0:T(8,128)} %second.1) | copy-start | bytes 983044
  2.6 23.1 %copy-start.3 = (f32[64,640]{1,0:T(8,128)S(1)}, f32[64,640]{1,0:T(8,128)}, u32[]{:S(2)}) copy-start(f32[64,640]{1,0:T(8,128)} %psecond.1) | copy-start | bytes 491524
  2.6 23.1 %copy-start.4 = (f32[1,1,32768]{2,1,0:T(1,128)S(1)}, f32[1,1,32768]{2,1,0:T(1,128)}, u32[]{:S(2)}) copy-start(f32[1,1,32768]{2,1,0:T(1,128)} %param.23) | copy-start | bytes 393220
  3.2 16.3 %collective-permute-start = (bf16[48,3200]{1,0:T(8,128)(2,1)S(1)}, bf16[48,3200]{1,0:T(8,128)(2,1)S(1)}, u32[]{:S(2)}, u32[]{:S(2)}) collective-permute-start(bf16[48,3200]{1,0:T(8,128)(2,1)S(1)} %get-tuple-element.69), channel_id=1, source_target_pairs={{0,16},{16,32},{32,48},{48,64},{64,80},{80,96},{96,112},{112,0},{1... | collective-permute-start | bytes 921608 | tf_op jit(solution)/shard_map/ppermute | solution.py:663
  7.0 16.5 %collective-permute-start.1 = (bf16[48,3200]{1,0:T(8,128)(2,1)S(1)}, bf16[48,3200]{1,0:T(8,128)(2,1)S(1)}, u32[]{:S(2)}, u32[]{:S(2)}) collective-permute-start(bf16[48,3200]{1,0:T(8,128)(2,1)S(1)} %get-tuple-element.70), channel_id=1, source_target_pairs={{16,0},{32,16},{48,32},{64,48},{80,64},{96,80},{112,96},{0,112},{1... | collective-permute-start | bytes 921608 | tf_op jit(solution)/shard_map/ppermute | solution.py:664
  23.5 5.9 %collective-permute-start.2 = (bf16[48,3200]{1,0:T(8,128)(2,1)S(1)}, bf16[48,3200]{1,0:T(8,128)(2,1)S(1)}, u32[]{:S(2)}, u32[]{:S(2)}) collective-permute-start(bf16[48,3200]{1,0:T(8,128)(2,1)S(1)} %get-tuple-element.72), channel_id=1, source_target_pairs={{0,1},{1,2},{2,3},{3,4},{4,5},{5,6},{6,7},{7,8},{8,9},{9,10},{10,1... | collective-permute-start | bytes 921608 | tf_op jit(solution)/shard_map/ppermute | solution.py:669
  25.6 6.6 %collective-permute-start.3 = (bf16[48,3200]{1,0:T(8,128)(2,1)S(1)}, bf16[48,3200]{1,0:T(8,128)(2,1)S(1)}, u32[]{:S(2)}, u32[]{:S(2)}) collective-permute-start(bf16[48,3200]{1,0:T(8,128)(2,1)S(1)} %get-tuple-element.73), channel_id=1, source_target_pairs={{1,0},{2,1},{3,2},{4,3},{5,4},{6,5},{7,6},{8,7},{9,8},{10,9},{11,1... | collective-permute-start | bytes 921608 | tf_op jit(solution)/shard_map/ppermute | solution.py:670
  25.7 6.5 %copy-start.2 = (f32[5,128,128]{2,1,0:T(8,128)S(1)}, f32[5,128,128]{2,1,0:T(8,128)}, u32[]{:S(2)}) copy-start(f32[5,128,128]{2,1,0:T(8,128)} %mixing.3) | copy-start | bytes 983044
  32.2 31.1 %copy-start.5 = (f32[128,128]{1,0:T(8,128)S(1)}, f32[128,128]{1,0:T(8,128)}, u32[]{:S(2)}) copy-start(f32[128,128]{1,0:T(8,128)} %first_readout.1) | copy-start | bytes 196612
  32.2 31.1 %copy-start.12 = (f32[128]{0:T(128)S(1)}, f32[128]{0:T(128)}, u32[]{:S(2)}) copy-start(f32[128]{0:T(128)} %param.31) | copy-start | bytes 1540
  38.2 13.5 %collective-permute-start.4 = (bf16[48,3200]{1,0:T(8,128)(2,1)S(1)}, bf16[48,3200]{1,0:T(8,128)(2,1)S(1)}, u32[]{:S(2)}, u32[]{:S(2)}) collective-permute-start(bf16[48,3200]{1,0:T(8,128)(2,1)S(1)} %get-tuple-element.79), channel_id=1, source_target_pairs={{0,16},{16,32},{32,48},{48,64},{64,80},{80,96},{96,112},{112,0},{1... | collective-permute-start | bytes 921608 | tf_op jit(solution)/shard_map/ppermute | solution.py:663
  39.0 16.2 %collective-permute-start.5 = (bf16[48,3200]{1,0:T(8,128)(2,1)S(1)}, bf16[48,3200]{1,0:T(8,128)(2,1)S(1)}, u32[]{:S(2)}, u32[]{:S(2)}) collective-permute-start(bf16[48,3200]{1,0:T(8,128)(2,1)S(1)} %get-tuple-element.80), channel_id=1, source_target_pairs={{16,0},{32,16},{48,32},{64,48},{80,64},{96,80},{112,96},{0,112},{1... | collective-permute-start | bytes 921608 | tf_op jit(solution)/shard_map/ppermute | solution.py:664
  55.2 5.3 %collective-permute-start.6 = (bf16[48,3200]{1,0:T(8,128)(2,1)S(1)}, bf16[48,3200]{1,0:T(8,128)(2,1)S(1)}, u32[]{:S(2)}, u32[]{:S(2)}) collective-permute-start(bf16[48,3200]{1,0:T(8,128)(2,1)S(1)} %get-tuple-element.82), channel_id=1, source_target_pairs={{0,1},{1,2},{2,3},{3,4},{4,5},{5,6},{6,7},{7,8},{8,9},{9,10},{10,1... | collective-permute-start | bytes 921608 | tf_op jit(solution)/shard_map/ppermute | solution.py:669
  56.7 6.6 %collective-permute-start.7 = (bf16[48,3200]{1,0:T(8,128)(2,1)S(1)}, bf16[48,3200]{1,0:T(8,128)(2,1)S(1)}, u32[]{:S(2)}, u32[]{:S(2)}) collective-permute-start(bf16[48,3200]{1,0:T(8,128)(2,1)S(1)} %get-tuple-element.83), channel_id=1, source_target_pairs={{1,0},{2,1},{3,2},{4,3},{5,4},{6,5},{7,6},{8,7},{9,8},{10,9},{11,1... | collective-permute-start | bytes 921608 | tf_op jit(solution)/shard_map/ppermute | solution.py:670
  68.5 10.6 %collective-permute-start.8 = (bf16[48,3200]{1,0:T(8,128)(2,1)S(1)}, bf16[48,3200]{1,0:T(8,128)(2,1)S(1)}, u32[]{:S(2)}, u32[]{:S(2)}) collective-permute-start(bf16[48,3200]{1,0:T(8,128)(2,1)S(1)} %get-tuple-element.89), channel_id=1, source_target_pairs={{0,16},{16,32},{32,48},{48,64},{64,80},{80,96},{96,112},{112,0},{1... | collective-permute-start | bytes 921608 | tf_op jit(solution)/shard_map/ppermute | solution.py:663
  68.6 15.4 %collective-permute-start.9 = (bf16[48,3200]{1,0:T(8,128)(2,1)S(1)}, bf16[48,3200]{1,0:T(8,128)(2,1)S(1)}, u32[]{:S(2)}, u32[]{:S(2)}) collective-permute-start(bf16[48,3200]{1,0:T(8,128)(2,1)S(1)} %get-tuple-element.90), channel_id=1, source_target_pairs={{16,0},{32,16},{48,32},{64,48},{80,64},{96,80},{112,96},{0,112},{1... | collective-permute-start | bytes 921608 | tf_op jit(solution)/shard_map/ppermute | solution.py:664
  84.0 5.2 %collective-permute-start.10 = (bf16[48,3200]{1,0:T(8,128)(2,1)S(1)}, bf16[48,3200]{1,0:T(8,128)(2,1)S(1)}, u32[]{:S(2)}, u32[]{:S(2)}) collective-permute-start(bf16[48,3200]{1,0:T(8,128)(2,1)S(1)} %get-tuple-element.92), channel_id=1, source_target_pairs={{0,1},{1,2},{2,3},{3,4},{4,5},{5,6},{6,7},{7,8},{8,9},{9,10},{10,1... | collective-permute-start | bytes 921608 | tf_op jit(solution)/shard_map/ppermute | solution.py:669
  85.5 6.6 %collective-permute-start.11 = (bf16[48,3200]{1,0:T(8,128)(2,1)S(1)}, bf16[48,3200]{1,0:T(8,128)(2,1)S(1)}, u32[]{:S(2)}, u32[]{:S(2)}) collective-permute-start(bf16[48,3200]{1,0:T(8,128)(2,1)S(1)} %get-tuple-element.93), channel_id=1, source_target_pairs={{1,0},{2,1},{3,2},{4,3},{5,4},{6,5},{7,6},{8,7},{9,8},{10,9},{11,1... | collective-permute-start | bytes 921608 | tf_op jit(solution)/shard_map/ppermute | solution.py:670
  99.5 12.8 %collective-permute-start.12 = (bf16[48,3200]{1,0:T(8,128)(2,1)S(1)}, bf16[48,3200]{1,0:T(8,128)(2,1)S(1)}, u32[]{:S(2)}, u32[]{:S(2)}) collective-permute-start(bf16[48,3200]{1,0:T(8,128)(2,1)S(1)} %get-tuple-element.110), channel_id=1, source_target_pairs={{0,16},{16,32},{32,48},{48,64},{64,80},{80,96},{96,112},{112,0},{1... | collective-permute-start | bytes 921608 | tf_op jit(solution)/shard_map/ppermute | solution.py:663
  99.8 19.3 %collective-permute-start.13 = (bf16[48,3200]{1,0:T(8,128)(2,1)S(1)}, bf16[48,3200]{1,0:T(8,128)(2,1)S(1)}, u32[]{:S(2)}, u32[]{:S(2)}) collective-permute-start(bf16[48,3200]{1,0:T(8,128)(2,1)S(1)} %get-tuple-element.111), channel_id=1, source_target_pairs={{16,0},{32,16},{48,32},{64,48},{80,64},{96,80},{112,96},{0,112},{1... | collective-permute-start | bytes 921608 | tf_op jit(solution)/shard_map/ppermute | solution.py:664
  119.2 2.1 %collective-permute-start.14 = (f32[1024,128]{1,0:T(8,128)S(1)}, f32[1024,128]{1,0:T(8,128)S(1)}, u32[]{:S(2)}, u32[]{:S(2)}) collective-permute-start(f32[1024,128]{1,0:T(8,128)S(1)} %get-tuple-element.113), channel_id=1, source_target_pairs={{0,1},{1,0},{2,3},{3,2},{4,5},{5,4},{6,7},{7,6},{8,9},{9,8},{10,11... | collective-permute-start | bytes 1572872 | tf_op jit(solution)/shard_map/ppermute | solution.py:680
  122.1 18.9 %all-to-all-start = ((f32[64,16,128]{2,1,0:T(8,128)}), f32[64,16,128]{2,1,0:T(8,128)S(1)}, u32[]{:S(2)}, u32[]{:S(2)}) async-start(f32[64,16,128]{2,1,0:T(8,128)} %bitcast.43), calls=%async_computation | async-start | bytes 1048576 | tf_op jit(solution)/shard_map/all_to_all | solution.py:681
  129.6 16.8 %collective-permute-start.15 = (bf16[48,3200]{1,0:T(8,128)(2,1)}, bf16[48,3200]{1,0:T(8,128)(2,1)S(1)}, u32[]{:S(2)}, u32[]{:S(2)}) collective-permute-start(bf16[48,3200]{1,0:T(8,128)(2,1)} %get-tuple-element.116), channel_id=1, source_target_pairs={{0,1},{1,2},{2,3},{3,4},{4,5},{5,6},{6,7},{7,8},{8,9},{9,10},{10,1... | collective-permute-start | bytes 921608 | tf_op jit(solution)/shard_map/ppermute | solution.py:669
  131.4 15.0 %collective-permute-start.16 = (bf16[48,3200]{1,0:T(8,128)(2,1)}, bf16[48,3200]{1,0:T(8,128)(2,1)S(1)}, u32[]{:S(2)}, u32[]{:S(2)}) collective-permute-start(bf16[48,3200]{1,0:T(8,128)(2,1)} %get-tuple-element.117), channel_id=1, source_target_pairs={{1,0},{2,1},{3,2},{4,3},{5,4},{6,5},{7,6},{8,7},{9,8},{10,9},{11,1... | collective-permute-start | bytes 921608 | tf_op jit(solution)/shard_map/ppermute | solution.py:670
  141.8 13.9 %all-to-all-start.1 = ((bf16[64,16,128]{2,1,0:T(8,128)(2,1)}), bf16[64,16,128]{2,1,0:T(8,128)(2,1)S(1)}, u32[]{:S(2)}, u32[]{:S(2)}) async-start(bf16[64,16,128]{2,1,0:T(8,128)(2,1)} %shard_map.233), calls=%async_computation.1 | async-start | bytes 524288 | tf_op jit(solution)/shard_map/all_to_all | solution.py:683
  155.7 4.5 %collective-permute-start.17 = (bf16[1024,128]{1,0:T(8,128)(2,1)S(1)}, bf16[1024,128]{1,0:T(8,128)(2,1)S(1)}, u32[]{:S(2)}, u32[]{:S(2)}) collective-permute-start(bf16[1024,128]{1,0:T(8,128)(2,1)S(1)} %bitcast.28), channel_id=1, source_target_pairs={{0,1},{1,0},{2,3},{3,2},{4,5},{5,4},{6,7},{7,6},{8,9},{9,8},{10,11... | collective-permute-start | bytes 786440 | tf_op jit(solution)/shard_map/ppermute | solution.py:685

commit v4 on v3

--- a/solution.py
+++ b/solution.py
@@ -100,7 +100,7 @@
 def pack_kernel(core, owner, features, send_index, own, low, middle, high, chosen_out, placed_out, lists):
     lists[...] = jnp.zeros_like(lists)
     for at in range(8):
-        i, j = divmod(at if at < 4 else at + 1, 3)
+        j, i = divmod(at if at < 4 else at + 1, 3)
         lists[at : at + 1, 0:16] = send_index[i, j : j + 1, :].astype(F32)
     turned = lists[...].T
     lane = lax.broadcasted_iota(jnp.int32, (16, C), 1).astype(F32)
@@ -212,7 +212,11 @@
     picked_out[...] = jnp.broadcast_to(values, (C, PROBES)).T
 
 
-def fill_ghosts(rows, base, low, high, left, right):
+TABLE_ORDER = (0, 3, 5, 1, 6, 2, 4, 7)
+PACKET_ORDER = tuple(range(8))
+
+
+def fill_ghosts(rows, base, low, high, left, right, order):
     pieces = (
         left[16:32],
         low[16:32],
@@ -223,7 +227,7 @@
         high[16:32],
         right[32:48],
     )
-    for at, piece in enumerate(pieces):
+    for at, piece in zip(order, pieces):
         rows[base + 16 * at : base + 16 * at + 16, :] = piece
 
 
@@ -272,7 +276,7 @@
     parts,
 ):
     table[0:ATOMS, :] = own[...]
-    fill_ghosts(table, ATOMS, low, high, left, right)
+    fill_ghosts(table, ATOMS, low, high, left, right, TABLE_ORDER)
 
     def block(step, carry):
         rows = pl.ds(pl.multiple_of(step * EB, EB), EB)
@@ -326,9 +330,14 @@
                 here = here + add[comp_rows(component), :]
             own_grad[comp_rows(component), :] = here
         ghosts = total[ATOMS:, :].astype(BF16)
-        low[:, wide] = ghosts[0:48]
-        middle[:, wide] = ghosts[48:80]
-        high[:, wide] = ghosts[80:128]
+        for place, at in enumerate(TABLE_ORDER):
+            piece = ghosts[16 * at : 16 * at + 16]
+            if place < 3:
+                low[16 * place : 16 * place + 16, wide] = piece
+            elif place < 5:
+                middle[16 * (place - 3) : 16 * (place - 3) + 16, wide] = piece
+            else:
+                high[16 * (place - 5) : 16 * (place - 5) + 16, wide] = piece
 
 
 def probe_kernel(
@@ -356,7 +365,7 @@
     messages,
 ):
     table[0:ATOMS, :] = own[...]
-    fill_ghosts(table, ATOMS, low, high, left, right)
+    fill_ghosts(table, ATOMS, low, high, left, right, TABLE_ORDER)
 
     def forward(step, carry):
         rows = pl.ds(pl.multiple_of(step * EB, EB), EB)
@@ -463,7 +472,7 @@
     parts,
     messages,
 ):
-    fill_ghosts(returned, 0, low, high, left, right)
+    fill_ghosts(returned, 0, low, high, left, right, PACKET_ORDER)
     for first, last in wide_chunks():
         back = dot(placed[...], returned[:, first * C : last * C])
         for component in range(first, last):
@@ -596,7 +605,7 @@
 
 
 def finish_kernel(field_grad, low, high, left, right, placed, out, returned):
-    fill_ghosts(returned, 0, low, high, left, right)
+    fill_ghosts(returned, 0, low, high, left, right, PACKET_ORDER)
     for first, last in wide_chunks():
         back = dot(placed[...], returned[:, first * C : last * C])
         for component in range(first, last):
@@ -659,15 +668,15 @@
 
 
 def exchange(low_packet, middle_packet, high_packet):
+    up, down = ring("by")
+    low = lax.ppermute(high_packet, "by", up)
+    high = lax.ppermute(low_packet, "by", down)
     up, down = ring("bx")
-    low = lax.ppermute(high_packet, "bx", up)
-    high = lax.ppermute(low_packet, "bx", down)
-    up, down = ring("by")
     to_right, to_left = call(
         relay_kernel, [((48, WIDE), BF16)] * 2, [], 10**5, middle_packet, low, high
     )
-    left = lax.ppermute(to_right, "by", up)
-    right = lax.ppermute(to_left, "by", down)
+    left = lax.ppermute(to_right, "bx", up)
+    right = lax.ppermute(to_left, "bx", down)
     return (low, high, left, right), (to_right, to_left)
 
 

time: 162 us -> 165 us (1.019)
  starting transfers between devices: 45.4 us -> 57.1 us
  waiting for transfers between devices: 78.6 us -> 69.9 us
    ppermute x1, starting transfers between devices: 3.34 us -> 13.6 us  [reduce_halves(): lax.ppermute(lax.optimization_barrier((whole, after))[0], 'by', swap)]
    all_to_all x1, waiting for transfers between devices: 7.75 us -> 2.46 us  [reduce_halves(): lax.all_to_all(spread, axes, 0, 0, axis_index_groups=groups, tiled=True)]
    all_to_all x1, waiting for transfers between devices: 9.53 us -> 5.97 us  [reduce_halves(): lax.all_to_all(pair, axes, 0, 0, axis_index_groups=groups, tiled=True)]
    ppermute x1, starting transfers between devices: 0.52 us -> 3.85 us  [reduce_halves(): pair = (mine + lax.ppermute(other, 'by', swap)).reshape(count, -1, C)]
  transfers between devices with their start and end apart: 20 -> 20, of which waited for: 17 -> 18; matrix products, arithmetic and copies ran while one was open for 0% -> 0% of each run, Pallas kernels for 8% -> 8%
where the time goes in v4:
time: 165 us; the launch traced here: 164 us
  waiting for transfers between devices  69.9 us (42%)
  starting transfers between devices  57.1 us (35%)
  Pallas kernels  33.5 us (20%)
  local copies, waits for them, and re-layouts  1.94 us (1%)
    pallas_call x14, Pallas kernels, call(): pl.pallas_call(kernel, out_shape=shapes, in_specs=[scalar if x.shape == (...  33.5 us
    ppermute x4, waiting for transfers between devices, exchange(): left = lax.ppermute(to_right, 'bx', up)  20.1 us
    ppermute x4, waiting for transfers between devices, exchange(): right = lax.ppermute(to_left, 'bx', down)  20 us
    ppermute x4, starting transfers between devices, exchange(): right = lax.ppermute(to_left, 'bx', down)  15 us
    ppermute x1, starting transfers between devices, reduce_halves(): lax.ppermute(lax.optimization_barrier((whole, after))[0], 'by', swap)  13.6 us
    ppermute x4, waiting for transfers between devices, exchange(): low = lax.ppermute(high_packet, 'by', up)  10.4 us
    ppermute x4, waiting for transfers between devices, exchange(): high = lax.ppermute(low_packet, 'by', down)  8.33 us
    ppermute x4, starting transfers between devices, exchange(): low = lax.ppermute(high_packet, 'by', up)  6.16 us
  transfers between devices with their start and end apart: 20, of which 18 were waited for; matrix products, arithmetic and copies ran while one was open for 0% of the time, Pallas kernels for 8%

profile of v4, /device:TPU:1, one launch (start us, length us, event | category | flops | bytes accessed | tf_op | source)
XLA Modules:
  0.0 164.2 jit_solution(2974994223507593781)
XLA Ops:
  0.6 0.0 copy-start.14
  0.7 0.0 copy-start.13
  0.7 0.0 copy-start.7
  0.7 0.0 copy-start.6
  0.7 0.0 copy-start.11
  0.7 0.0 copy-start.10
  0.7 0.0 copy-start.8
  0.7 0.0 copy-start.9
  0.7 0.7 copy.33
  1.5 1.1 copy-done
  2.6 0.5 shard_map.223
  3.2 3.1 %collective-permute-start = (bf16[48,3200]{1,0:T(8,128)(2,1)S(1)}, bf16[48,3200]{1,0:T(8,128)(2,1)S(1)}, u32[]{:S(2)}, u32[]{:S(2)}) collective-permute-start(bf16[48,3200]{1,0:T(8,128)(2,1)S(1)} %get-tuple-element.69), channel_id=1, source_target_pairs={{0,1},{1,2},{2,3},{3,4},{4,5},{5,6},{6,7},{7,8},{8,9},{9,10},{10,1... | collective-permute-start | bytes 921608 | tf_op jit(solution)/shard_map/ppermute | solution.py:672
  6.2 0.0 collective-permute-start.1
  6.2 3.8 %collective-permute-done.low = bf16[48,3200]{1,0:T(8,128)(2,1)S(1)} collective-permute-done((bf16[48,3200]{1,0:T(8,128)(2,1)S(1)}, bf16[48,3200]{1,0:T(8,128)(2,1)S(1)}, u32[]{:S(2)}, u32[]{:S(2)}) %collective-permute-start) | collective-permute-done | bytes 307232 | tf_op jit(solution)/shard_map/ppermute | solution.py:672
  10.0 2.8 %collective-permute-done.1.high = bf16[48,3200]{1,0:T(8,128)(2,1)S(1)} collective-permute-done((bf16[48,3200]{1,0:T(8,128)(2,1)S(1)}, bf16[48,3200]{1,0:T(8,128)(2,1)S(1)}, u32[]{:S(2)}, u32[]{:S(2)}) %collective-permute-start.1) | collective-permute-done | bytes 307232 | tf_op jit(solution)/shard_map/ppermute | solution.py:673
  12.9 3.0 %collective-permute-start.2 = (bf16[48,3200]{1,0:T(8,128)(2,1)S(1)}, bf16[48,3200]{1,0:T(8,128)(2,1)S(1)}, u32[]{:S(2)}, u32[]{:S(2)}) collective-permute-start(bf16[48,3200]{1,0:T(8,128)(2,1)S(1)} %get-tuple-element.72), channel_id=1, source_target_pairs={{0,16},{16,32},{32,48},{48,64},{64,80},{80,96},{96,112},{112,0},{1... | collective-permute-start | bytes 921608 | tf_op jit(solution)/shard_map/ppermute | solution.py:678
  15.9 2.3 %collective-permute-start.3 = (bf16[48,3200]{1,0:T(8,128)(2,1)S(1)}, bf16[48,3200]{1,0:T(8,128)(2,1)S(1)}, u32[]{:S(2)}, u32[]{:S(2)}) collective-permute-start(bf16[48,3200]{1,0:T(8,128)(2,1)S(1)} %get-tuple-element.73), channel_id=1, source_target_pairs={{16,0},{32,16},{48,32},{64,48},{80,64},{96,80},{112,96},{0,112},{1... | collective-permute-start | bytes 921608 | tf_op jit(solution)/shard_map/ppermute | solution.py:679
  18.1 0.0 copy-done.14
  18.2 0.0 copy-start.2
  18.3 1.7 %shard_map.225 = (f32[1024,128]{1,0:T(8,128)S(1)}, f32[24,1024]{1,0:T(8,128)S(1)}, f32[1024,64]{1,0:T(8,128)S(1)}, bf16[1024,192]{1,0:T(8,128)(2,1)S(1)}, bf16[1...) custom-call(f32[3,1024]{1,0:T(4,128)S(1)} %bitcast.32, ...), custom_call_target="tpu_custom_call" | custom-call | flops 1000000000 | bytes 3774976 | tf_op jit(solution)/shard_map/pallas_call | solution.py:640
  20.0 8.4 %collective-permute-done.2.left = bf16[48,3200]{1,0:T(8,128)(2,1)S(1)} collective-permute-done((bf16[48,3200]{1,0:T(8,128)(2,1)S(1)}, bf16[48,3200]{1,0:T(8,128)(2,1)S(1)}, u32[]{:S(2)}, u32[]{:S(2)}) %collective-permute-start.2) | collective-permute-done | bytes 307232 | tf_op jit(solution)/shard_map/ppermute | solution.py:678
  28.4 3.9 %collective-permute-done.3.right = bf16[48,3200]{1,0:T(8,128)(2,1)S(1)} collective-permute-done((bf16[48,3200]{1,0:T(8,128)(2,1)S(1)}, bf16[48,3200]{1,0:T(8,128)(2,1)S(1)}, u32[]{:S(2)}, u32[]{:S(2)}) %collective-permute-start.3) | collective-permute-done | bytes 307232 | tf_op jit(solution)/shard_map/ppermute | solution.py:679
  32.4 6.0 %shard_map.226 = (bf16[128,3200]{1,0:T(8,128)(2,1)S(1)}, bf16[3200,128]{1,0:T(8,128)(2,1)S(1)}, f32[3200,128]{1,0:T(8,128)S(1)}, bf16[256,3200]{1,0:T(8,128)(2,1...) custom-call(bf16[128,3200]{1,0:T(8,128)(2,1)S(1)} %get-tuple-element.68.own, ...), custom_call_target="tpu_custom_call" | custom-call | flops 4000000000 | bytes 9555968 | tf_op jit(solution)/shard_map/pallas_call | solution.py:640
  38.4 0.6 collective-permute-start.4
  39.0 0.0 collective-permute-start.5
  39.0 3.8 %collective-permute-done.4.low = bf16[48,3200]{1,0:T(8,128)(2,1)S(1)} collective-permute-done((bf16[48,3200]{1,0:T(8,128)(2,1)S(1)}, bf16[48,3200]{1,0:T(8,128)(2,1)S(1)}, u32[]{:S(2)}, u32[]{:S(2)}) %collective-permute-start.4) | collective-permute-done | bytes 307232 | tf_op jit(solution)/shard_map/ppermute | solution.py:672
  42.8 2.8 %collective-permute-done.5.high = bf16[48,3200]{1,0:T(8,128)(2,1)S(1)} collective-permute-done((bf16[48,3200]{1,0:T(8,128)(2,1)S(1)}, bf16[48,3200]{1,0:T(8,128)(2,1)S(1)}, u32[]{:S(2)}, u32[]{:S(2)}) %collective-permute-start.5) | collective-permute-done | bytes 307232 | tf_op jit(solution)/shard_map/ppermute | solution.py:673
  45.6 0.1 collective-permute-start.6
  45.7 5.1 %collective-permute-start.7 = (bf16[48,3200]{1,0:T(8,128)(2,1)S(1)}, bf16[48,3200]{1,0:T(8,128)(2,1)S(1)}, u32[]{:S(2)}, u32[]{:S(2)}) collective-permute-start(bf16[48,3200]{1,0:T(8,128)(2,1)S(1)} %get-tuple-element.83), channel_id=1, source_target_pairs={{16,0},{32,16},{48,32},{64,48},{80,64},{96,80},{112,96},{0,112},{1... | collective-permute-start | bytes 921608 | tf_op jit(solution)/shard_map/ppermute | solution.py:679
  50.8 6.7 %collective-permute-done.6.left = bf16[48,3200]{1,0:T(8,128)(2,1)S(1)} collective-permute-done((bf16[48,3200]{1,0:T(8,128)(2,1)S(1)}, bf16[48,3200]{1,0:T(8,128)(2,1)S(1)}, u32[]{:S(2)}, u32[]{:S(2)}) %collective-permute-start.6) | collective-permute-done | bytes 307232 | tf_op jit(solution)/shard_map/ppermute | solution.py:678
  57.5 3.9 %collective-permute-done.7.right = bf16[48,3200]{1,0:T(8,128)(2,1)S(1)} collective-permute-done((bf16[48,3200]{1,0:T(8,128)(2,1)S(1)}, bf16[48,3200]{1,0:T(8,128)(2,1)S(1)}, u32[]{:S(2)}, u32[]{:S(2)}) %collective-permute-start.7) | collective-permute-done | bytes 307232 | tf_op jit(solution)/shard_map/ppermute | solution.py:679
  61.4 5.2 %shard_map.228 = (f32[3200,128]{1,0:T(8,128)S(1)}, bf16[48,3200]{1,0:T(8,128)(2,1)S(1)}, bf16[32,3200]{1,0:T(8,128)(2,1)S(1)}, bf16[48,3200]{1,0:T(8,128)(2,1)S(...) custom-call(bf16[128,3200]{1,0:T(8,128)(2,1)S(1)} %get-tuple-element.78.own, ...), custom_call_target="tpu_custom_call" | custom-call | flops 4000000000 | bytes 6072832 | tf_op jit(solution)/shard_map/pallas_call | solution.py:640
  66.5 1.5 collective-permute-start.8
  68.1 1.0 collective-permute-start.9
  69.1 2.8 %collective-permute-done.8.low = bf16[48,3200]{1,0:T(8,128)(2,1)S(1)} collective-permute-done((bf16[48,3200]{1,0:T(8,128)(2,1)S(1)}, bf16[48,3200]{1,0:T(8,128)(2,1)S(1)}, u32[]{:S(2)}, u32[]{:S(2)}) %collective-permute-start.8) | collective-permute-done | bytes 307232 | tf_op jit(solution)/shard_map/ppermute | solution.py:672
  71.9 2.8 %collective-permute-done.9.high = bf16[48,3200]{1,0:T(8,128)(2,1)S(1)} collective-permute-done((bf16[48,3200]{1,0:T(8,128)(2,1)S(1)}, bf16[48,3200]{1,0:T(8,128)(2,1)S(1)}, u32[]{:S(2)}, u32[]{:S(2)}) %collective-permute-start.9) | collective-permute-done | bytes 307232 | tf_op jit(solution)/shard_map/ppermute | solution.py:673
  74.7 0.1 collective-permute-start.10
  74.8 5.1 %collective-permute-start.11 = (bf16[48,3200]{1,0:T(8,128)(2,1)S(1)}, bf16[48,3200]{1,0:T(8,128)(2,1)S(1)}, u32[]{:S(2)}, u32[]{:S(2)}) collective-permute-start(bf16[48,3200]{1,0:T(8,128)(2,1)S(1)} %get-tuple-element.93), channel_id=1, source_target_pairs={{16,0},{32,16},{48,32},{64,48},{80,64},{96,80},{112,96},{0,112},{1... | collective-permute-start | bytes 921608 | tf_op jit(solution)/shard_map/ppermute | solution.py:679
  79.9 0.8 shard_map.231.probe_grads
  80.7 3.5 %collective-permute-done.10.left = bf16[48,3200]{1,0:T(8,128)(2,1)S(1)} collective-permute-done((bf16[48,3200]{1,0:T(8,128)(2,1)S(1)}, bf16[48,3200]{1,0:T(8,128)(2,1)S(1)}, u32[]{:S(2)}, u32[]{:S(2)}) %collective-permute-start.10) | collective-permute-done | bytes 307232 | tf_op jit(solution)/shard_map/ppermute | solution.py:678
  84.2 8.4 %collective-permute-done.11.right = bf16[48,3200]{1,0:T(8,128)(2,1)S(1)} collective-permute-done((bf16[48,3200]{1,0:T(8,128)(2,1)S(1)}, bf16[48,3200]{1,0:T(8,128)(2,1)S(1)}, u32[]{:S(2)}, u32[]{:S(2)}) %collective-permute-start.11) | collective-permute-done | bytes 307232 | tf_op jit(solution)/shard_map/ppermute | solution.py:679
  92.6 7.4 %shard_map.230 = (f32[3200,128]{1,0:T(8,128)S(1)}, bf16[128,3200]{1,0:T(8,128)(2,1)S(1)}, bf16[3200,128]{1,0:T(8,128)(2,1)S(1)}, bf16[48,3200]{1,0:T(8,128)(2,1)...) custom-call(f32[3200,128]{1,0:T(8,128)S(1)} %get-tuple-element.88.grad_own, ...), custom_call_target="tpu_custom_call" | custom-call | flops 6000000000 | bytes 10375168 | tf_op jit(solution)/shard_map/pallas_call | solution.py:640
  100.0 0.9 collective-permute-start.12
  100.9 0.8 collective-permute-start.13
  101.7 7.4 %shard_map.232 = (f32[1024,128]{1,0:T(8,128)S(1)}, f32[1024,128]{1,0:T(8,128)S(1)}) custom-call(s32[1]{0:T(128)} %bitcast.core, bf16[128,3200]{1,0:T(8,128)(2,1)S(1)} %get-tuple-element.96.d_gathered, bf16[3200,128]{1,0:T(8,128)(2,1)S(1)} %get-tuple-element.97.d_mixed, bf16[256,3200]{1,0:T(8,128)(2,1)S(1)} %get-tuple-element.98.table, ...), custom_call_target="tpu_custom_call" | custom-call | flops 6000000000 | bytes 7045124 | tf_op jit(solution)/shard_map/pallas_call | solution.py:640
  109.2 0.0 collective-permute-done.12.low
  109.2 0.0 collective-permute-done.13.high
  109.2 3.9 %collective-permute-start.14 = (f32[1024,128]{1,0:T(8,128)S(1)}, f32[1024,128]{1,0:T(8,128)S(1)}, u32[]{:S(2)}, u32[]{:S(2)}) collective-permute-start(f32[1024,128]{1,0:T(8,128)S(1)} %get-tuple-element.113), channel_id=1, source_target_pairs={{0,1},{1,0},{2,3},{3,2},{4,5},{5,4},{6,7},{7,6},{8,9},{9,8},{10,11... | collective-permute-start | bytes 1572872 | tf_op jit(solution)/shard_map/ppermute | solution.py:689
  113.0 1.5 collective-permute-done.14
  114.6 0.9 add.12
  115.4 5.5 %all-to-all-start = ((f32[64,16,128]{2,1,0:T(8,128)}), f32[64,16,128]{2,1,0:T(8,128)S(1)}, u32[]{:S(2)}, u32[]{:S(2)}) async-start(f32[64,16,128]{2,1,0:T(8,128)} %bitcast.43), calls=%async_computation | async-start | bytes 1048576 | tf_op jit(solution)/shard_map/all_to_all | solution.py:690
  120.9 0.9 shard_map.234
  121.8 2.5 %collective-permute-start.15 = (bf16[48,3200]{1,0:T(8,128)(2,1)}, bf16[48,3200]{1,0:T(8,128)(2,1)S(1)}, u32[]{:S(2)}, u32[]{:S(2)}) collective-permute-start(bf16[48,3200]{1,0:T(8,128)(2,1)} %get-tuple-element.116), channel_id=1, source_target_pairs={{0,16},{16,32},{32,48},{48,64},{64,80},{80,96},{96,112},{112,0},{1... | collective-permute-start | bytes 921608 | tf_op jit(solution)/shard_map/ppermute | solution.py:678
  124.3 2.6 %collective-permute-start.16 = (bf16[48,3200]{1,0:T(8,128)(2,1)}, bf16[48,3200]{1,0:T(8,128)(2,1)S(1)}, u32[]{:S(2)}, u32[]{:S(2)}) collective-permute-start(bf16[48,3200]{1,0:T(8,128)(2,1)} %get-tuple-element.117), channel_id=1, source_target_pairs={{16,0},{32,16},{48,32},{64,48},{80,64},{96,80},{112,96},{0,112},{1... | collective-permute-start | bytes 921608 | tf_op jit(solution)/shard_map/ppermute | solution.py:679
  126.9 6.0 %all-to-all-done.pieces = f32[64,16,128]{2,1,0:T(8,128)S(1)} async-done(((f32[64,16,128]{2,1,0:T(8,128)}), f32[64,16,128]{2,1,0:T(8,128)S(1)}, u32[]{:S(2)}, u32[]{:S(2)}) %all-to-all-start) | async-done | bytes 524320 | tf_op jit(solution)/shard_map/all_to_all | solution.py:690
  132.8 0.8 shard_map.233
  133.7 5.5 %all-to-all-start.1 = ((bf16[64,16,128]{2,1,0:T(8,128)(2,1)}), bf16[64,16,128]{2,1,0:T(8,128)(2,1)S(1)}, u32[]{:S(2)}, u32[]{:S(2)}) async-start(bf16[64,16,128]{2,1,0:T(8,128)(2,1)} %shard_map.233), calls=%async_computation.1 | async-start | bytes 524288 | tf_op jit(solution)/shard_map/all_to_all | solution.py:692
  139.2 1.5 collective-permute-done.15.left
  140.7 3.8 %collective-permute-done.16.right = bf16[48,3200]{1,0:T(8,128)(2,1)S(1)} collective-permute-done((bf16[48,3200]{1,0:T(8,128)(2,1)}, bf16[48,3200]{1,0:T(8,128)(2,1)S(1)}, u32[]{:S(2)}, u32[]{:S(2)}) %collective-permute-start.16) | collective-permute-done | bytes 307232 | tf_op jit(solution)/shard_map/ppermute | solution.py:679
  144.4 1.5 shard_map.235
  146.0 2.5 %all-to-all-done.1 = bf16[64,16,128]{2,1,0:T(8,128)(2,1)S(1)} async-done(((bf16[64,16,128]{2,1,0:T(8,128)(2,1)}), bf16[64,16,128]{2,1,0:T(8,128)(2,1)S(1)}, u32[]{:S(2)}, u32[]{:S(2)}) %all-to-all-start.1) | async-done | bytes 262176 | tf_op jit(solution)/shard_map/all_to_all | solution.py:692
  148.5 13.6 %collective-permute-start.17 = (bf16[1024,128]{1,0:T(8,128)(2,1)S(1)}, bf16[1024,128]{1,0:T(8,128)(2,1)S(1)}, u32[]{:S(2)}, u32[]{:S(2)}) collective-permute-start(bf16[1024,128]{1,0:T(8,128)(2,1)S(1)} %bitcast.28), channel_id=1, source_target_pairs={{0,1},{1,0},{2,3},{3,2},{4,5},{5,4},{6,7},{7,6},{8,9},{9,8},{10,11... | collective-permute-start | bytes 786440 | tf_op jit(solution)/shard_map/ppermute | solution.py:694
  162.1 1.2 collective-permute-done.17.other
  163.2 1.0 shard_map.236
  (24 shorter events, 0.2 us)
Async XLA Ops:
  0.6 17.5 %copy-start.14 = (f32[1,1,3,512]{3,1,2,0:T(1,128)S(1)}, f32[1,1,3,512]{3,1,2,0:T(1,128)}, u32[]{:S(2)}) copy-start(f32[1,1,3,512]{3,1,2,0:T(1,128)} %param.21) | copy-start | bytes 18436
  0.7 17.5 %copy-start.13 = (f32[1,1,3,1024]{3,1,2,0:T(1,128)S(1)}, f32[1,1,3,1024]{3,1,2,0:T(1,128)}, u32[]{:S(2)}) copy-start(f32[1,1,3,1024]{3,1,2,0:T(1,128)} %param.18) | copy-start | bytes 36868
  0.7 17.5 %copy-start.7 = (f32[20,64]{1,0:T(8,128)S(1)}, f32[20,64]{1,0:T(8,128)}, u32[]{:S(2)}) copy-start(f32[20,64]{1,0:T(8,128)} %pfirst.1) | copy-start | bytes 15364
  0.7 17.5 %copy-start.6 = (f32[20,64]{1,0:T(8,128)S(1)}, f32[20,64]{1,0:T(8,128)}, u32[]{:S(2)}) copy-start(f32[20,64]{1,0:T(8,128)} %first.1) | copy-start | bytes 15364
  0.7 17.5 %copy-start.11 = (s32[1,1,128]{2,1,0:T(1,128)S(1)}, s32[1,1,128]{2,1,0:T(1,128)}, u32[]{:S(2)}) copy-start(s32[1,1,128]{2,1,0:T(1,128)} %param.24) | copy-start | bytes 1540
  0.7 17.5 %copy-start.10 = (s32[1,1,512]{2,1,0:T(1,128)S(1)}, s32[1,1,512]{2,1,0:T(1,128)}, u32[]{:S(2)}) copy-start(s32[1,1,512]{2,1,0:T(1,128)} %param.22) | copy-start | bytes 6148
  0.7 17.5 %copy-start.8 = (s32[1,1,1024]{2,1,0:T(1,128)S(1)}, s32[1,1,1024]{2,1,0:T(1,128)}, u32[]{:S(2)}) copy-start(s32[1,1,1024]{2,1,0:T(1,128)} %param.20) | copy-start | bytes 12292
  0.7 17.5 %copy-start.9 = (s32[1,1,1024]{2,1,0:T(1,128)S(1)}, s32[1,1,1024]{2,1,0:T(1,128)}, u32[]{:S(2)}) copy-start(s32[1,1,1024]{2,1,0:T(1,128)} %param.19) | copy-start | bytes 12292
  1.5 1.1 copy-start
  2.6 15.6 %copy-start.1 = (f32[64,1280]{1,0:T(8,128)S(1)}, f32[64,1280]{1,0:T(8,128)}, u32[]{:S(2)}) copy-start(f32[64,1280]{1,0:T(8,128)} %second.1) | copy-start | bytes 983044
  2.6 15.6 %copy-start.3 = (f32[64,640]{1,0:T(8,128)S(1)}, f32[64,640]{1,0:T(8,128)}, u32[]{:S(2)}) copy-start(f32[64,640]{1,0:T(8,128)} %psecond.1) | copy-start | bytes 491524
  2.6 15.6 %copy-start.4 = (f32[1,1,32768]{2,1,0:T(1,128)S(1)}, f32[1,1,32768]{2,1,0:T(1,128)}, u32[]{:S(2)}) copy-start(f32[1,1,32768]{2,1,0:T(1,128)} %param.23) | copy-start | bytes 393220
  3.2 6.9 %collective-permute-start = (bf16[48,3200]{1,0:T(8,128)(2,1)S(1)}, bf16[48,3200]{1,0:T(8,128)(2,1)S(1)}, u32[]{:S(2)}, u32[]{:S(2)}) collective-permute-start(bf16[48,3200]{1,0:T(8,128)(2,1)S(1)} %get-tuple-element.69), channel_id=1, source_target_pairs={{0,1},{1,2},{2,3},{3,4},{4,5},{5,6},{6,7},{7,8},{8,9},{9,10},{10,1... | collective-permute-start | bytes 921608 | tf_op jit(solution)/shard_map/ppermute | solution.py:672
  6.2 6.6 %collective-permute-start.1 = (bf16[48,3200]{1,0:T(8,128)(2,1)S(1)}, bf16[48,3200]{1,0:T(8,128)(2,1)S(1)}, u32[]{:S(2)}, u32[]{:S(2)}) collective-permute-start(bf16[48,3200]{1,0:T(8,128)(2,1)S(1)} %get-tuple-element.70), channel_id=1, source_target_pairs={{1,0},{2,1},{3,2},{4,3},{5,4},{6,5},{7,6},{8,7},{9,8},{10,9},{11,1... | collective-permute-start | bytes 921608 | tf_op jit(solution)/shard_map/ppermute | solution.py:673
  12.9 15.5 %collective-permute-start.2 = (bf16[48,3200]{1,0:T(8,128)(2,1)S(1)}, bf16[48,3200]{1,0:T(8,128)(2,1)S(1)}, u32[]{:S(2)}, u32[]{:S(2)}) collective-permute-start(bf16[48,3200]{1,0:T(8,128)(2,1)S(1)} %get-tuple-element.72), channel_id=1, source_target_pairs={{0,16},{16,32},{32,48},{48,64},{64,80},{80,96},{96,112},{112,0},{1... | collective-permute-start | bytes 921608 | tf_op jit(solution)/shard_map/ppermute | solution.py:678
  15.9 16.5 %collective-permute-start.3 = (bf16[48,3200]{1,0:T(8,128)(2,1)S(1)}, bf16[48,3200]{1,0:T(8,128)(2,1)S(1)}, u32[]{:S(2)}, u32[]{:S(2)}) collective-permute-start(bf16[48,3200]{1,0:T(8,128)(2,1)S(1)} %get-tuple-element.73), channel_id=1, source_target_pairs={{16,0},{32,16},{48,32},{64,48},{80,64},{96,80},{112,96},{0,112},{1... | collective-permute-start | bytes 921608 | tf_op jit(solution)/shard_map/ppermute | solution.py:679
  18.2 14.1 %copy-start.2 = (f32[5,128,128]{2,1,0:T(8,128)S(1)}, f32[5,128,128]{2,1,0:T(8,128)}, u32[]{:S(2)}) copy-start(f32[5,128,128]{2,1,0:T(8,128)} %mixing.3) | copy-start | bytes 983044
  32.4 29.0 %copy-start.5 = (f32[128,128]{1,0:T(8,128)S(1)}, f32[128,128]{1,0:T(8,128)}, u32[]{:S(2)}) copy-start(f32[128,128]{1,0:T(8,128)} %first_readout.1) | copy-start | bytes 196612
  32.4 29.0 %copy-start.12 = (f32[128]{0:T(128)S(1)}, f32[128]{0:T(128)}, u32[]{:S(2)}) copy-start(f32[128]{0:T(128)} %param.31) | copy-start | bytes 1540
  38.4 4.4 %collective-permute-start.4 = (bf16[48,3200]{1,0:T(8,128)(2,1)S(1)}, bf16[48,3200]{1,0:T(8,128)(2,1)S(1)}, u32[]{:S(2)}, u32[]{:S(2)}) collective-permute-start(bf16[48,3200]{1,0:T(8,128)(2,1)S(1)} %get-tuple-element.79), channel_id=1, source_target_pairs={{0,1},{1,2},{2,3},{3,4},{4,5},{5,6},{6,7},{7,8},{8,9},{9,10},{10,1... | collective-permute-start | bytes 921608 | tf_op jit(solution)/shard_map/ppermute | solution.py:672
  39.0 6.6 %collective-permute-start.5 = (bf16[48,3200]{1,0:T(8,128)(2,1)S(1)}, bf16[48,3200]{1,0:T(8,128)(2,1)S(1)}, u32[]{:S(2)}, u32[]{:S(2)}) collective-permute-start(bf16[48,3200]{1,0:T(8,128)(2,1)S(1)} %get-tuple-element.80), channel_id=1, source_target_pairs={{1,0},{2,1},{3,2},{4,3},{5,4},{6,5},{7,6},{8,7},{9,8},{10,9},{11,1... | collective-permute-start | bytes 921608 | tf_op jit(solution)/shard_map/ppermute | solution.py:673
  45.6 11.8 %collective-permute-start.6 = (bf16[48,3200]{1,0:T(8,128)(2,1)S(1)}, bf16[48,3200]{1,0:T(8,128)(2,1)S(1)}, u32[]{:S(2)}, u32[]{:S(2)}) collective-permute-start(bf16[48,3200]{1,0:T(8,128)(2,1)S(1)} %get-tuple-element.82), channel_id=1, source_target_pairs={{0,16},{16,32},{32,48},{48,64},{64,80},{80,96},{96,112},{112,0},{1... | collective-permute-start | bytes 921608 | tf_op jit(solution)/shard_map/ppermute | solution.py:678
  45.7 15.6 %collective-permute-start.7 = (bf16[48,3200]{1,0:T(8,128)(2,1)S(1)}, bf16[48,3200]{1,0:T(8,128)(2,1)S(1)}, u32[]{:S(2)}, u32[]{:S(2)}) collective-permute-start(bf16[48,3200]{1,0:T(8,128)(2,1)S(1)} %get-tuple-element.83), channel_id=1, source_target_pairs={{16,0},{32,16},{48,32},{64,48},{80,64},{96,80},{112,96},{0,112},{1... | collective-permute-start | bytes 921608 | tf_op jit(solution)/shard_map/ppermute | solution.py:679
  66.5 5.3 %collective-permute-start.8 = (bf16[48,3200]{1,0:T(8,128)(2,1)S(1)}, bf16[48,3200]{1,0:T(8,128)(2,1)S(1)}, u32[]{:S(2)}, u32[]{:S(2)}) collective-permute-start(bf16[48,3200]{1,0:T(8,128)(2,1)S(1)} %get-tuple-element.89), channel_id=1, source_target_pairs={{0,1},{1,2},{2,3},{3,4},{4,5},{5,6},{6,7},{7,8},{8,9},{9,10},{10,1... | collective-permute-start | bytes 921608 | tf_op jit(solution)/shard_map/ppermute | solution.py:672
  68.1 6.6 %collective-permute-start.9 = (bf16[48,3200]{1,0:T(8,128)(2,1)S(1)}, bf16[48,3200]{1,0:T(8,128)(2,1)S(1)}, u32[]{:S(2)}, u32[]{:S(2)}) collective-permute-start(bf16[48,3200]{1,0:T(8,128)(2,1)S(1)} %get-tuple-element.90), channel_id=1, source_target_pairs={{1,0},{2,1},{3,2},{4,3},{5,4},{6,5},{7,6},{8,7},{9,8},{10,9},{11,1... | collective-permute-start | bytes 921608 | tf_op jit(solution)/shard_map/ppermute | solution.py:673
  74.7 9.5 %collective-permute-start.10 = (bf16[48,3200]{1,0:T(8,128)(2,1)S(1)}, bf16[48,3200]{1,0:T(8,128)(2,1)S(1)}, u32[]{:S(2)}, u32[]{:S(2)}) collective-permute-start(bf16[48,3200]{1,0:T(8,128)(2,1)S(1)} %get-tuple-element.92), channel_id=1, source_target_pairs={{0,16},{16,32},{32,48},{48,64},{64,80},{80,96},{96,112},{112,0},{1... | collective-permute-start | bytes 921608 | tf_op jit(solution)/shard_map/ppermute | solution.py:678
  74.8 17.8 %collective-permute-start.11 = (bf16[48,3200]{1,0:T(8,128)(2,1)S(1)}, bf16[48,3200]{1,0:T(8,128)(2,1)S(1)}, u32[]{:S(2)}, u32[]{:S(2)}) collective-permute-start(bf16[48,3200]{1,0:T(8,128)(2,1)S(1)} %get-tuple-element.93), channel_id=1, source_target_pairs={{16,0},{32,16},{48,32},{64,48},{80,64},{96,80},{112,96},{0,112},{1... | collective-permute-start | bytes 921608 | tf_op jit(solution)/shard_map/ppermute | solution.py:679
  100.0 9.1 %collective-permute-start.12 = (bf16[48,3200]{1,0:T(8,128)(2,1)S(1)}, bf16[48,3200]{1,0:T(8,128)(2,1)S(1)}, u32[]{:S(2)}, u32[]{:S(2)}) collective-permute-start(bf16[48,3200]{1,0:T(8,128)(2,1)S(1)} %get-tuple-element.110), channel_id=1, source_target_pairs={{0,1},{1,2},{2,3},{3,4},{4,5},{5,6},{6,7},{7,8},{8,9},{9,10},{10,1... | collective-permute-start | bytes 921608 | tf_op jit(solution)/shard_map/ppermute | solution.py:672
  100.9 8.3 %collective-permute-start.13 = (bf16[48,3200]{1,0:T(8,128)(2,1)S(1)}, bf16[48,3200]{1,0:T(8,128)(2,1)S(1)}, u32[]{:S(2)}, u32[]{:S(2)}) collective-permute-start(bf16[48,3200]{1,0:T(8,128)(2,1)S(1)} %get-tuple-element.111), channel_id=1, source_target_pairs={{1,0},{2,1},{3,2},{4,3},{5,4},{6,5},{7,6},{8,7},{9,8},{10,9},{11,1... | collective-permute-start | bytes 921608 | tf_op jit(solution)/shard_map/ppermute | solution.py:673
  109.2 5.4 %collective-permute-start.14 = (f32[1024,128]{1,0:T(8,128)S(1)}, f32[1024,128]{1,0:T(8,128)S(1)}, u32[]{:S(2)}, u32[]{:S(2)}) collective-permute-start(f32[1024,128]{1,0:T(8,128)S(1)} %get-tuple-element.113), channel_id=1, source_target_pairs={{0,1},{1,0},{2,3},{3,2},{4,5},{5,4},{6,7},{7,6},{8,9},{9,8},{10,11... | collective-permute-start | bytes 1572872 | tf_op jit(solution)/shard_map/ppermute | solution.py:689
  115.4 17.4 %all-to-all-start = ((f32[64,16,128]{2,1,0:T(8,128)}), f32[64,16,128]{2,1,0:T(8,128)S(1)}, u32[]{:S(2)}, u32[]{:S(2)}) async-start(f32[64,16,128]{2,1,0:T(8,128)} %bitcast.43), calls=%async_computation | async-start | bytes 1048576 | tf_op jit(solution)/shard_map/all_to_all | solution.py:690
  121.8 18.9 %collective-permute-start.15 = (bf16[48,3200]{1,0:T(8,128)(2,1)}, bf16[48,3200]{1,0:T(8,128)(2,1)S(1)}, u32[]{:S(2)}, u32[]{:S(2)}) collective-permute-start(bf16[48,3200]{1,0:T(8,128)(2,1)} %get-tuple-element.116), channel_id=1, source_target_pairs={{0,16},{16,32},{32,48},{48,64},{64,80},{80,96},{96,112},{112,0},{1... | collective-permute-start | bytes 921608 | tf_op jit(solution)/shard_map/ppermute | solution.py:678
  124.3 20.1 %collective-permute-start.16 = (bf16[48,3200]{1,0:T(8,128)(2,1)}, bf16[48,3200]{1,0:T(8,128)(2,1)S(1)}, u32[]{:S(2)}, u32[]{:S(2)}) collective-permute-start(bf16[48,3200]{1,0:T(8,128)(2,1)} %get-tuple-element.117), channel_id=1, source_target_pairs={{16,0},{32,16},{48,32},{64,48},{80,64},{96,80},{112,96},{0,112},{1... | collective-permute-start | bytes 921608 | tf_op jit(solution)/shard_map/ppermute | solution.py:679
  133.7 14.8 %all-to-all-start.1 = ((bf16[64,16,128]{2,1,0:T(8,128)(2,1)}), bf16[64,16,128]{2,1,0:T(8,128)(2,1)S(1)}, u32[]{:S(2)}, u32[]{:S(2)}) async-start(bf16[64,16,128]{2,1,0:T(8,128)(2,1)} %shard_map.233), calls=%async_computation.1 | async-start | bytes 524288 | tf_op jit(solution)/shard_map/all_to_all | solution.py:692
  148.5 14.8 %collective-permute-start.17 = (bf16[1024,128]{1,0:T(8,128)(2,1)S(1)}, bf16[1024,128]{1,0:T(8,128)(2,1)S(1)}, u32[]{:S(2)}, u32[]{:S(2)}) collective-permute-start(bf16[1024,128]{1,0:T(8,128)(2,1)S(1)} %bitcast.28), channel_id=1, source_target_pairs={{0,1},{1,0},{2,3},{3,2},{4,5},{5,4},{6,7},{7,6},{8,9},{9,8},{10,11... | collective-permute-start | bytes 786440 | tf_op jit(solution)/shard_map/ppermute | solution.py:694

commit v5 on v3

--- a/solution.py
+++ b/solution.py
@@ -584,13 +584,16 @@
 
 def share_kernel(place, pieces, out):
     count = pieces.shape[0]
-    total = pieces[0]
+    total = pieces[0].astype(F32)
     for at in range(1, count):
-        total = total + pieces[at]
+        total = total + pieces[at].astype(F32)
     row = lax.broadcasted_iota(jnp.int32, total.shape, 0)
-    rest = total - total.astype(BF16).astype(F32)
-    ours = (row >= LOSS_ROW % total.shape[0] + 4) & (row < LOSS_ROW % total.shape[0] + 8)
-    total = jnp.where(ours & (place[0] == 1), rest, total).astype(BF16)
+    first = LOSS_ROW % total.shape[0]
+    loss_rows = (row >= first) & (row < first + 8)
+    loss = 0.25 * jnp.sum(jnp.where(loss_rows, total, 0.0), axis=0, keepdims=True)
+    rest = loss - loss.astype(BF16).astype(F32)
+    value = jnp.where(row < first + 4, loss, rest)
+    total = jnp.where(loss_rows & (place[0] == 1), value, total).astype(BF16)
     for at in range(count):
         out[at] = total
 
@@ -671,13 +674,20 @@
     return (low, high, left, right), (to_right, to_left)
 
 
-def reduce_halves(mine, other, owner):
+def reduce_halves(mine, other, core, owner):
     n_x, n_y = lax.axis_size("bx"), lax.axis_size("by")
     count = n_x * n_y // 2
     axes = ("bx", "by")
     swap = [(i, i ^ 1) for i in range(n_y)]
     groups = [[2 * i + core for i in range(count)] for core in range(2)]
     pair = (mine + lax.ppermute(other, "by", swap)).reshape(count, -1, C)
+    rounded = lax.reduce_precision(pair, 8, 7)
+    side, place = divmod(LOSS_ROW, REDUCE_ROWS // 2)
+    chunk, row = divmod(place, pair.shape[1])
+    chunk_at = lax.broadcasted_iota(jnp.int32, pair.shape, 0)
+    row_at = lax.broadcasted_iota(jnp.int32, pair.shape, 1)
+    rest = (core[0] == side) & (chunk_at == chunk) & (row_at >= row + 4) & (row_at < row + 8)
+    pair = jnp.where(rest, pair - rounded, rounded).astype(BF16)
     pieces = lax.all_to_all(pair, axes, 0, 0, axis_index_groups=groups, tiled=True)
     (spread,) = call(share_kernel, [(pair.shape, BF16)], [], 10**6, owner, pieces)
     whole = lax.all_to_all(spread, axes, 0, 0, axis_index_groups=groups, tiled=True)
@@ -882,7 +892,7 @@
         placed,
     )
     mine, other, *_ = lax.optimization_barrier((mine, other, received[0], received[1]))
-    mine, swapped = reduce_halves(mine, other, owner)
+    mine, swapped = reduce_halves(mine, other, core, owner)
     other = swapped(feature_grad)
     loss, first, second, mixing_grad, pfirst, psecond, readout, vector = call(
         unpack_kernel,

time: 162 us -> 161 us (level)
  waiting for transfers between devices: 78.6 us -> 75.2 us
  Pallas kernels: 33.5 us -> 35.7 us
    all_to_all x1, waiting for transfers between devices: 9.53 us -> 6.97 us  [reduce_halves(): lax.all_to_all(pair, axes, 0, 0, axis_index_groups=groups, tiled=True)]
    pallas_call x14, Pallas kernels: 33.5 us -> 35.7 us  [call(): pl.pallas_call(kernel, out_shape=shapes, in_specs=[scalar if x.shape == (...]
  transfers between devices with their start and end apart: 20 -> 20, of which waited for: 17 -> 17; matrix products, arithmetic and copies ran while one was open for 0% -> 0% of each run, Pallas kernels for 8% -> 9%
where the time goes in v5:
time: 161 us
  waiting for transfers between devices  75.2 us (47%)
  starting transfers between devices  45.3 us (28%)
  Pallas kernels  35.7 us (22%)
  other arithmetic  2.03 us (1%)
  local copies, waits for them, and re-layouts  1.94 us (1%)
    pallas_call x14, Pallas kernels, call(): pl.pallas_call(kernel, out_shape=shapes, in_specs=[scalar if x.shape == (...  35.7 us
    ppermute x4, waiting for transfers between devices, exchange(): low = lax.ppermute(high_packet, 'bx', up)  24.1 us
    ppermute x4, waiting for transfers between devices, exchange(): high = lax.ppermute(low_packet, 'bx', down)  18 us
    ppermute x4, starting transfers between devices, exchange(): high = lax.ppermute(low_packet, 'bx', down)  16.8 us
    ppermute x4, waiting for transfers between devices, exchange(): right = lax.ppermute(to_left, 'by', down)  8.33 us
    all_to_all x1, waiting for transfers between devices, reduce_halves(): lax.all_to_all(spread, axes, 0, 0, axis_index_groups=groups, tiled=True)  7.74 us
    ppermute x4, waiting for transfers between devices, exchange(): left = lax.ppermute(to_right, 'by', up)  7.05 us
    all_to_all x1, waiting for transfers between devices, reduce_halves(): lax.all_to_all(pair, axes, 0, 0, axis_index_groups=groups, tiled=True)  6.97 us
  transfers between devices with their start and end apart: 20, of which 17 were waited for; matrix products, arithmetic and copies ran while one was open for 0% of the time, Pallas kernels for 9%

profile of v5, /device:TPU:1, one launch (start us, length us, event | category | flops | bytes accessed | tf_op | source)
XLA Modules:
  0.0 161.1 jit_solution(13160041022394063107)
XLA Ops:
  0.6 0.0 copy-start.14
  0.7 0.0 copy-start.13
  0.7 0.0 copy-start.7
  0.7 0.0 copy-start.6
  0.7 0.0 copy-start.11
  0.7 0.0 copy-start.10
  0.7 0.0 copy-start.8
  0.7 0.7 copy.33
  1.5 1.1 copy-done
  2.6 0.5 shard_map.223
  3.2 3.8 %collective-permute-start = (bf16[48,3200]{1,0:T(8,128)(2,1)S(1)}, bf16[48,3200]{1,0:T(8,128)(2,1)S(1)}, u32[]{:S(2)}, u32[]{:S(2)}) collective-permute-start(bf16[48,3200]{1,0:T(8,128)(2,1)S(1)} %get-tuple-element.69), channel_id=1, source_target_pairs={{0,16},{16,32},{32,48},{48,64},{64,80},{80,96},{96,112},{112,0},{1... | collective-permute-start | bytes 921608 | tf_op jit(solution)/shard_map/ppermute | solution.py:666
  7.0 2.3 %collective-permute-start.1 = (bf16[48,3200]{1,0:T(8,128)(2,1)S(1)}, bf16[48,3200]{1,0:T(8,128)(2,1)S(1)}, u32[]{:S(2)}, u32[]{:S(2)}) collective-permute-start(bf16[48,3200]{1,0:T(8,128)(2,1)S(1)} %get-tuple-element.70), channel_id=1, source_target_pairs={{16,0},{32,16},{48,32},{64,48},{80,64},{96,80},{112,96},{0,112},{1... | collective-permute-start | bytes 921608 | tf_op jit(solution)/shard_map/ppermute | solution.py:667
  9.2 10.2 %collective-permute-done.low = bf16[48,3200]{1,0:T(8,128)(2,1)S(1)} collective-permute-done((bf16[48,3200]{1,0:T(8,128)(2,1)S(1)}, bf16[48,3200]{1,0:T(8,128)(2,1)S(1)}, u32[]{:S(2)}, u32[]{:S(2)}) %collective-permute-start) | collective-permute-done | bytes 307232 | tf_op jit(solution)/shard_map/ppermute | solution.py:666
  19.5 4.0 %collective-permute-done.1.high = bf16[48,3200]{1,0:T(8,128)(2,1)S(1)} collective-permute-done((bf16[48,3200]{1,0:T(8,128)(2,1)S(1)}, bf16[48,3200]{1,0:T(8,128)(2,1)S(1)}, u32[]{:S(2)}, u32[]{:S(2)}) %collective-permute-start.1) | collective-permute-done | bytes 307232 | tf_op jit(solution)/shard_map/ppermute | solution.py:667
  23.5 2.1 %collective-permute-start.2 = (bf16[48,3200]{1,0:T(8,128)(2,1)S(1)}, bf16[48,3200]{1,0:T(8,128)(2,1)S(1)}, u32[]{:S(2)}, u32[]{:S(2)}) collective-permute-start(bf16[48,3200]{1,0:T(8,128)(2,1)S(1)} %get-tuple-element.72), channel_id=1, source_target_pairs={{0,1},{1,2},{2,3},{3,4},{4,5},{5,6},{6,7},{7,8},{8,9},{9,10},{10,1... | collective-permute-start | bytes 921608 | tf_op jit(solution)/shard_map/ppermute | solution.py:672
  25.6 0.0 collective-permute-start.3
  25.7 0.0 copy-start.2
  25.7 1.7 %shard_map.225 = (f32[1024,128]{1,0:T(8,128)S(1)}, f32[24,1024]{1,0:T(8,128)S(1)}, f32[1024,64]{1,0:T(8,128)S(1)}, bf16[1024,192]{1,0:T(8,128)(2,1)S(1)}, bf16[1...) custom-call(f32[3,1024]{1,0:T(4,128)S(1)} %bitcast.32, ...), custom_call_target="tpu_custom_call" | custom-call | flops 1000000000 | bytes 3774976 | tf_op jit(solution)/shard_map/pallas_call | solution.py:634
  27.5 1.9 %collective-permute-done.2.left = bf16[48,3200]{1,0:T(8,128)(2,1)S(1)} collective-permute-done((bf16[48,3200]{1,0:T(8,128)(2,1)S(1)}, bf16[48,3200]{1,0:T(8,128)(2,1)S(1)}, u32[]{:S(2)}, u32[]{:S(2)}) %collective-permute-start.2) | collective-permute-done | bytes 307232 | tf_op jit(solution)/shard_map/ppermute | solution.py:672
  29.4 2.8 %collective-permute-done.3.right = bf16[48,3200]{1,0:T(8,128)(2,1)S(1)} collective-permute-done((bf16[48,3200]{1,0:T(8,128)(2,1)S(1)}, bf16[48,3200]{1,0:T(8,128)(2,1)S(1)}, u32[]{:S(2)}, u32[]{:S(2)}) %collective-permute-start.3) | collective-permute-done | bytes 307232 | tf_op jit(solution)/shard_map/ppermute | solution.py:673
  32.2 6.5 %shard_map.226 = (bf16[128,3200]{1,0:T(8,128)(2,1)S(1)}, bf16[3200,128]{1,0:T(8,128)(2,1)S(1)}, f32[3200,128]{1,0:T(8,128)S(1)}, bf16[256,3200]{1,0:T(8,128)(2,1...) custom-call(bf16[128,3200]{1,0:T(8,128)(2,1)S(1)} %get-tuple-element.68.own, ...), custom_call_target="tpu_custom_call" | custom-call | flops 4000000000 | bytes 9555968 | tf_op jit(solution)/shard_map/pallas_call | solution.py:634
  38.7 0.7 collective-permute-start.4
  39.4 4.4 %collective-permute-start.5 = (bf16[48,3200]{1,0:T(8,128)(2,1)S(1)}, bf16[48,3200]{1,0:T(8,128)(2,1)S(1)}, u32[]{:S(2)}, u32[]{:S(2)}) collective-permute-start(bf16[48,3200]{1,0:T(8,128)(2,1)S(1)} %get-tuple-element.80), channel_id=1, source_target_pairs={{16,0},{32,16},{48,32},{64,48},{80,64},{96,80},{112,96},{0,112},{1... | collective-permute-start | bytes 921608 | tf_op jit(solution)/shard_map/ppermute | solution.py:667
  43.8 8.4 %collective-permute-done.4.low = bf16[48,3200]{1,0:T(8,128)(2,1)S(1)} collective-permute-done((bf16[48,3200]{1,0:T(8,128)(2,1)S(1)}, bf16[48,3200]{1,0:T(8,128)(2,1)S(1)}, u32[]{:S(2)}, u32[]{:S(2)}) %collective-permute-start.4) | collective-permute-done | bytes 307232 | tf_op jit(solution)/shard_map/ppermute | solution.py:666
  52.2 3.4 %collective-permute-done.5.high = bf16[48,3200]{1,0:T(8,128)(2,1)S(1)} collective-permute-done((bf16[48,3200]{1,0:T(8,128)(2,1)S(1)}, bf16[48,3200]{1,0:T(8,128)(2,1)S(1)}, u32[]{:S(2)}, u32[]{:S(2)}) %collective-permute-start.5) | collective-permute-done | bytes 307232 | tf_op jit(solution)/shard_map/ppermute | solution.py:667
  55.7 1.5 collective-permute-start.6
  57.1 0.4 collective-permute-start.7
  57.6 3.4 %collective-permute-done.6.left = bf16[48,3200]{1,0:T(8,128)(2,1)S(1)} collective-permute-done((bf16[48,3200]{1,0:T(8,128)(2,1)S(1)}, bf16[48,3200]{1,0:T(8,128)(2,1)S(1)}, u32[]{:S(2)}, u32[]{:S(2)}) %collective-permute-start.6) | collective-permute-done | bytes 307232 | tf_op jit(solution)/shard_map/ppermute | solution.py:672
  60.9 2.8 %collective-permute-done.7.right = bf16[48,3200]{1,0:T(8,128)(2,1)S(1)} collective-permute-done((bf16[48,3200]{1,0:T(8,128)(2,1)S(1)}, bf16[48,3200]{1,0:T(8,128)(2,1)S(1)}, u32[]{:S(2)}, u32[]{:S(2)}) %collective-permute-start.7) | collective-permute-done | bytes 307232 | tf_op jit(solution)/shard_map/ppermute | solution.py:673
  63.7 0.0 copy-done.12
  63.7 5.5 %shard_map.228 = (f32[3200,128]{1,0:T(8,128)S(1)}, bf16[48,3200]{1,0:T(8,128)(2,1)S(1)}, bf16[32,3200]{1,0:T(8,128)(2,1)S(1)}, bf16[48,3200]{1,0:T(8,128)(2,1)S(...) custom-call(bf16[128,3200]{1,0:T(8,128)(2,1)S(1)} %get-tuple-element.78.own, ...), custom_call_target="tpu_custom_call" | custom-call | flops 4000000000 | bytes 6072832 | tf_op jit(solution)/shard_map/pallas_call | solution.py:634
  69.2 0.1 collective-permute-start.8
  69.3 5.1 %collective-permute-start.9 = (bf16[48,3200]{1,0:T(8,128)(2,1)S(1)}, bf16[48,3200]{1,0:T(8,128)(2,1)S(1)}, u32[]{:S(2)}, u32[]{:S(2)}) collective-permute-start(bf16[48,3200]{1,0:T(8,128)(2,1)S(1)} %get-tuple-element.90), channel_id=1, source_target_pairs={{16,0},{32,16},{48,32},{64,48},{80,64},{96,80},{112,96},{0,112},{1... | collective-permute-start | bytes 921608 | tf_op jit(solution)/shard_map/ppermute | solution.py:667
  74.4 5.4 %collective-permute-done.8.low = bf16[48,3200]{1,0:T(8,128)(2,1)S(1)} collective-permute-done((bf16[48,3200]{1,0:T(8,128)(2,1)S(1)}, bf16[48,3200]{1,0:T(8,128)(2,1)S(1)}, u32[]{:S(2)}, u32[]{:S(2)}) %collective-permute-start.8) | collective-permute-done | bytes 307232 | tf_op jit(solution)/shard_map/ppermute | solution.py:666
  79.8 4.9 %collective-permute-done.9.high = bf16[48,3200]{1,0:T(8,128)(2,1)S(1)} collective-permute-done((bf16[48,3200]{1,0:T(8,128)(2,1)S(1)}, bf16[48,3200]{1,0:T(8,128)(2,1)S(1)}, u32[]{:S(2)}, u32[]{:S(2)}) %collective-permute-start.9) | collective-permute-done | bytes 307232 | tf_op jit(solution)/shard_map/ppermute | solution.py:667
  84.8 1.4 collective-permute-start.10
  86.2 1.2 collective-permute-start.11
  87.4 0.8 shard_map.231.probe_grads
  88.3 1.7 %collective-permute-done.10.left = bf16[48,3200]{1,0:T(8,128)(2,1)S(1)} collective-permute-done((bf16[48,3200]{1,0:T(8,128)(2,1)S(1)}, bf16[48,3200]{1,0:T(8,128)(2,1)S(1)}, u32[]{:S(2)}, u32[]{:S(2)}) %collective-permute-start.10) | collective-permute-done | bytes 307232 | tf_op jit(solution)/shard_map/ppermute | solution.py:672
  90.0 2.8 %collective-permute-done.11.right = bf16[48,3200]{1,0:T(8,128)(2,1)S(1)} collective-permute-done((bf16[48,3200]{1,0:T(8,128)(2,1)S(1)}, bf16[48,3200]{1,0:T(8,128)(2,1)S(1)}, u32[]{:S(2)}, u32[]{:S(2)}) %collective-permute-start.11) | collective-permute-done | bytes 307232 | tf_op jit(solution)/shard_map/ppermute | solution.py:673
  92.8 7.8 %shard_map.230 = (f32[3200,128]{1,0:T(8,128)S(1)}, bf16[128,3200]{1,0:T(8,128)(2,1)S(1)}, bf16[3200,128]{1,0:T(8,128)(2,1)S(1)}, bf16[48,3200]{1,0:T(8,128)(2,1)...) custom-call(f32[3200,128]{1,0:T(8,128)S(1)} %get-tuple-element.88.grad_own, ...), custom_call_target="tpu_custom_call" | custom-call | flops 6000000000 | bytes 10375168 | tf_op jit(solution)/shard_map/pallas_call | solution.py:634
  100.6 0.3 collective-permute-start.12
  100.9 5.1 %collective-permute-start.13 = (bf16[48,3200]{1,0:T(8,128)(2,1)S(1)}, bf16[48,3200]{1,0:T(8,128)(2,1)S(1)}, u32[]{:S(2)}, u32[]{:S(2)}) collective-permute-start(bf16[48,3200]{1,0:T(8,128)(2,1)S(1)} %get-tuple-element.111), channel_id=1, source_target_pairs={{16,0},{32,16},{48,32},{64,48},{80,64},{96,80},{112,96},{0,112},{1... | collective-permute-start | bytes 921608 | tf_op jit(solution)/shard_map/ppermute | solution.py:667
  105.9 8.7 %shard_map.232 = (f32[1024,128]{1,0:T(8,128)S(1)}, f32[1024,128]{1,0:T(8,128)}) custom-call(s32[1]{0:T(128)} %bitcast.core, bf16[128,3200]{1,0:T(8,128)(2,1)S(1)} %get-tuple-element.96.d_gathered, bf16[3200,128]{1,0:T(8,128)(2,1)S(1)} %get-tuple-element.97.d_mixed, bf16[256,3200]{1,0:T(8,128)(2,1)S(1)} %get-tuple-element.98.table, ...), custom_call_target="tpu_custom_call" | custom-call | flops 6000000000 | bytes 7045124 | tf_op jit(solution)/shard_map/pallas_call | solution.py:634
  114.6 0.0 collective-permute-done.12.low
  114.6 5.6 %collective-permute-done.13.high = bf16[48,3200]{1,0:T(8,128)(2,1)S(1)} collective-permute-done((bf16[48,3200]{1,0:T(8,128)(2,1)S(1)}, bf16[48,3200]{1,0:T(8,128)(2,1)S(1)}, u32[]{:S(2)}, u32[]{:S(2)}) %collective-permute-start.13) | collective-permute-done | bytes 307232 | tf_op jit(solution)/shard_map/ppermute | solution.py:667
  120.2 0.5 collective-permute-start.14
  120.8 1.9 %collective-permute-done.14 = f32[1024,128]{1,0:T(8,128)} collective-permute-done((f32[1024,128]{1,0:T(8,128)}, f32[1024,128]{1,0:T(8,128)}, u32[]{:S(2)}, u32[]{:S(2)}) %collective-permute-start.14) | collective-permute-done | bytes 524320 | tf_op jit(solution)/shard_map/ppermute | solution.py:683
  122.6 1.1 add.12
  123.7 0.9 fusion
  124.6 6.7 %all-to-all-start = ((bf16[64,16,128]{2,1,0:T(8,128)(2,1)}), bf16[64,16,128]{2,1,0:T(8,128)(2,1)S(1)}, u32[]{:S(2)}, u32[]{:S(2)}) async-start(bf16[64,16,128]{2,1,0:T(8,128)(2,1)} %fusion), calls=%async_computation | async-start | bytes 524288 | tf_op jit(solution)/shard_map/all_to_all | solution.py:691
  131.3 0.8 shard_map.234
  132.1 1.8 %collective-permute-start.15 = (bf16[48,3200]{1,0:T(8,128)(2,1)}, bf16[48,3200]{1,0:T(8,128)(2,1)S(1)}, u32[]{:S(2)}, u32[]{:S(2)}) collective-permute-start(bf16[48,3200]{1,0:T(8,128)(2,1)} %get-tuple-element.116), channel_id=1, source_target_pairs={{0,1},{1,2},{2,3},{3,4},{4,5},{5,6},{6,7},{7,8},{8,9},{9,10},{10,1... | collective-permute-start | bytes 921608 | tf_op jit(solution)/shard_map/ppermute | solution.py:672
  133.9 0.0 collective-permute-start.16
  133.9 7.0 %all-to-all-done.pieces = bf16[64,16,128]{2,1,0:T(8,128)(2,1)S(1)} async-done(((bf16[64,16,128]{2,1,0:T(8,128)(2,1)}), bf16[64,16,128]{2,1,0:T(8,128)(2,1)S(1)}, u32[]{:S(2)}, u32[]{:S(2)}) %all-to-all-start) | async-done | bytes 262176 | tf_op jit(solution)/shard_map/all_to_all | solution.py:691
  140.9 0.8 shard_map.233
  141.7 4.8 %all-to-all-start.1 = ((bf16[64,16,128]{2,1,0:T(8,128)(2,1)}), bf16[64,16,128]{2,1,0:T(8,128)(2,1)S(1)}, u32[]{:S(2)}, u32[]{:S(2)}) async-start(bf16[64,16,128]{2,1,0:T(8,128)(2,1)} %shard_map.233), calls=%async_computation.1 | async-start | bytes 524288 | tf_op jit(solution)/shard_map/all_to_all | solution.py:693
  146.5 0.0 collective-permute-done.15.left
  146.5 0.0 collective-permute-done.16.right
  146.5 1.5 shard_map.235
  148.0 7.7 %all-to-all-done.1 = bf16[64,16,128]{2,1,0:T(8,128)(2,1)S(1)} async-done(((bf16[64,16,128]{2,1,0:T(8,128)(2,1)}), bf16[64,16,128]{2,1,0:T(8,128)(2,1)S(1)}, u32[]{:S(2)}, u32[]{:S(2)}) %all-to-all-start.1) | async-done | bytes 262176 | tf_op jit(solution)/shard_map/all_to_all | solution.py:693
  155.8 3.1 %collective-permute-start.17 = (bf16[1024,128]{1,0:T(8,128)(2,1)S(1)}, bf16[1024,128]{1,0:T(8,128)(2,1)S(1)}, u32[]{:S(2)}, u32[]{:S(2)}) collective-permute-start(bf16[1024,128]{1,0:T(8,128)(2,1)S(1)} %bitcast.28), channel_id=1, source_target_pairs={{0,1},{1,0},{2,3},{3,2},{4,5},{5,4},{6,7},{7,6},{8,9},{9,8},{10,11... | collective-permute-start | bytes 786440 | tf_op jit(solution)/shard_map/ppermute | solution.py:695
  158.9 1.2 collective-permute-done.17.other
  160.1 1.0 shard_map.236
  (27 shorter events, 0.2 us)
Async XLA Ops:
  0.6 25.0 %copy-start.14 = (f32[1,1,3,512]{3,1,2,0:T(1,128)S(1)}, f32[1,1,3,512]{3,1,2,0:T(1,128)}, u32[]{:S(2)}) copy-start(f32[1,1,3,512]{3,1,2,0:T(1,128)} %param.21) | copy-start | bytes 18436
  0.7 25.0 %copy-start.13 = (f32[1,1,3,1024]{3,1,2,0:T(1,128)S(1)}, f32[1,1,3,1024]{3,1,2,0:T(1,128)}, u32[]{:S(2)}) copy-start(f32[1,1,3,1024]{3,1,2,0:T(1,128)} %param.18) | copy-start | bytes 36868
  0.7 25.0 %copy-start.7 = (f32[20,64]{1,0:T(8,128)S(1)}, f32[20,64]{1,0:T(8,128)}, u32[]{:S(2)}) copy-start(f32[20,64]{1,0:T(8,128)} %pfirst.1) | copy-start | bytes 15364
  0.7 25.0 %copy-start.6 = (f32[20,64]{1,0:T(8,128)S(1)}, f32[20,64]{1,0:T(8,128)}, u32[]{:S(2)}) copy-start(f32[20,64]{1,0:T(8,128)} %first.1) | copy-start | bytes 15364
  0.7 25.0 %copy-start.11 = (s32[1,1,128]{2,1,0:T(1,128)S(1)}, s32[1,1,128]{2,1,0:T(1,128)}, u32[]{:S(2)}) copy-start(s32[1,1,128]{2,1,0:T(1,128)} %param.24) | copy-start | bytes 1540
  0.7 25.0 %copy-start.10 = (s32[1,1,512]{2,1,0:T(1,128)S(1)}, s32[1,1,512]{2,1,0:T(1,128)}, u32[]{:S(2)}) copy-start(s32[1,1,512]{2,1,0:T(1,128)} %param.22) | copy-start | bytes 6148
  0.7 25.0 %copy-start.8 = (s32[1,1,1024]{2,1,0:T(1,128)S(1)}, s32[1,1,1024]{2,1,0:T(1,128)}, u32[]{:S(2)}) copy-start(s32[1,1,1024]{2,1,0:T(1,128)} %param.20) | copy-start | bytes 12292
  0.7 25.0 %copy-start.9 = (s32[1,1,1024]{2,1,0:T(1,128)S(1)}, s32[1,1,1024]{2,1,0:T(1,128)}, u32[]{:S(2)}) copy-start(s32[1,1,1024]{2,1,0:T(1,128)} %param.19) | copy-start | bytes 12292
  1.5 1.1 copy-start
  2.6 23.1 %copy-start.1 = (f32[64,1280]{1,0:T(8,128)S(1)}, f32[64,1280]{1,0:T(8,128)}, u32[]{:S(2)}) copy-start(f32[64,1280]{1,0:T(8,128)} %second.1) | copy-start | bytes 983044
  2.6 23.1 %copy-start.3 = (f32[64,640]{1,0:T(8,128)S(1)}, f32[64,640]{1,0:T(8,128)}, u32[]{:S(2)}) copy-start(f32[64,640]{1,0:T(8,128)} %psecond.1) | copy-start | bytes 491524
  2.6 23.1 %copy-start.4 = (f32[1,1,32768]{2,1,0:T(1,128)S(1)}, f32[1,1,32768]{2,1,0:T(1,128)}, u32[]{:S(2)}) copy-start(f32[1,1,32768]{2,1,0:T(1,128)} %param.23) | copy-start | bytes 393220
  3.2 16.3 %collective-permute-start = (bf16[48,3200]{1,0:T(8,128)(2,1)S(1)}, bf16[48,3200]{1,0:T(8,128)(2,1)S(1)}, u32[]{:S(2)}, u32[]{:S(2)}) collective-permute-start(bf16[48,3200]{1,0:T(8,128)(2,1)S(1)} %get-tuple-element.69), channel_id=1, source_target_pairs={{0,16},{16,32},{32,48},{48,64},{64,80},{80,96},{96,112},{112,0},{1... | collective-permute-start | bytes 921608 | tf_op jit(solution)/shard_map/ppermute | solution.py:666
  7.0 16.5 %collective-permute-start.1 = (bf16[48,3200]{1,0:T(8,128)(2,1)S(1)}, bf16[48,3200]{1,0:T(8,128)(2,1)S(1)}, u32[]{:S(2)}, u32[]{:S(2)}) collective-permute-start(bf16[48,3200]{1,0:T(8,128)(2,1)S(1)} %get-tuple-element.70), channel_id=1, source_target_pairs={{16,0},{32,16},{48,32},{64,48},{80,64},{96,80},{112,96},{0,112},{1... | collective-permute-start | bytes 921608 | tf_op jit(solution)/shard_map/ppermute | solution.py:667
  23.5 5.9 %collective-permute-start.2 = (bf16[48,3200]{1,0:T(8,128)(2,1)S(1)}, bf16[48,3200]{1,0:T(8,128)(2,1)S(1)}, u32[]{:S(2)}, u32[]{:S(2)}) collective-permute-start(bf16[48,3200]{1,0:T(8,128)(2,1)S(1)} %get-tuple-element.72), channel_id=1, source_target_pairs={{0,1},{1,2},{2,3},{3,4},{4,5},{5,6},{6,7},{7,8},{8,9},{9,10},{10,1... | collective-permute-start | bytes 921608 | tf_op jit(solution)/shard_map/ppermute | solution.py:672
  25.6 6.6 %collective-permute-start.3 = (bf16[48,3200]{1,0:T(8,128)(2,1)S(1)}, bf16[48,3200]{1,0:T(8,128)(2,1)S(1)}, u32[]{:S(2)}, u32[]{:S(2)}) collective-permute-start(bf16[48,3200]{1,0:T(8,128)(2,1)S(1)} %get-tuple-element.73), channel_id=1, source_target_pairs={{1,0},{2,1},{3,2},{4,3},{5,4},{6,5},{7,6},{8,7},{9,8},{10,9},{11,1... | collective-permute-start | bytes 921608 | tf_op jit(solution)/shard_map/ppermute | solution.py:673
  25.7 6.5 %copy-start.2 = (f32[5,128,128]{2,1,0:T(8,128)S(1)}, f32[5,128,128]{2,1,0:T(8,128)}, u32[]{:S(2)}) copy-start(f32[5,128,128]{2,1,0:T(8,128)} %mixing.3) | copy-start | bytes 983044
  32.2 31.5 %copy-start.5 = (f32[128,128]{1,0:T(8,128)S(1)}, f32[128,128]{1,0:T(8,128)}, u32[]{:S(2)}) copy-start(f32[128,128]{1,0:T(8,128)} %first_readout.1) | copy-start | bytes 196612
  32.2 31.5 %copy-start.12 = (f32[128]{0:T(128)S(1)}, f32[128]{0:T(128)}, u32[]{:S(2)}) copy-start(f32[128]{0:T(128)} %param.31) | copy-start | bytes 1540
  38.7 13.6 %collective-permute-start.4 = (bf16[48,3200]{1,0:T(8,128)(2,1)S(1)}, bf16[48,3200]{1,0:T(8,128)(2,1)S(1)}, u32[]{:S(2)}, u32[]{:S(2)}) collective-permute-start(bf16[48,3200]{1,0:T(8,128)(2,1)S(1)} %get-tuple-element.79), channel_id=1, source_target_pairs={{0,16},{16,32},{32,48},{48,64},{64,80},{80,96},{96,112},{112,0},{1... | collective-permute-start | bytes 921608 | tf_op jit(solution)/shard_map/ppermute | solution.py:666
  39.4 16.2 %collective-permute-start.5 = (bf16[48,3200]{1,0:T(8,128)(2,1)S(1)}, bf16[48,3200]{1,0:T(8,128)(2,1)S(1)}, u32[]{:S(2)}, u32[]{:S(2)}) collective-permute-start(bf16[48,3200]{1,0:T(8,128)(2,1)S(1)} %get-tuple-element.80), channel_id=1, source_target_pairs={{16,0},{32,16},{48,32},{64,48},{80,64},{96,80},{112,96},{0,112},{1... | collective-permute-start | bytes 921608 | tf_op jit(solution)/shard_map/ppermute | solution.py:667
  55.7 5.3 %collective-permute-start.6 = (bf16[48,3200]{1,0:T(8,128)(2,1)S(1)}, bf16[48,3200]{1,0:T(8,128)(2,1)S(1)}, u32[]{:S(2)}, u32[]{:S(2)}) collective-permute-start(bf16[48,3200]{1,0:T(8,128)(2,1)S(1)} %get-tuple-element.82), channel_id=1, source_target_pairs={{0,1},{1,2},{2,3},{3,4},{4,5},{5,6},{6,7},{7,8},{8,9},{9,10},{10,1... | collective-permute-start | bytes 921608 | tf_op jit(solution)/shard_map/ppermute | solution.py:672
  57.1 6.6 %collective-permute-start.7 = (bf16[48,3200]{1,0:T(8,128)(2,1)S(1)}, bf16[48,3200]{1,0:T(8,128)(2,1)S(1)}, u32[]{:S(2)}, u32[]{:S(2)}) collective-permute-start(bf16[48,3200]{1,0:T(8,128)(2,1)S(1)} %get-tuple-element.83), channel_id=1, source_target_pairs={{1,0},{2,1},{3,2},{4,3},{5,4},{6,5},{7,6},{8,7},{9,8},{10,9},{11,1... | collective-permute-start | bytes 921608 | tf_op jit(solution)/shard_map/ppermute | solution.py:673
  69.2 10.6 %collective-permute-start.8 = (bf16[48,3200]{1,0:T(8,128)(2,1)S(1)}, bf16[48,3200]{1,0:T(8,128)(2,1)S(1)}, u32[]{:S(2)}, u32[]{:S(2)}) collective-permute-start(bf16[48,3200]{1,0:T(8,128)(2,1)S(1)} %get-tuple-element.89), channel_id=1, source_target_pairs={{0,16},{16,32},{32,48},{48,64},{64,80},{80,96},{96,112},{112,0},{1... | collective-permute-start | bytes 921608 | tf_op jit(solution)/shard_map/ppermute | solution.py:666
  69.3 15.4 %collective-permute-start.9 = (bf16[48,3200]{1,0:T(8,128)(2,1)S(1)}, bf16[48,3200]{1,0:T(8,128)(2,1)S(1)}, u32[]{:S(2)}, u32[]{:S(2)}) collective-permute-start(bf16[48,3200]{1,0:T(8,128)(2,1)S(1)} %get-tuple-element.90), channel_id=1, source_target_pairs={{16,0},{32,16},{48,32},{64,48},{80,64},{96,80},{112,96},{0,112},{1... | collective-permute-start | bytes 921608 | tf_op jit(solution)/shard_map/ppermute | solution.py:667
  84.8 5.2 %collective-permute-start.10 = (bf16[48,3200]{1,0:T(8,128)(2,1)S(1)}, bf16[48,3200]{1,0:T(8,128)(2,1)S(1)}, u32[]{:S(2)}, u32[]{:S(2)}) collective-permute-start(bf16[48,3200]{1,0:T(8,128)(2,1)S(1)} %get-tuple-element.92), channel_id=1, source_target_pairs={{0,1},{1,2},{2,3},{3,4},{4,5},{5,6},{6,7},{7,8},{8,9},{9,10},{10,1... | collective-permute-start | bytes 921608 | tf_op jit(solution)/shard_map/ppermute | solution.py:672
  86.2 6.6 %collective-permute-start.11 = (bf16[48,3200]{1,0:T(8,128)(2,1)S(1)}, bf16[48,3200]{1,0:T(8,128)(2,1)S(1)}, u32[]{:S(2)}, u32[]{:S(2)}) collective-permute-start(bf16[48,3200]{1,0:T(8,128)(2,1)S(1)} %get-tuple-element.93), channel_id=1, source_target_pairs={{1,0},{2,1},{3,2},{4,3},{5,4},{6,5},{7,6},{8,7},{9,8},{10,9},{11,1... | collective-permute-start | bytes 921608 | tf_op jit(solution)/shard_map/ppermute | solution.py:673
  100.6 14.0 %collective-permute-start.12 = (bf16[48,3200]{1,0:T(8,128)(2,1)S(1)}, bf16[48,3200]{1,0:T(8,128)(2,1)S(1)}, u32[]{:S(2)}, u32[]{:S(2)}) collective-permute-start(bf16[48,3200]{1,0:T(8,128)(2,1)S(1)} %get-tuple-element.110), channel_id=1, source_target_pairs={{0,16},{16,32},{32,48},{48,64},{64,80},{80,96},{96,112},{112,0},{1... | collective-permute-start | bytes 921608 | tf_op jit(solution)/shard_map/ppermute | solution.py:666
  100.9 19.4 %collective-permute-start.13 = (bf16[48,3200]{1,0:T(8,128)(2,1)S(1)}, bf16[48,3200]{1,0:T(8,128)(2,1)S(1)}, u32[]{:S(2)}, u32[]{:S(2)}) collective-permute-start(bf16[48,3200]{1,0:T(8,128)(2,1)S(1)} %get-tuple-element.111), channel_id=1, source_target_pairs={{16,0},{32,16},{48,32},{64,48},{80,64},{96,80},{112,96},{0,112},{1... | collective-permute-start | bytes 921608 | tf_op jit(solution)/shard_map/ppermute | solution.py:667
  120.2 2.4 %collective-permute-start.14 = (f32[1024,128]{1,0:T(8,128)}, f32[1024,128]{1,0:T(8,128)}, u32[]{:S(2)}, u32[]{:S(2)}) collective-permute-start(f32[1024,128]{1,0:T(8,128)} %get-tuple-element.113), channel_id=1, source_target_pairs={{0,1},{1,0},{2,3},{3,2},{4,5},{5,4},{6,7},{7,6},{8,9},{9,8},{10,11... | collective-permute-start | bytes 1572872 | tf_op jit(solution)/shard_map/ppermute | solution.py:683
  124.6 16.2 %all-to-all-start = ((bf16[64,16,128]{2,1,0:T(8,128)(2,1)}), bf16[64,16,128]{2,1,0:T(8,128)(2,1)S(1)}, u32[]{:S(2)}, u32[]{:S(2)}) async-start(bf16[64,16,128]{2,1,0:T(8,128)(2,1)} %fusion), calls=%async_computation | async-start | bytes 524288 | tf_op jit(solution)/shard_map/all_to_all | solution.py:691
  132.1 14.4 %collective-permute-start.15 = (bf16[48,3200]{1,0:T(8,128)(2,1)}, bf16[48,3200]{1,0:T(8,128)(2,1)S(1)}, u32[]{:S(2)}, u32[]{:S(2)}) collective-permute-start(bf16[48,3200]{1,0:T(8,128)(2,1)} %get-tuple-element.116), channel_id=1, source_target_pairs={{0,1},{1,2},{2,3},{3,4},{4,5},{5,6},{6,7},{7,8},{8,9},{9,10},{10,1... | collective-permute-start | bytes 921608 | tf_op jit(solution)/shard_map/ppermute | solution.py:672
  133.9 12.6 %collective-permute-start.16 = (bf16[48,3200]{1,0:T(8,128)(2,1)S(1)}, bf16[48,3200]{1,0:T(8,128)(2,1)S(1)}, u32[]{:S(2)}, u32[]{:S(2)}) collective-permute-start(bf16[48,3200]{1,0:T(8,128)(2,1)S(1)} %get-tuple-element.117), channel_id=1, source_target_pairs={{1,0},{2,1},{3,2},{4,3},{5,4},{6,5},{7,6},{8,7},{9,8},{10,9},{11,1... | collective-permute-start | bytes 921608 | tf_op jit(solution)/shard_map/ppermute | solution.py:673
  141.7 14.1 %all-to-all-start.1 = ((bf16[64,16,128]{2,1,0:T(8,128)(2,1)}), bf16[64,16,128]{2,1,0:T(8,128)(2,1)S(1)}, u32[]{:S(2)}, u32[]{:S(2)}) async-start(bf16[64,16,128]{2,1,0:T(8,128)(2,1)} %shard_map.233), calls=%async_computation.1 | async-start | bytes 524288 | tf_op jit(solution)/shard_map/all_to_all | solution.py:693
  155.8 4.3 %collective-permute-start.17 = (bf16[1024,128]{1,0:T(8,128)(2,1)S(1)}, bf16[1024,128]{1,0:T(8,128)(2,1)S(1)}, u32[]{:S(2)}, u32[]{:S(2)}) collective-permute-start(bf16[1024,128]{1,0:T(8,128)(2,1)S(1)} %bitcast.28), channel_id=1, source_target_pairs={{0,1},{1,0},{2,3},{3,2},{4,5},{5,4},{6,7},{7,6},{8,9},{9,8},{10,11... | collective-permute-start | bytes 786440 | tf_op jit(solution)/shard_map/ppermute | solution.py:695
